TPU v7x, 256 devices: a whole 4x4x8 slice. The times are simulated.
256 devices in a mesh: seq: 64 (over z, y, core), head: 4 (over x).
Axes of the slice: x: 4, y: 4, z: 8, core: 2. Of those that a mesh axis runs over, the one named last changes fastest.
Arguments:
- queries: bfloat16 [32768, 1024], P('seq', 'head'), may hold values from -5 to 5
- keys: bfloat16 [32768, 1024], P('seq', 'head'), may hold values from -5 to 5
- values: bfloat16 [32768, 1024], P('seq', 'head'), may hold values from -6 to 6
- out_weight: bfloat16 [1024, 1024], P(None, 'head'), may hold values from -0.1875 to 0.1875
- grad_out: bfloat16 [32768, 1024], P('seq', 'head'), may hold values from -16 to 16
Outputs:
- output: bfloat16 [32768, 1024], P('seq', 'head')
- grad_queries: bfloat16 [32768, 1024], P('seq', 'head')
- grad_keys: bfloat16 [32768, 1024], P('seq', 'head')
- grad_values: bfloat16 [32768, 1024], P('seq', 'head')
- grad_weight: float32 [1024, 1024], P('seq', 'head')
All inputs are finite; a program needn't handle non-finite values.
Results may differ from a plain program's by a relative error of at most 0.019.
Values may be sent and summed in bfloat16 or wider, within the bound.
No kernel may reach another device: no remote copies, remote signals or barrier semaphores. Data moves between devices by JAX's collectives and lax.ppermute only.
A program may use at most 64 MiB of HBM per device.

v0:
```python
import math

import jax
import jax.numpy as jnp
from jax import lax
from jax.sharding import PartitionSpec as P

HEAD_DIM = 128
BLOCK = 128


def with_halo(block, sides, width):
    for axis, dim in sides:
        count = lax.axis_size(axis)
        forward = [(i, i + 1) for i in range(count - 1)]
        backward = [(target, source) for source, target in forward]
        low = lax.ppermute(
            lax.slice_in_dim(block, block.shape[dim] - width, None, axis=dim), axis, forward
        )
        high = lax.ppermute(lax.slice_in_dim(block, 0, width, axis=dim), axis, backward)
        block = jnp.concatenate([low, block, high], axis=dim)
    return block


def key_sets(levels, nblocks):
    first_level, second_level, third_level = levels
    stacked = []
    for index in range(nblocks):
        half = index // 2
        quarter = index // 4
        stacked.append(
            jnp.concatenate(
                [
                    first_level[BLOCK * index : BLOCK * index + 3 * BLOCK],
                    second_level[BLOCK * half : BLOCK * half + BLOCK],
                    second_level[BLOCK * half + 2 * BLOCK : BLOCK * half + 3 * BLOCK],
                    third_level[BLOCK * quarter : BLOCK * quarter + BLOCK],
                    third_level[BLOCK * quarter + 2 * BLOCK : BLOCK * quarter + 3 * BLOCK],
                ],
                axis=0,
            )
        )
    return jnp.stack(stacked)


def set_masks(first, total, nblocks):
    flags = []
    biases = []
    for index in range(nblocks):
        half = index // 2
        quarter = index // 4
        starts = [
            (first - BLOCK + BLOCK * index, 0, 3),
            (first // 2 - BLOCK + BLOCK * half, 1, 1),
            (first // 2 + BLOCK + BLOCK * half, 1, 1),
            (first // 4 - BLOCK + BLOCK * quarter, 2, 1),
            (first // 4 + BLOCK + BLOCK * quarter, 2, 1),
        ]
        row_flags = []
        row_bias = []
        for begin, level, blocks in starts:
            where = begin + jnp.arange(blocks * BLOCK, dtype=jnp.int32)
            row_flags.append((where >= 0) & (where < total // 2**level))
            row_bias.append(jnp.full((blocks * BLOCK,), level * math.log(2.0), jnp.float32))
        flags.append(jnp.concatenate(row_flags))
        biases.append(jnp.concatenate(row_bias))
    return (jnp.stack(flags), jnp.stack(biases))


def weights_of(queries, key_set, flags, biases):
    nblocks = queries.shape[0] // BLOCK
    nheads = queries.shape[1] // HEAD_DIM
    query_blocks = queries.reshape(nblocks, BLOCK, nheads, HEAD_DIM)
    key_blocks = key_set.reshape(nblocks, -1, nheads, HEAD_DIM)
    scores = jnp.einsum(
        "jqhe,jkhe->jhqk", query_blocks, key_blocks, preferred_element_type=jnp.float32
    ) * HEAD_DIM ** (-0.5)
    scores = scores + biases[:, None, None, :]
    scores = jnp.where(flags[:, None, None, :], scores, jnp.float32(-1e30))
    top = jnp.max(scores, axis=-1, keepdims=True)
    expd = jnp.exp(scores - top)
    return expd / jnp.sum(expd, axis=-1, keepdims=True)


def attend(queries, key_set, value_set, flags, biases):
    nblocks = queries.shape[0] // BLOCK
    nheads = queries.shape[1] // HEAD_DIM
    weight = weights_of(queries, key_set, flags, biases).astype(jnp.bfloat16)
    value_blocks = value_set.reshape(nblocks, -1, nheads, HEAD_DIM)
    result = jnp.einsum("jhqk,jkhe->jqhe", weight, value_blocks, preferred_element_type=jnp.float32)
    return result.reshape(queries.shape).astype(jnp.bfloat16)


def attend_back(queries, key_set, value_set, flags, biases, grad_attn):
    nblocks = queries.shape[0] // BLOCK
    nheads = queries.shape[1] // HEAD_DIM
    weight = weights_of(queries, key_set, flags, biases)
    rounded = weight.astype(jnp.bfloat16)
    query_blocks = queries.reshape(nblocks, BLOCK, nheads, HEAD_DIM)
    key_blocks = key_set.reshape(nblocks, -1, nheads, HEAD_DIM)
    value_blocks = value_set.reshape(nblocks, -1, nheads, HEAD_DIM)
    grad_blocks = grad_attn.reshape(nblocks, BLOCK, nheads, HEAD_DIM)
    dprob = jnp.einsum(
        "jqhe,jkhe->jhqk", grad_blocks, value_blocks, preferred_element_type=jnp.float32
    )
    delta = jnp.sum(weight * dprob, axis=-1, keepdims=True)
    dscore = (weight * (dprob - delta)).astype(jnp.bfloat16)
    grad_q = jnp.einsum(
        "jhqk,jkhe->jqhe", dscore, key_blocks, preferred_element_type=jnp.float32
    ) * HEAD_DIM ** (-0.5)
    grad_k = jnp.einsum(
        "jhqk,jqhe->jkhe", dscore, query_blocks, preferred_element_type=jnp.float32
    ) * HEAD_DIM ** (-0.5)
    grad_v = jnp.einsum("jhqk,jqhe->jkhe", rounded, grad_blocks, preferred_element_type=jnp.float32)
    members = jnp.concatenate(
        [
            grad_k.reshape(nblocks, -1, nheads * HEAD_DIM),
            grad_v.reshape(nblocks, -1, nheads * HEAD_DIM),
        ],
        axis=-1,
    )
    return (grad_q.reshape(queries.shape).astype(jnp.bfloat16), members)


def shifted(blocks, before, after):
    return jnp.pad(blocks, ((before, after), (0, 0), (0, 0)))


def spread(members):
    nblocks = members.shape[0]
    width = members.shape[2]
    pieces = [members[:, number * BLOCK : (number + 1) * BLOCK] for number in range(7)]
    first_level = shifted(pieces[0], 0, 2) + shifted(pieces[1], 1, 1) + shifted(pieces[2], 2, 0)
    lower_two = jnp.sum(pieces[3].reshape(nblocks // 2, 2, BLOCK, width), axis=1)
    upper_two = jnp.sum(pieces[4].reshape(nblocks // 2, 2, BLOCK, width), axis=1)
    second_level = shifted(lower_two, 0, 2) + shifted(upper_two, 2, 0)
    lower_four = jnp.sum(pieces[5].reshape(nblocks // 4, 4, BLOCK, width), axis=1)
    upper_four = jnp.sum(pieces[6].reshape(nblocks // 4, 4, BLOCK, width), axis=1)
    third_level = shifted(lower_four, 0, 2) + shifted(upper_four, 2, 0)
    return (
        first_level.reshape(-1, width),
        second_level.reshape(-1, width),
        third_level.reshape(-1, width),
    )


def pooled(array, factor):
    rows, width = array.shape
    return jnp.mean(
        array.reshape(rows // factor, factor, width).astype(jnp.float32), axis=1
    ).astype(jnp.bfloat16)


def local(queries, keys, values, out_weight, grad_out):
    rows = queries.shape[0]
    width = queries.shape[1]
    nblocks = rows // BLOCK
    shards = lax.axis_size("seq")
    first = lax.axis_index("seq") * rows
    total = rows * shards
    owned = [keys, values, pooled(keys, 2), pooled(values, 2), pooled(keys, 4), pooled(values, 4)]
    front = jnp.concatenate([piece[:BLOCK] for piece in owned], axis=1)
    back = jnp.concatenate([piece[-BLOCK:] for piece in owned], axis=1)
    edges = with_halo(jnp.stack([front, back]), (("seq", 0),), 1)
    extended = []
    for number, piece in enumerate(owned):
        extended.append(
            jnp.concatenate(
                [
                    edges[0][:, number * width : (number + 1) * width],
                    piece,
                    edges[3][:, number * width : (number + 1) * width],
                ],
                axis=0,
            )
        )
    key_set = key_sets((extended[0], extended[2], extended[4]), nblocks)
    value_set = key_sets((extended[1], extended[3], extended[5]), nblocks)
    flags, biases = set_masks(first, total, nblocks)
    attention = attend(queries, key_set, value_set, flags, biases)
    partial_sum = lax.dot_general(
        attention, out_weight, (((1,), (1,)), ((), ())), preferred_element_type=jnp.float32
    )
    output = lax.psum_scatter(
        partial_sum.astype(jnp.bfloat16), "head", scatter_dimension=1, tiled=True
    )
    full_cot = lax.all_gather(grad_out, "head", axis=1, tiled=True)
    grad_attention = jnp.dot(full_cot, out_weight, preferred_element_type=jnp.float32).astype(
        jnp.bfloat16
    )
    grad_weight = lax.psum_scatter(
        lax.dot_general(
            full_cot, attention, (((0,), (0,)), ((), ())), preferred_element_type=jnp.float32
        ),
        "seq",
        scatter_dimension=0,
        tiled=True,
    )
    grad_q, members = attend_back(queries, key_set, value_set, flags, biases, grad_attention)
    levels = spread(members)
    grad_front = jnp.concatenate([level[:BLOCK] for level in levels], axis=1)
    grad_back = jnp.concatenate([level[-BLOCK:] for level in levels], axis=1)
    returned = with_halo(
        jnp.stack([grad_front, grad_back]).astype(jnp.bfloat16), (("seq", 0),), 1
    ).astype(jnp.float32)
    span = 2 * width
    settled = []
    for number, level in enumerate(levels):
        middle = level[BLOCK:-BLOCK]
        middle = middle.at[:BLOCK].add(returned[0][:, number * span : (number + 1) * span])
        middle = middle.at[-BLOCK:].add(returned[3][:, number * span : (number + 1) * span])
        settled.append(middle)
    summed = (
        settled[0]
        + jnp.repeat(settled[1] * 0.5, 2, axis=0)
        + jnp.repeat(settled[2] * 0.25, 4, axis=0)
    )
    grad_keys = summed[:, :width].astype(jnp.bfloat16)
    grad_values = summed[:, width:].astype(jnp.bfloat16)
    return (output, grad_q, grad_keys, grad_values, grad_weight)


def solution(mesh):
    in_specs = (
        P("seq", "head"),
        P("seq", "head"),
        P("seq", "head"),
        P(None, "head"),
        P("seq", "head"),
    )
    out_specs = (
        P("seq", "head"),
        P("seq", "head"),
        P("seq", "head"),
        P("seq", "head"),
        P("seq", "head"),
    )
    return jax.shard_map(local, mesh=mesh, in_specs=in_specs, out_specs=out_specs, check_vma=False)
```

profile of v0, /device:TPU:2, one launch (start us, length us, event | category | flops | bytes accessed | tf_op | source)
XLA Modules:
  0.0 246.5 jit_solution(17832997621829827808)
XLA Ops:
  9.1 1.2 reshape.260
  11.4 1.2 reshape.261
  12.6 1.6 constant_dynamic-update-slice_fusion.5
  19.6 1.3 collective-permute-start.1
  20.9 3.2 %collective-permute-start = (bf16[1,128,1536]{2,1,0:T(8,128)(2,1)}, bf16[1,128,1536]{2,1,0:T(8,128)(2,1)S(1)}, u32[]{:S(2)}, u32[]{:S(2)}) collective-permute-start(bf16[1,128,1536]{2,1,0:T(8,128)(2,1)} %bitcast.139), channel_id=1, source_target_pairs={{0,4},{4,8},{8,12},{12,16},{16,20},{20,24},{24,28},{28,32},{32,36}... | collective-permute-start | bytes 1179656 | tf_op jit(solution)/shard_map/ppermute | solution.py:17
  38.1 2.1 copy.172
  41.1 2.0 copy.170
  43.2 3.9 %fusion.26 = f32[4,2,896,128]{3,2,1,0:T(8,128)} fusion(bf16[4,128,2,128]{1,3,2,0:T(8,128)(2,1)S(1)} %copy.184, bf16[1,896,2,128]{3,1,2,0:T(8,128)(2,1)} %copy.172, bf16[1,896,2,128]{3,1,2,0:T(8,128)(2,1)} %copy.171, bf16[1,896,2,128]{3,1,2,0:T(8,128)(2,1)} %copy.170, bf16[1,896,2,128]{3,1,2,0:T(8,128)(2,1)} %copy.169), kind=kOutput, calls=%fused_computation.72 | convolution fusion | flops 237633536 | bytes 5767168 | tf_op jit(solution)/shard_map/jqhe,jkhe->jhqk/dot_general | solution.py:75
  49.6 5.5 %fusion.71 = (f32[4,2,128]{2,1,0:T(2,128)S(1)}, f32[4,2,128,896]{2,3,1,0:T(8,128)S(1)}) fusion(f32[4,2,896,128]{3,2,1,0:T(8,128)} %fusion.26, f32[4,896]{1,0:T(4,128)S(1)} %copy-done.25, pred[4,896]{1,0:T(4,128)(4,1)S(1)} %pad_add_fusion.3), kind=kOutput, calls=%fused_computation.196 | output fusion | flops 7340927 | bytes 7362048 | tf_op jit(solution)/shard_map/sub | solution.py:81
  55.1 1.8 copy-done.5
  57.9 1.4 convolution_convert_fusion
  59.6 1.7 convolution_convert_fusion.2
  61.6 2.8 %multiply_reduce_fusion = (f32[4,2,128]{2,1,0:T(2,128)S(1)}, f32[4,2,128,896]{2,3,1,0:T(8,128)S(1)}) fusion(f32[4,2,128,896]{2,3,1,0:T(8,128)} %copy-done.5, f32[4,2,128]{2,1,0:T(2,128)S(1)} %get-tuple-element.197, bf16[4,128,2,128]{1,3,2,0:T(8,128)(2,1)S(1)} %copy.187, bf16[1,896,2,128]{1,3,2,0:T(8,128)(2,1)S(1)} %bitcast.129, ...), kind=kOutput, calls=%fused_computation.19 | convolution fusion | flops 240385024 | bytes 9445376 | tf_op jit(solution)/shard_map/jqhe,jkhe->jhqk/dot_general | solution.py:103
  64.7 2.5 %fusion.21 = f32[4,2,128,896]{3,2,1,0:T(8,128)} fusion(bf16[4,128,2,128]{1,3,2,0:T(8,128)(2,1)S(1)} %copy.187, f32[4,2,128,896]{2,3,1,0:T(8,128)S(1)} %copy-done.6, f32[4,2,128]{2,1,0:T(2,128)S(1)} %get-tuple-element.197), kind=kOutput, calls=%fused_computation.60 | convolution fusion | flops 236716032 | bytes 7606272 | tf_op jit(solution)/shard_map/jhqk,jqhe->jkhe/dot_general | solution.py:114
  69.5 2.5 multiply_bitcast_fusion
  72.5 1.4 copy.207
  74.7 4.6 %copy.186 = f32[4,896,2,128]{1,3,2,0:T(8,128)} copy(f32[4,896,2,128]{3,1,2,0:T(8,128)} %multiply_bitcast_fusion) | data formatting | bytes 7340032 | tf_op jit(solution)/shard_map/mul | solution.py:111
  79.4 2.0 bitcast_reduce_fusion.2
  82.1 1.2 copy-done.3
  83.8 1.4 fusion.66
  85.3 1.3 collective-permute-start.3
  87.4 4.5 %collective-permute-start.2 = (bf16[1,128,1536]{1,2,0:T(8,128)(2,1)}, bf16[1,128,1536]{1,2,0:T(8,128)(2,1)}, u32[]{:S(2)}, u32[]{:S(2)}) collective-permute-start(bf16[1,128,1536]{1,2,0:T(8,128)(2,1)} %maximum_bitcast_fusion), channel_id=1, source_target_pairs={{0,4},{4,8},{8,12},{12,16},{16,20},{20,24},{24,28},{28,32},{32,36}... | collective-permute-start | bytes 1179656 | tf_op jit(solution)/shard_map/ppermute | solution.py:17
  92.4 1.4 copy_bitcast_fusion
  93.8 1.2 convert_bitcast_fusion
  95.1 1.4 fusion.39
  97.2 1.7 reshape.258
  98.9 1.6 copy.193
  100.5 1.2 broadcast_in_dim.32
  101.6 2.6 %reshape.259 = f32[512,512]{1,0:T(8,128)} reshape(f32[128,4,512]{2,1,0:T(4,128)} %broadcast_in_dim.32) | data formatting | bytes 2097152 | tf_op jit(solution)/shard_map/reshape | solution.py:216
  104.2 2.6 %copy.195 = f32[512,512]{0,1:T(8,128)} copy(f32[512,512]{1,0:T(8,128)} %reshape.259) | data formatting | bytes 2097152 | tf_op jit(solution)/shard_map/reshape | solution.py:216
  107.8 1.5 add_convert_fusion
  111.1 128.9 %reduce-scatter.7.cloned.1.call-done = f32[16,256]{1,0:T(8,128)} async-done(((f32[1024,256]{1,0:T(8,128)}), f32[16,256]{1,0:T(8,128)}) %reduce-scatter.7.cloned.1.call-update) | async-done | bytes 16400
  (171 shorter events, 37.0 us)
Async XLA Ops:
  7.2 50.7 %copy-start = (bf16[1024,256]{1,0:T(8,128)(2,1)S(1)}, bf16[1024,256]{1,0:T(8,128)(2,1)}, u32[]{:S(2)}) copy-start(bf16[1024,256]{1,0:T(8,128)(2,1)} %param.24) | copy-start | bytes 1572868
  7.2 8.9 %copy-start.4 = (bf16[512,256]{1,0:T(8,128)(2,1)S(1)}, bf16[512,256]{1,0:T(8,128)(2,1)}, u32[]{:S(2)}) copy-start(bf16[512,256]{1,0:T(8,128)(2,1)} %param.23) | copy-start | bytes 786436
  7.2 52.4 %all-gather.2.cloned.1.call-start = ((), (), s32[]{:S(2)}) async-start(), calls=%async_computation.3 | async-start | bytes 1310720 | tf_op jit(solution)/shard_map/all_gather | solution.py:187
  7.9 103.1 %reduce-scatter.5.cloned.1.call-start = ((), (), s32[]{:S(2)}) async-start(), calls=%async_computation.2 | async-start | bytes 1310720 | tf_op jit(solution)/shard_map/reduce_scatter | solution.py:184
  10.3 14.0 %copy-start.7 = (bf16[512,256]{1,0:T(8,128)(2,1)S(1)}, bf16[512,256]{1,0:T(8,128)(2,1)}, u32[]{:S(2)}) copy-start(bf16[512,256]{1,0:T(8,128)(2,1)} %param.22) | copy-start | bytes 786436
  10.3 18.2 %copy-start.24 = (bf16[512,256]{1,0:T(8,128)(2,1)S(1)}, bf16[512,256]{1,0:T(8,128)(2,1)}, u32[]{:S(2)}) copy-start(bf16[512,256]{1,0:T(8,128)(2,1)} %param.21) | copy-start | bytes 786436
  19.6 9.4 %collective-permute-start.1 = (bf16[1,128,1536]{2,1,0:T(8,128)(2,1)}, bf16[1,128,1536]{2,1,0:T(8,128)(2,1)S(1)}, u32[]{:S(2)}, u32[]{:S(2)}) collective-permute-start(bf16[1,128,1536]{2,1,0:T(8,128)(2,1)} %bitcast.140), channel_id=1, source_target_pairs={{4,0},{8,4},{12,8},{16,12},{20,16},{24,20},{28,24},{32,28},{36,32}... | collective-permute-start | bytes 1179656 | tf_op jit(solution)/shard_map/ppermute | solution.py:20
  20.9 8.2 %collective-permute-start = (bf16[1,128,1536]{2,1,0:T(8,128)(2,1)}, bf16[1,128,1536]{2,1,0:T(8,128)(2,1)S(1)}, u32[]{:S(2)}, u32[]{:S(2)}) collective-permute-start(bf16[1,128,1536]{2,1,0:T(8,128)(2,1)} %bitcast.139), channel_id=1, source_target_pairs={{0,4},{4,8},{8,12},{12,16},{16,20},{20,24},{24,28},{28,32},{32,36}... | collective-permute-start | bytes 1179656 | tf_op jit(solution)/shard_map/ppermute | solution.py:17
  29.0 0.8 copy-start.22
  29.1 0.9 copy-start.23
  34.1 0.9 copy-start.14
  35.6 0.8 copy-start.10
  36.3 0.8 copy-start.11
  43.2 3.9 %copy-start.15 = (bf16[896,256]{1,0:T(8,128)(2,1)S(1)}, bf16[896,256]{1,0:T(8,128)(2,1)}, u32[]{:S(2)}) copy-start(bf16[896,256]{1,0:T(8,128)(2,1)} %copy-done.14) | copy-start | bytes 1376260
  43.2 5.4 %copy-start.13 = (bf16[896,256]{1,0:T(8,128)(2,1)S(1)}, bf16[896,256]{1,0:T(8,128)(2,1)}, u32[]{:S(2)}) copy-start(bf16[896,256]{1,0:T(8,128)(2,1)} %copy-done.12) | copy-start | bytes 1376260
  43.2 6.4 %copy-start.25 = (f32[4,896]{1,0:T(4,128)S(1)}, f32[4,896]{1,0:T(4,128)}, u32[]{:S(2)}) copy-start(f32[4,896]{1,0:T(4,128)} %constant.279.clone.1) | copy-start | bytes 43012
  49.6 7.3 %copy-start.20 = (bf16[896,256]{0,1:T(8,128)(2,1)S(1)}, bf16[896,256]{0,1:T(8,128)(2,1)}, u32[]{:S(2)}) copy-start(bf16[896,256]{0,1:T(8,128)(2,1)} %copy.144) | copy-start | bytes 1376260
  49.6 7.3 %copy-start.21 = (bf16[896,256]{0,1:T(8,128)(2,1)S(1)}, bf16[896,256]{0,1:T(8,128)(2,1)}, u32[]{:S(2)}) copy-start(bf16[896,256]{0,1:T(8,128)(2,1)} %copy.143) | copy-start | bytes 1376260
  55.1 1.8 copy-start.5
  59.3 180.7 %reduce-scatter.7.cloned.1.call-start = ((), (), s32[]{:S(2)}) async-start(), calls=%async_computation.4 | async-start | bytes 1064960
  61.5 3.1 %copy-start.6 = (f32[4,2,128,896]{2,3,1,0:T(8,128)S(1)}, f32[4,2,128,896]{2,3,1,0:T(8,128)}, u32[]{:S(2)}) copy-start(f32[4,2,128,896]{2,3,1,0:T(8,128)} %copy-done.5) | copy-start | bytes 11010052
  67.2 1.0 copy-start.16
  67.2 1.2 copy-start.17
  67.2 1.3 copy-start.18
  67.2 1.4 copy-start.19
  69.5 2.5 %copy-start.9 = (bf16[512,1024]{1,0:T(8,128)(2,1)S(1)}, bf16[512,1024]{1,0:T(8,128)(2,1)}, u32[]{:S(2)}) copy-start(bf16[512,1024]{1,0:T(8,128)(2,1)} %all-gather.2.cloned.1.call-done) | copy-start | bytes 3145732
  79.4 2.7 %copy-start.2 = (f32[4,896,2,128]{1,3,2,0:T(8,128)S(1)}, f32[4,896,2,128]{1,3,2,0:T(8,128)}, u32[]{:S(2)}) copy-start(f32[4,896,2,128]{1,3,2,0:T(8,128)} %copy.186) | copy-start | bytes 11010052
  79.4 3.9 %copy-start.3 = (f32[4,2,128,896]{3,2,1,0:T(8,128)S(1)}, f32[4,2,128,896]{3,2,1,0:T(8,128)}, u32[]{:S(2)}) copy-start(f32[4,2,128,896]{3,2,1,0:T(8,128)} %fusion.21) | copy-start | bytes 11010052
  85.3 8.4 %collective-permute-start.3 = (bf16[1,128,1536]{1,2,0:T(8,128)(2,1)S(1)}, bf16[1,128,1536]{1,2,0:T(8,128)(2,1)}, u32[]{:S(2)}, u32[]{:S(2)}) collective-permute-start(bf16[1,128,1536]{1,2,0:T(8,128)(2,1)S(1)} %maximum_bitcast_fusion.1), channel_id=1, source_target_pairs={{4,0},{8,4},{12,8},{16,12},{20,16},{24,20},{28,24},{32,28},{36,32}... | collective-permute-start | bytes 1179656 | tf_op jit(solution)/shard_map/ppermute | solution.py:20
  87.4 6.4 %collective-permute-start.2 = (bf16[1,128,1536]{1,2,0:T(8,128)(2,1)}, bf16[1,128,1536]{1,2,0:T(8,128)(2,1)}, u32[]{:S(2)}, u32[]{:S(2)}) collective-permute-start(bf16[1,128,1536]{1,2,0:T(8,128)(2,1)} %maximum_bitcast_fusion), channel_id=1, source_target_pairs={{0,4},{4,8},{8,12},{12,16},{16,20},{20,24},{24,28},{28,32},{32,36}... | collective-permute-start | bytes 1179656 | tf_op jit(solution)/shard_map/ppermute | solution.py:17
  95.0 1.5 copy-start.8
  104.2 135.8 %copy-start.1 = (bf16[1024,256]{1,0:T(8,128)(2,1)S(1)}, bf16[1024,256]{1,0:T(8,128)(2,1)}, u32[]{:S(2)}) copy-start(bf16[1024,256]{1,0:T(8,128)(2,1)} %param.24) | copy-start | bytes 1572868
  (1 other events, 0.8 us)
Sparse Core Ops, SparseCore 0:
  9.8 30.7 all-gather.1
  59.5 31.4 reduce-scatter.4
  96.0 143.9 reduce-scatter.6
where the time goes:
time: 248 us; the launch traced here: 247 us
  waiting for transfers between devices  130 us (52%)
  local copies, waits for them, and re-layouts  55.3 us (22%)
  other arithmetic  19.5 us (8%)
  matrix products  16.9 us (7%)
  between operations  14.5 us (6%)
  starting transfers between devices  10.7 us (4%)
    unnamed x4, waiting for transfers between devices  130 us
    unnamed x83, local copies, waits for them, and re-layouts  20.1 us
    ppermute x2, starting transfers between devices, with_halo(): lax.ppermute(lax.slice_in_dim(block, block.shape[dim] - width, None, axis...  7.76 us
    another operation x4, local copies, waits for them, and re-layouts, key_sets(): return jnp.stack(stacked)  6.05 us
    sub x1, other arithmetic, weights_of(): expd = jnp.exp(scores - top)  5.53 us
    reshape x2, local copies, waits for them, and re-layouts, local(): jnp.repeat(settled[2] * 0.25, 4, axis=0)  5.16 us
  transfers between devices with their start and end apart: 7, of which 1 were waited for; matrix products, arithmetic and copies ran while one was open for 34% of the time, Pallas kernels for 0%

commit v1 on v0

v1 whole, which is shorter than its diff:
```python
import math

import jax
import jax.numpy as jnp
from jax import lax
from jax.experimental import pallas as pl
from jax.experimental.pallas import tpu as pltpu
from jax.sharding import PartitionSpec as P

HEAD_DIM = 128
BLOCK = 128
SCALE = HEAD_DIM ** -0.5
LOG2 = SCALE / math.log(2.0)
NEG = -1e30
VMEM = pl.BlockSpec(memory_space=pltpu.VMEM)
FAR = pl.BlockSpec(memory_space=pl.ANY)
PIECES = 4
NT = (((1,), (1,)), ((), ()))
TN = (((0,), (0,)), ((), ()))
NN = (((1,), (0,)), ((), ()))


def mm(a, b, dims):
    return lax.dot_general(a, b, dims, preferred_element_type=jnp.float32)


def run(body, args, outs, scratch=(), flops=0, moved=0, far_args=(), far_outs=(), room=24):
    return pl.pallas_call(
        body,
        in_specs=[FAR if number in far_args else VMEM for number in range(len(args))],
        out_shape=[jax.ShapeDtypeStruct(shape, kind) for shape, kind in outs],
        out_specs=[FAR if number in far_outs else VMEM for number in range(len(outs))],
        scratch_shapes=list(scratch),
        cost_estimate=pl.CostEstimate(flops=flops, bytes_accessed=moved, transcendentals=0),
        compiler_params=pltpu.CompilerParams(vmem_limit_bytes=room * 1024 * 1024),
    )(*args)


def pool_matrix(rows, factor):
    row = lax.broadcasted_iota(jnp.int32, (rows, rows * factor), 0)
    col = lax.broadcasted_iota(jnp.int32, (rows, rows * factor), 1)
    inside = (col >= row * factor) & (col < row * factor + factor)
    return jnp.where(inside, 1.0 / factor, 0.0).astype(jnp.bfloat16)


def repeat_matrix(rows, factor):
    row = lax.broadcasted_iota(jnp.int32, (rows * factor, rows), 0)
    col = lax.broadcasted_iota(jnp.int32, (rows * factor, rows), 1)
    inside = (row >= col * factor) & (row < col * factor + factor)
    return jnp.where(inside, 1.0, 0.0).astype(jnp.bfloat16)


def repeated(part, factor):
    matrix = repeat_matrix(part.shape[0], factor)
    high = part.astype(jnp.bfloat16)
    low = (part - high.astype(jnp.float32)).astype(jnp.bfloat16)
    return mm(matrix, high, NN) + mm(matrix, low, NN)


def in_pieces(source, target, sems):
    count = sems.shape[0]
    size = source.shape[0] // count
    return [pltpu.make_async_copy(source.at[pl.ds(number * size, size)], target.at[pl.ds(number * size, size)],
                                  sems.at[number]) for number in range(count)]


def on_even():
    return lax.rem(lax.axis_index("seq"), 2) == 0


def prepare(keys, values, mine, to_next, to_prev):
    width = keys.shape[1]
    two = pool_matrix(256, 2)
    four = pool_matrix(64, 4)
    for number, source in enumerate((keys, values)):
        cols = slice(number * width, (number + 1) * width)
        mine[:, cols] = source[...]
        first = mm(two, source[...], NN).astype(jnp.bfloat16)
        to_next[0:128, cols] = source[384:512]
        to_next[128:192, cols] = first[128:192]
        to_next[192:256, cols] = mm(four, source[0:256], NN).astype(jnp.bfloat16)
        to_prev[0:128, cols] = source[0:128]
        to_prev[128:192, cols] = first[64:128]
        to_prev[192:256, cols] = mm(four, source[256:512], NN).astype(jnp.bfloat16)


def fetch(queries, weight, _, queries_here, weight_here):
    queries_here[...] = queries[...]
    weight_here[...] = weight[...]


def widen(before, after, edge):
    half = pool_matrix(64, 2)
    both = pool_matrix(32, 2)
    quarter = pool_matrix(32, 4)
    edge[0:128] = before[0:128]
    edge[128:256] = after[0:128]
    edge[256:320] = before[128:192]
    edge[320:384] = mm(half, before[0:128], NN).astype(jnp.bfloat16)
    edge[384:448] = mm(half, after[0:128], NN).astype(jnp.bfloat16)
    edge[448:512] = after[128:192]
    edge[512:576] = before[192:256]
    edge[576:608] = mm(both, before[128:192], NN).astype(jnp.bfloat16)
    edge[608:640] = mm(quarter, before[0:128], NN).astype(jnp.bfloat16)
    edge[640:672] = mm(quarter, after[0:128], NN).astype(jnp.bfloat16)
    edge[672:704] = mm(both, after[128:192], NN).astype(jnp.bfloat16)
    edge[704:768] = after[192:256]


def own_set(half, mine, pooled):
    both = (0, 256)
    if half == 0:
        return [(mine, 0, 128, 0, both), (mine, 128, 256, 0, both), (mine, 256, 384, 0, (128, 256)), (pooled, 128, 1024, 1, both)]
    return [(mine, 128, 256, 0, (0, 128)), (mine, 256, 384, 0, both), (mine, 384, 512, 0, both), (pooled, 0, 896, 1, both)]


def edge_set(half, edge):
    place = lax.axis_index("seq")
    has_prev = place > 0
    has_next = place < lax.axis_size("seq") - 1
    both = (0, 256)
    far = [(edge, 512, 1280, 2, both, has_prev), (edge, 640, 1408, 2, both, has_next)]
    if half == 0:
        return [(edge, 0, 0, 0, (0, 128), has_prev), (edge, 256, 768, 1, both, has_prev)] + far
    return [(edge, 128, 640, 0, (128, 256), has_next), (edge, 384, 1152, 1, both, has_next)] + far


def logits_of(blocks, mine_q, cols):
    scores = []
    for source, row, _, level, seen, *there in blocks:
        score = mm(source[row:row + 128, cols], mine_q, NT) * LOG2
        if there:
            score = score + jnp.where(there[0], float(level), NEG)
        elif level:
            score = score + float(level)
        empty = jnp.full((128, 128), NEG, jnp.float32)
        if seen == (0, 128):
            score = jnp.concatenate([score[:, :128], empty], axis=1)
        if seen == (128, 256):
            score = jnp.concatenate([empty, score[:, 128:]], axis=1)
        scores.append(score)
    return scores


def gather(blocks, scores, top, value_cols):
    total = jnp.zeros((128, 256), jnp.float32)
    summed = jnp.zeros((128, 256), jnp.float32)
    for (source, row, *_), score in zip(blocks, scores):
        expd = jnp.exp2(score - top)
        total = total + expd
        summed = summed + mm(source[row:row + 128, value_cols], expd.astype(jnp.bfloat16), TN)
    return jnp.sum(total, axis=0, keepdims=True), summed


def top_of(scores):
    top = scores[0]
    for score in scores[1:]:
        top = jnp.maximum(top, score)
    return jnp.max(top, axis=0, keepdims=True)


def forward_own(queries, mine, _, tops, totals, sums, pooled):
    pooled[...] = mm(pool_matrix(256, 2), mine[...], NN).astype(jnp.bfloat16)
    width = queries.shape[1]
    for head in range(2):
        cols = slice(head * 128, head * 128 + 128)
        value_cols = slice(width + head * 128, width + head * 128 + 128)
        for half in range(2):
            span = slice(256 * half, 256 * half + 256)
            blocks = own_set(half, mine, pooled)
            scores = logits_of(blocks, queries[span, cols], cols)
            top = top_of(scores)
            tops[head:head + 1, span] = top
            totals[head:head + 1, span], sums[head * 128:head * 128 + 128, span] = gather(blocks, scores, top, value_cols)


def forward(queries, before, after, weight, tops, totals, sums,
            attention, lse, own, first_up, second_up, first_down, edge):
    widen(before, after, edge)
    width = queries.shape[1]
    for head in range(2):
        cols = slice(head * 128, head * 128 + 128)
        value_cols = slice(width + head * 128, width + head * 128 + 128)
        for half in range(2):
            span = slice(256 * half, 256 * half + 256)
            blocks = edge_set(half, edge)
            scores = logits_of(blocks, queries[span, cols], cols)
            before_top = tops[head:head + 1, span]
            top = jnp.maximum(before_top, top_of(scores))
            total, summed = gather(blocks, scores, top, value_cols)
            scale = jnp.exp2(before_top - top)
            total = total + scale * totals[head:head + 1, span]
            lse[head:head + 1, span] = top + jnp.log2(total)
            result = ((summed + scale * sums[head * 128:head * 128 + 128, span]) / total).T
            attention[span, cols] = result.astype(jnp.bfloat16)
    heads = lax.axis_size("head")
    here = lax.axis_index("head")

    def partial_to(target):
        start = pl.multiple_of(lax.rem(target, heads) * width, width)
        return mm(attention[...], weight[pl.ds(start, width), :], NT)

    own[...] = partial_to(here).astype(jnp.bfloat16)
    first_up[...] = partial_to(here + 2).astype(jnp.bfloat16)
    second_up[...] = partial_to(here + 1).astype(jnp.bfloat16)
    first_down[...] = partial_to(here + 3).astype(jnp.bfloat16)


def products(mine, below, above, opposite, attention, weight, keep, send, grad_attention, deltas):
    heads = lax.axis_size("head")
    here = lax.axis_index("head")
    even = on_even()
    groups, rows, width = keep.shape
    each = groups // heads
    total = jnp.zeros(grad_attention.shape, jnp.float32)
    for shift, cot in ((0, mine), (heads - 1, below), (1, above), (2, opposite)):
        owner = lax.rem(here + shift, heads)
        chunks = mm(cot[...], attention[...], TN).reshape(each, 2, rows, width)
        first, second = chunks[:, 0], chunks[:, 1]
        start = owner * each
        keep[pl.ds(start, each)] = jnp.where(even, first, second)
        send[pl.ds(start, each)] = jnp.where(even, second, first).astype(jnp.bfloat16)
        total = total + mm(cot[...], weight[pl.ds(pl.multiple_of(owner * width, width), width), :], NN)
    rounded = total.astype(jnp.bfloat16)
    grad_attention[...] = rounded
    terms = rounded.astype(jnp.float32) * attention[...].astype(jnp.float32)
    high = terms.astype(jnp.bfloat16)
    low = (terms - high.astype(jnp.float32)).astype(jnp.bfloat16)
    ones = jnp.ones((16, HEAD_DIM), jnp.bfloat16)
    for head in range(2):
        cols = slice(head * HEAD_DIM, head * HEAD_DIM + HEAD_DIM)
        deltas[head:head + 1] = (mm(ones, high[:, cols], NT) + mm(ones, low[:, cols], NT))[0:1]


def pair_sum(keep, sibling, pairs):
    pairs[...] = (keep[...] + sibling[...].astype(jnp.float32)).astype(jnp.bfloat16)


def score_grads(blocks, scores, norm, delta, cot, value_cols):
    pairs = []
    for (source, row, *_), score in zip(blocks, scores):
        prob = jnp.exp2(score - norm)
        dprob = mm(source[row:row + 128, value_cols], cot, NT)
        pairs.append((prob.astype(jnp.bfloat16), (prob * (dprob - delta)).astype(jnp.bfloat16)))
    return pairs


def backward(queries, before, after, lse, grad_attention, deltas, second_up, from_below,
             dscores, to_next, to_prev, edge, send_up, total):
    send_up[...] = (second_up[...].astype(jnp.float32) + from_below[...].astype(jnp.float32)).astype(jnp.bfloat16)
    widen(before, after, edge)
    width = queries.shape[1]
    for half in range(2):
        span = slice(256 * half, 256 * half + 256)
        blocks = edge_set(half, edge)
        for head in range(2):
            cols = slice(head * 128, head * 128 + 128)
            value_cols = slice(width + head * 128, width + head * 128 + 128)
            mine_q = queries[span, cols]
            cot = grad_attention[span, cols]
            pairs = score_grads(blocks, logits_of(blocks, mine_q, cols), lse[head:head + 1, span],
                                deltas[head:head + 1, span], cot, value_cols)
            for number, ((_, _, at, *_), (prob, dscore)) in enumerate(zip(blocks, pairs)):
                dscores[2 * half + head, 128 * number:128 * number + 128] = dscore
                grad_k = mm(dscore, mine_q, NN) * SCALE
                grad_v = mm(prob, cot, NN)
                if half == 1 and at >= 1280:
                    total[at:at + 128, cols] += grad_k
                    total[at:at + 128, value_cols] += grad_v
                else:
                    total[at:at + 128, cols] = grad_k
                    total[at:at + 128, value_cols] = grad_v
    to_prev[0:128] = (total[0:128] + repeated(total[832:896] * 0.5, 2)
                      + repeated(total[1376:1408] * 0.25, 4)).astype(jnp.bfloat16)
    to_prev[128:192] = (total[768:832] * 0.5 + repeated(total[1344:1376] * 0.25, 2)).astype(jnp.bfloat16)
    to_prev[192:256] = (total[1280:1344] * 0.25).astype(jnp.bfloat16)
    to_next[0:128] = (total[640:768] + repeated(total[1152:1216] * 0.5, 2)
                      + repeated(total[1408:1440] * 0.25, 4)).astype(jnp.bfloat16)
    to_next[128:192] = (total[1216:1280] * 0.5 + repeated(total[1440:1472] * 0.25, 2)).astype(jnp.bfloat16)
    to_next[192:256] = (total[1472:1536] * 0.25).astype(jnp.bfloat16)


def own_grads(queries, mine, edge, lse, grad_attention, deltas, dscores,
              grad_queries, own, total, pooled, grad_q_here, sems):
    pooled[...] = mm(pool_matrix(256, 2), mine[...], NN).astype(jnp.bfloat16)
    stores = []
    width = queries.shape[1]
    for half in range(2):
        span = slice(256 * half, 256 * half + 256)
        blocks = own_set(half, mine, pooled)
        for head in range(2):
            cols = slice(head * 128, head * 128 + 128)
            value_cols = slice(width + head * 128, width + head * 128 + 128)
            mine_q = queries[span, cols]
            cot = grad_attention[span, cols]
            pairs = score_grads(blocks, logits_of(blocks, mine_q, cols), lse[head:head + 1, span],
                                deltas[head:head + 1, span], cot, value_cols)
            grad_q = jnp.zeros((128, 256), jnp.float32)
            for number, (source, row, *_) in enumerate(edge_set(half, edge)):
                grad_q = grad_q + mm(source[row:row + 128, cols], dscores[2 * half + head, 128 * number:128 * number + 128], TN)
            for (source, row, at, *_), (prob, dscore) in zip(blocks, pairs):
                grad_q = grad_q + mm(source[row:row + 128, cols], dscore, TN)
                grad_k = mm(dscore, mine_q, NN) * SCALE
                grad_v = mm(prob, cot, NN)
                if half == 1 and 256 <= at < 512:
                    total[at:at + 128, cols] += grad_k
                    total[at:at + 128, value_cols] += grad_v
                else:
                    total[at:at + 128, cols] = grad_k
                    total[at:at + 128, value_cols] = grad_v
            grad_q_here[span, cols] = (grad_q * SCALE).T.astype(jnp.bfloat16)
        store = pltpu.make_async_copy(grad_q_here.at[span], grad_queries.at[span], sems.at[half])
        store.start()
        stores.append(store)
    own[...] = (total[128:640] + repeated(total[896:1152] * 0.5, 2)).astype(jnp.bfloat16)
    for store in stores:
        store.wait()


def finish(own_out, from_above, last_below, own, from_prev, from_next, spread,
           output, grad_keys, grad_values, grad_weight,
           output_here, grad_keys_here, grad_values_here, grad_weight_here, spread_here, load_sems, sems):
    loads = in_pieces(spread, spread_here, load_sems)
    for copy in loads:
        copy.start()
    width = grad_keys.shape[1]
    stores = []

    def store(source, target):
        copy = pltpu.make_async_copy(source, target, sems.at[len(stores)])
        copy.start()
        stores.append(copy)

    top, bottom = pl.ds(0, 256), pl.ds(256, 256)
    output_here[top] = (own_out[top].astype(jnp.float32) + last_below[top].astype(jnp.float32)
                        + from_above[top].astype(jnp.float32)).astype(jnp.bfloat16)
    store(output_here.at[top], output.at[top])
    output_here[bottom] = (own_out[bottom].astype(jnp.float32) + last_below[bottom].astype(jnp.float32)
                           + from_above[bottom].astype(jnp.float32)).astype(jnp.bfloat16)
    store(output_here.at[bottom], output.at[bottom])
    twice = repeat_matrix(64, 2)
    four = repeat_matrix(64, 4)
    coarse = mm(four, from_next[192:256], NN)
    low = mm(four, from_prev[192:256], NN)
    first = own[0:128].astype(jnp.float32) + coarse[0:128] + from_prev[0:128].astype(jnp.float32)
    second = own[128:256].astype(jnp.float32) + coarse[128:256] + mm(twice, from_prev[128:192], NN)
    third = own[256:384].astype(jnp.float32) + low[0:128] + mm(twice, from_next[128:192], NN)
    fourth = own[384:512].astype(jnp.float32) + low[128:256] + from_next[0:128].astype(jnp.float32)
    for number, part in enumerate((first, second, third, fourth)):
        span = pl.ds(128 * number, 128)
        part = part.astype(jnp.bfloat16)
        grad_keys_here[span] = part[:, :width]
        grad_values_here[span] = part[:, width:]
        if number % 2:
            half = pl.ds(128 * (number - 1), 256)
            store(grad_keys_here.at[half], grad_keys.at[half])
            store(grad_values_here.at[half], grad_values.at[half])
    for copy in loads:
        copy.wait()
    grad_weight_here[...] = jnp.sum(spread_here[...].astype(jnp.float32), axis=0)
    store(grad_weight_here, grad_weight)
    for copy in stores:
        copy.wait()


def local(queries, keys, values, out_weight, grad_out):
    bf16, f32 = jnp.bfloat16, jnp.float32
    rows, width = queries.shape
    shards = lax.axis_size("seq")
    heads = lax.axis_size("head")
    features = out_weight.shape[0]
    up = [(i, (i + 1) % heads) for i in range(heads)]
    down = [(target, source) for source, target in up]
    swap = [(i, i ^ 1) for i in range(shards)]
    onward = [(i, (i + 1) % shards) for i in range(shards)]
    back = [(target, source) for source, target in onward]
    dma = pltpu.SemaphoreType.DMA

    below = lax.ppermute(grad_out, "head", up)
    above = lax.ppermute(grad_out, "head", down)

    mine, to_next, to_prev = run(
        prepare, (keys, values),
        [((512, 2 * width), bf16), ((256, 2 * width), bf16), ((256, 2 * width), bf16)],
        flops=2 * 384 * 512 * 512, moved=1 << 20)
    before = lax.ppermute(to_next, "seq", onward)
    after = lax.ppermute(to_prev, "seq", back)
    queries, out_weight = run(
        fetch, (queries, out_weight, to_next), [((rows, width), bf16), ((features, width), bf16)],
        moved=2 << 20, far_args=(2,))
    tops, totals, sums = run(
        forward_own, (queries, mine, to_next),
        [((2, rows), f32), ((2, rows), f32), ((2 * HEAD_DIM, rows), f32)],
        [pltpu.VMEM((256, 2 * width), bf16)], flops=10 ** 9, moved=2 << 20, far_args=(2,))
    opposite = lax.ppermute(below, "head", up)

    attention, lse, own_out, first_up, second_up, first_down = run(
        forward, (queries, before, after, out_weight, tops, totals, sums),
        [((rows, width), bf16), ((2, rows), f32), ((rows, width), bf16), ((rows, width), bf16),
         ((rows, width), bf16), ((rows, width), bf16)],
        [pltpu.VMEM((768, 2 * width), bf16)], flops=10 ** 9, moved=3 << 20)
    from_below = lax.ppermute(first_up, "head", up)
    from_above = lax.ppermute(first_down, "head", down)

    chunk = features // shards
    keep, send, grad_attention, deltas = run(
        products, (grad_out, below, above, opposite, attention, out_weight),
        [((shards // 2, chunk, width), f32), ((shards // 2, chunk, width), bf16), ((rows, width), bf16), ((2, rows), f32)],
        flops=6 * 10 ** 8, moved=2 << 20)
    half_sum = lax.ppermute(send, "seq", swap)
    pairs, = run(pair_sum, (keep, half_sum), [((shards // 2, chunk, width), bf16)], moved=1 << 20)
    groups = [list(range(core, shards, 2)) for core in range(2)]
    spread = lax.all_to_all(pairs, "seq", 0, 0, axis_index_groups=groups)

    dscores, to_next, to_prev, edge, send_up = run(
        backward, (queries, before, after, lse, grad_attention, deltas, second_up, from_below),
        [((4, 512, 256), bf16), ((256, 2 * width), bf16), ((256, 2 * width), bf16), ((768, 2 * width), bf16),
         ((rows, width), bf16)],
        [pltpu.VMEM((1536, 2 * width), f32)], flops=2 * 10 ** 9, moved=4 << 20)
    last_below = lax.ppermute(send_up, "head", up)
    grad_before = lax.ppermute(to_next, "seq", onward)
    grad_after = lax.ppermute(to_prev, "seq", back)
    grad_queries, own_grad = run(
        own_grads, (queries, mine, edge, lse, grad_attention, deltas, dscores),
        [((rows, width), bf16), ((rows, 2 * width), bf16)],
        [pltpu.VMEM((1536, 2 * width), f32), pltpu.VMEM((256, 2 * width), bf16), pltpu.VMEM((rows, width), bf16), dma((2,))],
        flops=3 * 10 ** 9, moved=6 << 20, far_outs=(0,))

    output, grad_keys, grad_values, grad_weight = run(
        finish,
        (own_out, from_above, last_below, own_grad, grad_before, grad_after, spread),
        [((rows, width), bf16)] * 3 + [((chunk, width), f32)],
        [pltpu.VMEM((rows, width), bf16)] * 3 + [pltpu.VMEM((chunk, width), f32)]
        + [pltpu.VMEM((shards // 2, chunk, width), bf16), dma((PIECES,)), dma((7,))],
        moved=4 << 20, far_args=(6,), far_outs=(0, 1, 2, 3))
    return output, grad_queries, grad_keys, grad_values, grad_weight


def solution(mesh):
    split = P("seq", "head")
    return jax.shard_map(
        local, mesh=mesh, in_specs=(split, split, split, P(None, "head"), split),
        out_specs=(split,) * 5, check_vma=False)
```

time: 248 us -> 51.2 us (0.21)
  the two profiles are of different devices: /device:TPU:2 before, /device:TPU:127 now
where the time goes in v1:
time: 51.2 us; the launch traced here: 50.9 us
  starting transfers between devices  26.4 us (52%)
  Pallas kernels  12.2 us (24%)
  waiting for transfers between devices  8.54 us (17%)
  local copies, waits for them, and re-layouts  2.86 us (6%)
  between operations  0.92 us (2%)
    pallas_call x9, Pallas kernels, run(): pl.pallas_call(body, in_specs=[FAR if number in far_args else VMEM for nu...  12.2 us
    all_to_all x1, starting transfers between devices, local(): spread = lax.all_to_all(pairs, 'seq', 0, 0, axis_index_groups=groups)  8.17 us
    ppermute x1, waiting for transfers between devices, local(): grad_after = lax.ppermute(to_prev, 'seq', back)  5.8 us
    ppermute x1, starting transfers between devices, local(): before = lax.ppermute(to_next, 'seq', onward)  4.11 us
    ppermute x1, starting transfers between devices, local(): grad_before = lax.ppermute(to_next, 'seq', onward)  3.74 us
    unnamed x10, local copies, waits for them, and re-layouts  2.86 us
    ppermute x1, starting transfers between devices, local(): last_below = lax.ppermute(send_up, 'head', up)  2.73 us
    ppermute x1, starting transfers between devices, local(): from_below = lax.ppermute(first_up, 'head', up)  2.62 us
  transfers between devices with their start and end apart: 12, of which 3 were waited for; matrix products, arithmetic and copies ran while one was open for 0% of the time, Pallas kernels for 18%

profile of v1, /device:TPU:127, one launch (start us, length us, event | category | flops | bytes accessed | tf_op | source)
XLA Modules:
  0.0 50.9 jit_solution(6938700105588449688)
XLA Ops:
  0.6 0.3 collective-permute-start.3
  0.9 0.9 %copy-done.2 = bf16[512,256]{1,0:T(8,128)(2,1)S(1)} copy-done((bf16[512,256]{1,0:T(8,128)(2,1)S(1)}, bf16[512,256]{1,0:T(8,128)(2,1)}, u32[]{:S(2)}) %copy-start.2) | copy-done | bytes 262168
  1.9 0.9 %copy-done.3 = bf16[512,256]{1,0:T(8,128)(2,1)S(1)} copy-done((bf16[512,256]{1,0:T(8,128)(2,1)S(1)}, bf16[512,256]{1,0:T(8,128)(2,1)}, u32[]{:S(2)}) %copy-start.3) | copy-done | bytes 262168
  2.8 0.4 shard_map.92
  3.2 1.0 %collective-permute-start.1 = (bf16[256,512]{1,0:T(8,128)(2,1)S(1)}, bf16[256,512]{1,0:T(8,128)(2,1)S(1)}, u32[]{:S(2)}, u32[]{:S(2)}) collective-permute-start(bf16[256,512]{1,0:T(8,128)(2,1)S(1)} %get-tuple-element.36), channel_id=1, source_target_pairs={{4,0},{8,4},{12,8},{16,12},{20,16},{24,20},{28,24},{32,28},{36,32}... | collective-permute-start | bytes 786440 | tf_op jit(solution)/shard_map/ppermute | solution.py:387
  4.3 4.1 %collective-permute-start = (bf16[256,512]{1,0:T(8,128)(2,1)S(1)}, bf16[256,512]{1,0:T(8,128)(2,1)S(1)}, u32[]{:S(2)}, u32[]{:S(2)}) collective-permute-start(bf16[256,512]{1,0:T(8,128)(2,1)S(1)} %get-tuple-element.34._), channel_id=1, source_target_pairs={{0,4},{4,8},{8,12},{12,16},{16,20},{20,24},{24,28},{28,32},{32,36}... | collective-permute-start | bytes 786440 | tf_op jit(solution)/shard_map/ppermute | solution.py:386
  8.4 1.3 %collective-permute-start.4 = (bf16[512,256]{1,0:T(8,128)(2,1)}, bf16[512,256]{1,0:T(8,128)(2,1)S(1)}, u32[]{:S(2)}, u32[]{:S(2)}) collective-permute-start(bf16[512,256]{1,0:T(8,128)(2,1)} %mine.1), channel_id=1, source_target_pairs={{1,0},{2,1},{3,2},{0,3},{5,4},{6,5},{7,6},{4,7},{9,8},{10,9},{11,1... | collective-permute-start | bytes 786440 | tf_op jit(solution)/shard_map/ppermute | solution.py:380
  9.6 0.0 collective-permute-done.3.below
  9.6 1.4 %collective-permute-start.5 = (bf16[512,256]{1,0:T(8,128)(2,1)S(1)}, bf16[512,256]{1,0:T(8,128)(2,1)S(1)}, u32[]{:S(2)}, u32[]{:S(2)}) collective-permute-start(bf16[512,256]{1,0:T(8,128)(2,1)S(1)} %collective-permute-done.3.below), channel_id=1, source_target_pairs={{0,1},{1,2},{2,3},{3,0},{4,5},{5,6},{6,7},{7,4},{8,9},{9,10},{10,1... | collective-permute-start | bytes 786440 | tf_op jit(solution)/shard_map/ppermute | solution.py:395
  11.0 0.9 %copy-done.1 = bf16[512,256]{1,0:T(8,128)(2,1)S(1)} copy-done((bf16[512,256]{1,0:T(8,128)(2,1)S(1)}, bf16[512,256]{1,0:T(8,128)(2,1)}, u32[]{:S(2)}) %copy-start.1) | copy-done | bytes 262168
  12.0 0.1 shard_map.93
  12.1 1.3 %shard_map.94 = (f32[2,512]{1,0:T(2,128)S(1)}, f32[2,512]{1,0:T(2,128)S(1)}, f32[256,512]{1,0:T(8,128)S(1)}) custom-call(bf16[512,256]{1,0:T(8,128)(2,1)S(1)} %get-tuple-element.35.queries, bf16[512,512]{1,0:T(8,128)(2,1)S(1)} %get-tuple-element.38.mine, bf16[256,512]{1,0:T(8,128)(2,1)S(1)} %get-tuple-element.34._), custom_call_target="tpu_custom_call" | custom-call | flops 1000000000 | bytes 2097152 | tf_op jit(solution)/shard_map/pallas_call | solution.py:28
  13.3 0.0 collective-permute-done.before
  13.3 0.0 copy-start.4
  13.3 1.7 %shard_map.95 = (bf16[512,256]{1,0:T(8,128)(2,1)S(1)}, f32[2,512]{1,0:T(2,128)S(1)}, bf16[512,256]{1,0:T(8,128)(2,1)S(1)}, bf16[512,256]{1,0:T(8,128)(2,1)S(1)},...) custom-call(bf16[512,256]{1,0:T(8,128)(2,1)S(1)} %get-tuple-element.35.queries, ...), custom_call_target="tpu_custom_call" | custom-call | flops 1000000000 | bytes 3145728 | tf_op jit(solution)/shard_map/pallas_call | solution.py:28
  15.0 0.0 collective-permute-done.4.above
  15.0 2.5 %collective-permute-done.5.opposite = bf16[512,256]{1,0:T(8,128)(2,1)S(1)} collective-permute-done((bf16[512,256]{1,0:T(8,128)(2,1)S(1)}, bf16[512,256]{1,0:T(8,128)(2,1)S(1)}, u32[]{:S(2)}, u32[]{:S(2)}) %collective-permute-start.5) | collective-permute-done | bytes 262176 | tf_op jit(solution)/shard_map/ppermute | solution.py:395
  17.6 1.2 %shard_map.96 = (f32[32,16,256]{2,1,0:T(8,128)S(1)}, bf16[32,16,256]{2,1,0:T(8,128)(2,1)S(1)}, bf16[512,256]{1,0:T(8,128)(2,1)S(1)}, f32[2,512]{1,0:T(2,128)S(1)}) custom-call(bf16[512,256]{1,0:T(8,128)(2,1)S(1)} %copy-done.4, bf16[512,256]{1,0:T(8,128)(2,1)S(1)} %collective-permute-done.3.below, bf16[512,256]{1,0:T(8,128)(2,1)S(1)} %collective-permute-done.4.above, ...), custom_call_target="tpu_custom_call" | custom-call | flops 600000000 | bytes 2097152 | tf_op jit(solution)/shard_map/pallas_call | solution.py:28
  18.7 0.8 %collective-permute-start.10 = (bf16[32,16,256]{2,1,0:T(8,128)(2,1)S(1)}, bf16[32,16,256]{2,1,0:T(8,128)(2,1)S(1)}, u32[]{:S(2)}, u32[]{:S(2)}) collective-permute-start(bf16[32,16,256]{2,1,0:T(8,128)(2,1)S(1)} %get-tuple-element.57), channel_id=1, source_target_pairs={{0,4},{4,0},{8,12},{12,8},{16,20},{20,16},{24,28},{28,24},{32,36},... | collective-permute-start | bytes 786440 | tf_op jit(solution)/shard_map/ppermute | solution.py:410
  19.6 2.6 %collective-permute-start.6 = (bf16[512,256]{1,0:T(8,128)(2,1)S(1)}, bf16[512,256]{1,0:T(8,128)(2,1)S(1)}, u32[]{:S(2)}, u32[]{:S(2)}) collective-permute-start(bf16[512,256]{1,0:T(8,128)(2,1)S(1)} %get-tuple-element.49), channel_id=1, source_target_pairs={{0,1},{1,2},{2,3},{3,0},{4,5},{5,6},{6,7},{7,4},{8,9},{9,10},{10,1... | collective-permute-start | bytes 786440 | tf_op jit(solution)/shard_map/ppermute | solution.py:402
  22.2 0.7 %shard_map.99 = bf16[32,16,256]{2,1,0:T(8,128)(2,1)} custom-call(f32[32,16,256]{2,1,0:T(8,128)S(1)} %get-tuple-element.56.keep, bf16[32,16,256]{2,1,0:T(8,128)(2,1)S(1)} %collective-permute-done.10.sibling), custom_call_target="tpu_custom_call" | custom-call | bytes 1048576 | tf_op jit(solution)/shard_map/pallas_call | solution.py:28
  22.9 8.2 %all-to-all-start = ((bf16[32,16,256]{2,1,0:T(8,128)(2,1)}), bf16[32,16,256]{2,1,0:T(8,128)(2,1)S(1)}, u32[]{:S(2)}, u32[]{:S(2)}) async-start(bf16[32,16,256]{2,1,0:T(8,128)(2,1)} %shard_map.99), calls=%async_computation | async-start | bytes 524288 | tf_op jit(solution)/shard_map/all_to_all | solution.py:413
  31.1 0.3 collective-permute-start.2
  31.4 0.0 collective-permute-done.6.from_below
  31.4 2.1 %shard_map.97 = (bf16[4,512,256]{2,1,0:T(8,128)(2,1)S(1)}, bf16[256,512]{1,0:T(8,128)(2,1)S(1)}, bf16[256,512]{1,0:T(8,128)(2,1)S(1)}, bf16[768,512]{1,0:T(8,128)(2,1)S(1)}, bf16[512,256]{1,0:T(8,128)(2,1)S(1)}) custom-call(bf16[512,256]{1,0:T(8,128)(2,1)S(1)} %get-tuple-element.35.queries, bf16[256,512]{1,0:T(8,128)(2,1)S(1)} %collective-permute-done.before, ...), custom_call_target="tpu_custom_call" | custom-call | flops 2000000000 | bytes 4194304 | tf_op jit(solution)/shard_map/pallas_call | solution.py:28
  33.5 2.7 %collective-permute-start.7 = (bf16[512,256]{1,0:T(8,128)(2,1)S(1)}, bf16[512,256]{1,0:T(8,128)(2,1)S(1)}, u32[]{:S(2)}, u32[]{:S(2)}) collective-permute-start(bf16[512,256]{1,0:T(8,128)(2,1)S(1)} %get-tuple-element.50), channel_id=1, source_target_pairs={{0,1},{1,2},{2,3},{3,0},{4,5},{5,6},{6,7},{7,4},{8,9},{9,10},{10,1... | collective-permute-start | bytes 786440 | tf_op jit(solution)/shard_map/ppermute | solution.py:420
  36.2 3.7 %collective-permute-start.8 = (bf16[256,512]{1,0:T(8,128)(2,1)S(1)}, bf16[256,512]{1,0:T(8,128)(2,1)S(1)}, u32[]{:S(2)}, u32[]{:S(2)}) collective-permute-start(bf16[256,512]{1,0:T(8,128)(2,1)S(1)} %get-tuple-element.54), channel_id=1, source_target_pairs={{0,4},{4,8},{8,12},{12,16},{16,20},{20,24},{24,28},{28,32},{32,36}... | collective-permute-start | bytes 786440 | tf_op jit(solution)/shard_map/ppermute | solution.py:421
  40.0 3.1 %shard_map.98 = (bf16[512,256]{1,0:T(8,128)(2,1)}, bf16[512,512]{1,0:T(8,128)(2,1)S(1)}) custom-call(bf16[512,256]{1,0:T(8,128)(2,1)S(1)} %get-tuple-element.35.queries, bf16[512,512]{1,0:T(8,128)(2,1)S(1)} %get-tuple-element.38.mine, bf16[768,512]{1,0:T(8,128)(2,1)S(1)} %get-tuple-element.51.edge, f32[2,512]{1,0:T(2,128)S(1)} %get-tuple-element.44.lse, ...), custom_call_target="tpu_custom_call" | custom-call | flops 3000000000 | bytes 6291456 | tf_op jit(solution)/shard_map/pallas_call | solution.py:28
  43.1 0.0 collective-permute-done.2.from_above
  43.1 0.2 collective-permute-done.8.from_prev
  43.3 5.8 %collective-permute-done.9.from_next = bf16[256,512]{1,0:T(8,128)(2,1)S(1)} collective-permute-done((bf16[256,512]{1,0:T(8,128)(2,1)S(1)}, bf16[256,512]{1,0:T(8,128)(2,1)S(1)}, u32[]{:S(2)}, u32[]{:S(2)}) %collective-permute-start.9) | collective-permute-done | bytes 262176 | tf_op jit(solution)/shard_map/ppermute | solution.py:422
  49.1 1.7 %shard_map.100 = (bf16[512,256]{1,0:T(8,128)(2,1)}, bf16[512,256]{1,0:T(8,128)(2,1)}, bf16[512,256]{1,0:T(8,128)(2,1)}, f32[16,256]{1,0:T(8,128)}) custom-call(bf16[512,256]{1,0:T(8,128)(2,1)S(1)} %get-tuple-element.42.own_out, bf16[512,256]{1,0:T(8,128)(2,1)S(1)} %collective-permute-done.2.from_above, ...), custom_call_target="tpu_custom_call" | custom-call | bytes 4194304 | tf_op jit(solution)/shard_map/pallas_call | solution.py:28
  (11 shorter events, 0.0 us)
Async XLA Ops:
  0.6 10.4 %copy-start = (bf16[1024,256]{1,0:T(8,128)(2,1)S(1)}, bf16[1024,256]{1,0:T(8,128)(2,1)}, u32[]{:S(2)}) copy-start(bf16[1024,256]{1,0:T(8,128)(2,1)} %weight.1) | copy-start | bytes 1572868
  0.6 9.0 %collective-permute-start.3 = (bf16[512,256]{1,0:T(8,128)(2,1)}, bf16[512,256]{1,0:T(8,128)(2,1)S(1)}, u32[]{:S(2)}, u32[]{:S(2)}) collective-permute-start(bf16[512,256]{1,0:T(8,128)(2,1)} %mine.1), channel_id=1, source_target_pairs={{0,1},{1,2},{2,3},{3,0},{4,5},{5,6},{6,7},{7,4},{8,9},{9,10},{10,1... | collective-permute-start | bytes 786440 | tf_op jit(solution)/shard_map/ppermute | solution.py:379
  0.9 0.9 %copy-start.2 = (bf16[512,256]{1,0:T(8,128)(2,1)S(1)}, bf16[512,256]{1,0:T(8,128)(2,1)}, u32[]{:S(2)}) copy-start(bf16[512,256]{1,0:T(8,128)(2,1)} %keys.1) | copy-start | bytes 786436
  1.9 0.9 %copy-start.3 = (bf16[512,256]{1,0:T(8,128)(2,1)S(1)}, bf16[512,256]{1,0:T(8,128)(2,1)}, u32[]{:S(2)}) copy-start(bf16[512,256]{1,0:T(8,128)(2,1)} %values.1) | copy-start | bytes 786436
  3.2 10.1 %collective-permute-start.1 = (bf16[256,512]{1,0:T(8,128)(2,1)S(1)}, bf16[256,512]{1,0:T(8,128)(2,1)S(1)}, u32[]{:S(2)}, u32[]{:S(2)}) collective-permute-start(bf16[256,512]{1,0:T(8,128)(2,1)S(1)} %get-tuple-element.36), channel_id=1, source_target_pairs={{4,0},{8,4},{12,8},{16,12},{20,16},{24,20},{28,24},{32,28},{36,32}... | collective-permute-start | bytes 786440 | tf_op jit(solution)/shard_map/ppermute | solution.py:387
  4.3 9.1 %collective-permute-start = (bf16[256,512]{1,0:T(8,128)(2,1)S(1)}, bf16[256,512]{1,0:T(8,128)(2,1)S(1)}, u32[]{:S(2)}, u32[]{:S(2)}) collective-permute-start(bf16[256,512]{1,0:T(8,128)(2,1)S(1)} %get-tuple-element.34._), channel_id=1, source_target_pairs={{0,4},{4,8},{8,12},{12,16},{16,20},{20,24},{24,28},{28,32},{32,36}... | collective-permute-start | bytes 786440 | tf_op jit(solution)/shard_map/ppermute | solution.py:386
  8.4 6.7 %collective-permute-start.4 = (bf16[512,256]{1,0:T(8,128)(2,1)}, bf16[512,256]{1,0:T(8,128)(2,1)S(1)}, u32[]{:S(2)}, u32[]{:S(2)}) collective-permute-start(bf16[512,256]{1,0:T(8,128)(2,1)} %mine.1), channel_id=1, source_target_pairs={{1,0},{2,1},{3,2},{0,3},{5,4},{6,5},{7,6},{4,7},{9,8},{10,9},{11,1... | collective-permute-start | bytes 786440 | tf_op jit(solution)/shard_map/ppermute | solution.py:380
  9.6 7.9 %collective-permute-start.5 = (bf16[512,256]{1,0:T(8,128)(2,1)S(1)}, bf16[512,256]{1,0:T(8,128)(2,1)S(1)}, u32[]{:S(2)}, u32[]{:S(2)}) collective-permute-start(bf16[512,256]{1,0:T(8,128)(2,1)S(1)} %collective-permute-done.3.below), channel_id=1, source_target_pairs={{0,1},{1,2},{2,3},{3,0},{4,5},{5,6},{6,7},{7,4},{8,9},{9,10},{10,1... | collective-permute-start | bytes 786440 | tf_op jit(solution)/shard_map/ppermute | solution.py:395
  11.0 1.0 %copy-start.1 = (bf16[512,256]{1,0:T(8,128)(2,1)S(1)}, bf16[512,256]{1,0:T(8,128)(2,1)}, u32[]{:S(2)}) copy-start(bf16[512,256]{1,0:T(8,128)(2,1)} %queries.1) | copy-start | bytes 786436
  13.3 4.2 %copy-start.4 = (bf16[512,256]{1,0:T(8,128)(2,1)S(1)}, bf16[512,256]{1,0:T(8,128)(2,1)}, u32[]{:S(2)}) copy-start(bf16[512,256]{1,0:T(8,128)(2,1)} %mine.1) | copy-start | bytes 786436
  18.7 3.4 %collective-permute-start.10 = (bf16[32,16,256]{2,1,0:T(8,128)(2,1)S(1)}, bf16[32,16,256]{2,1,0:T(8,128)(2,1)S(1)}, u32[]{:S(2)}, u32[]{:S(2)}) collective-permute-start(bf16[32,16,256]{2,1,0:T(8,128)(2,1)S(1)} %get-tuple-element.57), channel_id=1, source_target_pairs={{0,4},{4,0},{8,12},{12,8},{16,20},{20,16},{24,28},{28,24},{32,36},... | collective-permute-start | bytes 786440 | tf_op jit(solution)/shard_map/ppermute | solution.py:410
  19.6 11.8 %collective-permute-start.6 = (bf16[512,256]{1,0:T(8,128)(2,1)S(1)}, bf16[512,256]{1,0:T(8,128)(2,1)S(1)}, u32[]{:S(2)}, u32[]{:S(2)}) collective-permute-start(bf16[512,256]{1,0:T(8,128)(2,1)S(1)} %get-tuple-element.49), channel_id=1, source_target_pairs={{0,1},{1,2},{2,3},{3,0},{4,5},{5,6},{6,7},{7,4},{8,9},{9,10},{10,1... | collective-permute-start | bytes 786440 | tf_op jit(solution)/shard_map/ppermute | solution.py:402
  22.9 26.1 %all-to-all-start = ((bf16[32,16,256]{2,1,0:T(8,128)(2,1)}), bf16[32,16,256]{2,1,0:T(8,128)(2,1)S(1)}, u32[]{:S(2)}, u32[]{:S(2)}) async-start(bf16[32,16,256]{2,1,0:T(8,128)(2,1)} %shard_map.99), calls=%async_computation | async-start | bytes 524288 | tf_op jit(solution)/shard_map/all_to_all | solution.py:413
  31.1 12.0 %collective-permute-start.2 = (bf16[512,256]{1,0:T(8,128)(2,1)S(1)}, bf16[512,256]{1,0:T(8,128)(2,1)S(1)}, u32[]{:S(2)}, u32[]{:S(2)}) collective-permute-start(bf16[512,256]{1,0:T(8,128)(2,1)S(1)} %get-tuple-element.43), channel_id=1, source_target_pairs={{1,0},{2,1},{3,2},{0,3},{5,4},{6,5},{7,6},{4,7},{9,8},{10,9},{11,1... | collective-permute-start | bytes 786440 | tf_op jit(solution)/shard_map/ppermute | solution.py:403
  33.5 9.6 %collective-permute-start.7 = (bf16[512,256]{1,0:T(8,128)(2,1)S(1)}, bf16[512,256]{1,0:T(8,128)(2,1)S(1)}, u32[]{:S(2)}, u32[]{:S(2)}) collective-permute-start(bf16[512,256]{1,0:T(8,128)(2,1)S(1)} %get-tuple-element.50), channel_id=1, source_target_pairs={{0,1},{1,2},{2,3},{3,0},{4,5},{5,6},{6,7},{7,4},{8,9},{9,10},{10,1... | collective-permute-start | bytes 786440 | tf_op jit(solution)/shard_map/ppermute | solution.py:420
  36.2 7.1 %collective-permute-start.8 = (bf16[256,512]{1,0:T(8,128)(2,1)S(1)}, bf16[256,512]{1,0:T(8,128)(2,1)S(1)}, u32[]{:S(2)}, u32[]{:S(2)}) collective-permute-start(bf16[256,512]{1,0:T(8,128)(2,1)S(1)} %get-tuple-element.54), channel_id=1, source_target_pairs={{0,4},{4,8},{8,12},{12,16},{16,20},{20,24},{24,28},{28,32},{32,36}... | collective-permute-start | bytes 786440 | tf_op jit(solution)/shard_map/ppermute | solution.py:421
  40.0 9.1 %collective-permute-start.9 = (bf16[256,512]{1,0:T(8,128)(2,1)S(1)}, bf16[256,512]{1,0:T(8,128)(2,1)S(1)}, u32[]{:S(2)}, u32[]{:S(2)}) collective-permute-start(bf16[256,512]{1,0:T(8,128)(2,1)S(1)} %get-tuple-element.55), channel_id=1, source_target_pairs={{4,0},{8,4},{12,8},{16,12},{20,16},{24,20},{28,24},{32,28},{36,32}... | collective-permute-start | bytes 786440 | tf_op jit(solution)/shard_map/ppermute | solution.py:422

commit v2 on v1

--- a/solution.py
+++ b/solution.py
@@ -206,22 +206,31 @@
     first_down[...] = partial_to(here + 3).astype(jnp.bfloat16)
 
 
-def products(mine, below, above, opposite, attention, weight, keep, send, grad_attention, deltas):
+def product_of(shift, cot, attention, weight, keep, send):
     heads = lax.axis_size("head")
-    here = lax.axis_index("head")
+    owner = lax.rem(lax.axis_index("head") + shift, heads)
     even = on_even()
     groups, rows, width = keep.shape
     each = groups // heads
-    total = jnp.zeros(grad_attention.shape, jnp.float32)
-    for shift, cot in ((0, mine), (heads - 1, below), (1, above), (2, opposite)):
-        owner = lax.rem(here + shift, heads)
-        chunks = mm(cot[...], attention[...], TN).reshape(each, 2, rows, width)
-        first, second = chunks[:, 0], chunks[:, 1]
-        start = owner * each
-        keep[pl.ds(start, each)] = jnp.where(even, first, second)
-        send[pl.ds(start, each)] = jnp.where(even, second, first).astype(jnp.bfloat16)
-        total = total + mm(cot[...], weight[pl.ds(pl.multiple_of(owner * width, width), width), :], NN)
-    rounded = total.astype(jnp.bfloat16)
+    chunks = mm(cot[...], attention[...], TN).reshape(each, 2, rows, width)
+    first, second = chunks[:, 0], chunks[:, 1]
+    start = owner * each
+    keep[pl.ds(start, each)] = jnp.where(even, first, second)
+    send[pl.ds(start, each)] = jnp.where(even, second, first).astype(jnp.bfloat16)
+    return mm(cot[...], weight[pl.ds(pl.multiple_of(owner * width, width), width), :], NN)
+
+
+def near_products(mine, below, above, attention, weight, keep, send, part):
+    heads = lax.axis_size("head")
+    part[...] = (product_of(0, mine, attention, weight, keep, send)
+                 + product_of(heads - 1, below, attention, weight, keep, send)
+                 + product_of(1, above, attention, weight, keep, send))
+
+
+def far_products(opposite, attention, weight, near_keep, near_send, part, keep, send, grad_attention, deltas):
+    keep[...] = near_keep[...]
+    send[...] = near_send[...]
+    rounded = (part[...] + product_of(2, opposite, attention, weight, keep, send)).astype(jnp.bfloat16)
     grad_attention[...] = rounded
     terms = rounded.astype(jnp.float32) * attention[...].astype(jnp.float32)
     high = terms.astype(jnp.bfloat16)
@@ -232,8 +241,15 @@
         deltas[head:head + 1] = (mm(ones, high[:, cols], NT) + mm(ones, low[:, cols], NT))[0:1]
 
 
-def pair_sum(keep, sibling, pairs):
-    pairs[...] = (keep[...] + sibling[...].astype(jnp.float32)).astype(jnp.bfloat16)
+def pair_sum(keep, sibling, pairs, pairs_here, sems):
+    stores = in_pieces(pairs_here, pairs, sems)
+    size = pairs.shape[0] // len(stores)
+    for number, store in enumerate(stores):
+        span = pl.ds(number * size, size)
+        pairs_here[span] = (keep[span] + sibling[span].astype(jnp.float32)).astype(jnp.bfloat16)
+        store.start()
+    for store in stores:
+        store.wait()
 
 
 def score_grads(blocks, scores, norm, delta, cot, value_cols):
@@ -245,9 +261,10 @@
     return pairs
 
 
-def backward(queries, before, after, lse, grad_attention, deltas, second_up, from_below,
-             dscores, to_next, to_prev, edge, send_up, total):
+def backward(queries, before, after, lse, grad_attention, deltas, second_up, from_below, own, from_above,
+             dscores, to_next, to_prev, edge, send_up, near, total):
     send_up[...] = (second_up[...].astype(jnp.float32) + from_below[...].astype(jnp.float32)).astype(jnp.bfloat16)
+    near[...] = own[...].astype(jnp.float32) + from_above[...].astype(jnp.float32)
     widen(before, after, edge)
     width = queries.shape[1]
     for half in range(2):
@@ -317,7 +334,7 @@
         store.wait()
 
 
-def finish(own_out, from_above, last_below, own, from_prev, from_next, spread,
+def finish(near_out, last_below, own, from_prev, from_next, spread,
            output, grad_keys, grad_values, grad_weight,
            output_here, grad_keys_here, grad_values_here, grad_weight_here, spread_here, load_sems, sems):
     loads = in_pieces(spread, spread_here, load_sems)
@@ -332,11 +349,9 @@
         stores.append(copy)
 
     top, bottom = pl.ds(0, 256), pl.ds(256, 256)
-    output_here[top] = (own_out[top].astype(jnp.float32) + last_below[top].astype(jnp.float32)
-                        + from_above[top].astype(jnp.float32)).astype(jnp.bfloat16)
+    output_here[top] = (near_out[top] + last_below[top].astype(jnp.float32)).astype(jnp.bfloat16)
     store(output_here.at[top], output.at[top])
-    output_here[bottom] = (own_out[bottom].astype(jnp.float32) + last_below[bottom].astype(jnp.float32)
-                           + from_above[bottom].astype(jnp.float32)).astype(jnp.bfloat16)
+    output_here[bottom] = (near_out[bottom] + last_below[bottom].astype(jnp.float32)).astype(jnp.bfloat16)
     store(output_here.at[bottom], output.at[bottom])
     twice = repeat_matrix(64, 2)
     four = repeat_matrix(64, 4)
@@ -403,19 +418,24 @@
     from_above = lax.ppermute(first_down, "head", down)
 
     chunk = features // shards
+    shapes = [((shards // 2, chunk, width), f32), ((shards // 2, chunk, width), bf16)]
+    keep, send, part = run(
+        near_products, (grad_out, below, above, attention, out_weight), shapes + [((rows, width), f32)],
+        flops=4 * 10 ** 8, moved=1 << 20)
     keep, send, grad_attention, deltas = run(
-        products, (grad_out, below, above, opposite, attention, out_weight),
-        [((shards // 2, chunk, width), f32), ((shards // 2, chunk, width), bf16), ((rows, width), bf16), ((2, rows), f32)],
-        flops=6 * 10 ** 8, moved=2 << 20)
+        far_products, (opposite, attention, out_weight, keep, send, part),
+        shapes + [((rows, width), bf16), ((2, rows), f32)])
     half_sum = lax.ppermute(send, "seq", swap)
-    pairs, = run(pair_sum, (keep, half_sum), [((shards // 2, chunk, width), bf16)], moved=1 << 20)
+    pairs, = run(pair_sum, (keep, half_sum), [((shards // 2, chunk, width), bf16)],
+                 [pltpu.VMEM((shards // 2, chunk, width), bf16), dma((PIECES,))], far_outs=(0,))
     groups = [list(range(core, shards, 2)) for core in range(2)]
     spread = lax.all_to_all(pairs, "seq", 0, 0, axis_index_groups=groups)
 
-    dscores, to_next, to_prev, edge, send_up = run(
-        backward, (queries, before, after, lse, grad_attention, deltas, second_up, from_below),
+    dscores, to_next, to_prev, edge, send_up, near_out = run(
+        backward,
+        (queries, before, after, lse, grad_attention, deltas, second_up, from_below, own_out, from_above),
         [((4, 512, 256), bf16), ((256, 2 * width), bf16), ((256, 2 * width), bf16), ((768, 2 * width), bf16),
-         ((rows, width), bf16)],
+         ((rows, width), bf16), ((rows, width), f32)],
         [pltpu.VMEM((1536, 2 * width), f32)], flops=2 * 10 ** 9, moved=4 << 20)
     last_below = lax.ppermute(send_up, "head", up)
     grad_before = lax.ppermute(to_next, "seq", onward)
@@ -428,11 +448,11 @@
 
     output, grad_keys, grad_values, grad_weight = run(
         finish,
-        (own_out, from_above, last_below, own_grad, grad_before, grad_after, spread),
+        (near_out, last_below, own_grad, grad_before, grad_after, spread),
         [((rows, width), bf16)] * 3 + [((chunk, width), f32)],
         [pltpu.VMEM((rows, width), bf16)] * 3 + [pltpu.VMEM((chunk, width), f32)]
         + [pltpu.VMEM((shards // 2, chunk, width), bf16), dma((PIECES,)), dma((7,))],
-        moved=4 << 20, far_args=(6,), far_outs=(0, 1, 2, 3))
+        moved=4 << 20, far_args=(5,), far_outs=(0, 1, 2, 3))
     return output, grad_queries, grad_keys, grad_values, grad_weight
 
 

time: 51.2 us -> 50.4 us (0.984)
  waiting for transfers between devices: 8.54 us -> 7.88 us
    ppermute x1, waiting for transfers between devices: 2.53 us -> 1.87 us  [local(): opposite = lax.ppermute(below, 'head', up)]
    pallas_call x9 -> x10, Pallas kernels: 12.2 us -> 12.2 us  [run(): pl.pallas_call(body, in_specs=[FAR if number in far_args else VMEM for nu...]
  transfers between devices with their start and end apart: 12 -> 12, of which waited for: 3 -> 3; matrix products, arithmetic and copies ran while one was open for 0% -> 0% of each run, Pallas kernels for 18% -> 20%
where the time goes in v2:
time: 50.4 us; the launch traced here: 50.1 us
  starting transfers between devices  26.3 us (52%)
  Pallas kernels  12.2 us (24%)
  waiting for transfers between devices  7.88 us (16%)
  local copies, waits for them, and re-layouts  2.86 us (6%)
  between operations  0.94 us (2%)
    pallas_call x10, Pallas kernels, run(): pl.pallas_call(body, in_specs=[FAR if number in far_args else VMEM for nu...  12.2 us
    all_to_all x1, starting transfers between devices, local(): spread = lax.all_to_all(pairs, 'seq', 0, 0, axis_index_groups=groups)  8.19 us
    ppermute x1, waiting for transfers between devices, local(): grad_after = lax.ppermute(to_prev, 'seq', back)  5.8 us
    ppermute x1, starting transfers between devices, local(): before = lax.ppermute(to_next, 'seq', onward)  4.11 us
    ppermute x1, starting transfers between devices, local(): grad_before = lax.ppermute(to_next, 'seq', onward)  3.76 us
    unnamed x10, local copies, waits for them, and re-layouts  2.86 us
    ppermute x1, starting transfers between devices, local(): last_below = lax.ppermute(send_up, 'head', up)  2.75 us
    ppermute x1, starting transfers between devices, local(): from_below = lax.ppermute(first_up, 'head', up)  2.63 us
  transfers between devices with their start and end apart: 12, of which 3 were waited for; matrix products, arithmetic and copies ran while one was open for 0% of the time, Pallas kernels for 20%

profile of v2, /device:TPU:127, one launch (start us, length us, event | category | flops | bytes accessed | tf_op | source)
XLA Modules:
  0.0 50.1 jit_solution(15491296075940059224)
XLA Ops:
  0.6 0.3 collective-permute-start.2
  0.9 0.9 %copy-done.3 = bf16[512,256]{1,0:T(8,128)(2,1)S(1)} copy-done((bf16[512,256]{1,0:T(8,128)(2,1)S(1)}, bf16[512,256]{1,0:T(8,128)(2,1)}, u32[]{:S(2)}) %copy-start.3) | copy-done | bytes 262168
  1.9 0.9 %copy-done.4 = bf16[512,256]{1,0:T(8,128)(2,1)S(1)} copy-done((bf16[512,256]{1,0:T(8,128)(2,1)S(1)}, bf16[512,256]{1,0:T(8,128)(2,1)}, u32[]{:S(2)}) %copy-start.4) | copy-done | bytes 262168
  2.8 0.4 shard_map.92
  3.2 1.0 %collective-permute-start.1 = (bf16[256,512]{1,0:T(8,128)(2,1)S(1)}, bf16[256,512]{1,0:T(8,128)(2,1)S(1)}, u32[]{:S(2)}, u32[]{:S(2)}) collective-permute-start(bf16[256,512]{1,0:T(8,128)(2,1)S(1)} %get-tuple-element.40), channel_id=1, source_target_pairs={{4,0},{8,4},{12,8},{16,12},{20,16},{24,20},{28,24},{32,28},{36,32}... | collective-permute-start | bytes 786440 | tf_op jit(solution)/shard_map/ppermute | solution.py:402
  4.3 4.1 %collective-permute-start = (bf16[256,512]{1,0:T(8,128)(2,1)S(1)}, bf16[256,512]{1,0:T(8,128)(2,1)S(1)}, u32[]{:S(2)}, u32[]{:S(2)}) collective-permute-start(bf16[256,512]{1,0:T(8,128)(2,1)S(1)} %get-tuple-element.38._), channel_id=1, source_target_pairs={{0,4},{4,8},{8,12},{12,16},{16,20},{20,24},{24,28},{28,32},{32,36}... | collective-permute-start | bytes 786440 | tf_op jit(solution)/shard_map/ppermute | solution.py:401
  8.4 1.3 %collective-permute-start.4 = (bf16[512,256]{1,0:T(8,128)(2,1)}, bf16[512,256]{1,0:T(8,128)(2,1)S(1)}, u32[]{:S(2)}, u32[]{:S(2)}) collective-permute-start(bf16[512,256]{1,0:T(8,128)(2,1)} %mine.1), channel_id=1, source_target_pairs={{1,0},{2,1},{3,2},{0,3},{5,4},{6,5},{7,6},{4,7},{9,8},{10,9},{11,1... | collective-permute-start | bytes 786440 | tf_op jit(solution)/shard_map/ppermute | solution.py:395
  9.6 0.0 collective-permute-done.2.below
  9.6 1.4 %collective-permute-start.3 = (bf16[512,256]{1,0:T(8,128)(2,1)S(1)}, bf16[512,256]{1,0:T(8,128)(2,1)S(1)}, u32[]{:S(2)}, u32[]{:S(2)}) collective-permute-start(bf16[512,256]{1,0:T(8,128)(2,1)S(1)} %collective-permute-done.2.below), channel_id=1, source_target_pairs={{0,1},{1,2},{2,3},{3,0},{4,5},{5,6},{6,7},{7,4},{8,9},{9,10},{10,1... | collective-permute-start | bytes 786440 | tf_op jit(solution)/shard_map/ppermute | solution.py:410
  11.1 0.9 %copy-done.1 = bf16[512,256]{1,0:T(8,128)(2,1)S(1)} copy-done((bf16[512,256]{1,0:T(8,128)(2,1)S(1)}, bf16[512,256]{1,0:T(8,128)(2,1)}, u32[]{:S(2)}) %copy-start.1) | copy-done | bytes 262168
  12.0 0.1 shard_map.93
  12.1 1.3 %shard_map.94 = (f32[2,512]{1,0:T(2,128)S(1)}, f32[2,512]{1,0:T(2,128)S(1)}, f32[256,512]{1,0:T(8,128)S(1)}) custom-call(bf16[512,256]{1,0:T(8,128)(2,1)S(1)} %get-tuple-element.39.queries, bf16[512,512]{1,0:T(8,128)(2,1)S(1)} %get-tuple-element.42.mine, bf16[256,512]{1,0:T(8,128)(2,1)S(1)} %get-tuple-element.38._), custom_call_target="tpu_custom_call" | custom-call | flops 1000000000 | bytes 2097152 | tf_op jit(solution)/shard_map/pallas_call | solution.py:28
  13.4 0.0 collective-permute-done.before
  13.4 0.0 copy-start.2
  13.4 1.7 %shard_map.95 = (bf16[512,256]{1,0:T(8,128)(2,1)S(1)}, f32[2,512]{1,0:T(2,128)S(1)}, bf16[512,256]{1,0:T(8,128)(2,1)S(1)}, bf16[512,256]{1,0:T(8,128)(2,1)S(1)},...) custom-call(bf16[512,256]{1,0:T(8,128)(2,1)S(1)} %get-tuple-element.39.queries, ...), custom_call_target="tpu_custom_call" | custom-call | flops 1000000000 | bytes 3145728 | tf_op jit(solution)/shard_map/pallas_call | solution.py:28
  15.1 0.6 %shard_map.96 = (f32[32,16,256]{2,1,0:T(8,128)S(1)}, bf16[32,16,256]{2,1,0:T(8,128)(2,1)S(1)}, f32[512,256]{1,0:T(8,128)S(1)}) custom-call(bf16[512,256]{1,0:T(8,128)(2,1)S(1)} %copy-done.2, bf16[512,256]{1,0:T(8,128)(2,1)S(1)} %collective-permute-done.2.below, bf16[512,256]{1,0:T(8,128)(2,1)S(1)} %collective-permute-done.4.above, ...), custom_call_target="tpu_custom_call" | custom-call | flops 400000000 | bytes 1048576 | tf_op jit(solution)/shard_map/pallas_call | solution.py:28
  15.7 1.9 %collective-permute-done.3.opposite = bf16[512,256]{1,0:T(8,128)(2,1)S(1)} collective-permute-done((bf16[512,256]{1,0:T(8,128)(2,1)S(1)}, bf16[512,256]{1,0:T(8,128)(2,1)S(1)}, u32[]{:S(2)}, u32[]{:S(2)}) %collective-permute-start.3) | collective-permute-done | bytes 262176 | tf_op jit(solution)/shard_map/ppermute | solution.py:410
  17.6 0.6 %shard_map.97 = (f32[32,16,256]{2,1,0:T(8,128)S(1)}, bf16[32,16,256]{2,1,0:T(8,128)(2,1)S(1)}, bf16[512,256]{1,0:T(8,128)(2,1)S(1)}, f32[2,512]{1,0:T(2,128)S(1)}) custom-call(bf16[512,256]{1,0:T(8,128)(2,1)S(1)} %collective-permute-done.3.opposite, bf16[512,256]{1,0:T(8,128)(2,1)S(1)} %get-tuple-element.47.attention, ...), custom_call_target="tpu_custom_call" | custom-call | tf_op jit(solution)/shard_map/pallas_call | solution.py:28
  18.1 0.8 %collective-permute-start.10 = (bf16[32,16,256]{2,1,0:T(8,128)(2,1)S(1)}, bf16[32,16,256]{2,1,0:T(8,128)(2,1)S(1)}, u32[]{:S(2)}, u32[]{:S(2)}) collective-permute-start(bf16[32,16,256]{2,1,0:T(8,128)(2,1)S(1)} %get-tuple-element.65), channel_id=1, source_target_pairs={{0,4},{4,0},{8,12},{12,8},{16,20},{20,16},{24,28},{28,24},{32,36},... | collective-permute-start | bytes 786440 | tf_op jit(solution)/shard_map/ppermute | solution.py:428
  19.0 2.6 %collective-permute-start.5 = (bf16[512,256]{1,0:T(8,128)(2,1)S(1)}, bf16[512,256]{1,0:T(8,128)(2,1)S(1)}, u32[]{:S(2)}, u32[]{:S(2)}) collective-permute-start(bf16[512,256]{1,0:T(8,128)(2,1)S(1)} %get-tuple-element.54), channel_id=1, source_target_pairs={{0,1},{1,2},{2,3},{3,0},{4,5},{5,6},{6,7},{7,4},{8,9},{9,10},{10,1... | collective-permute-start | bytes 786440 | tf_op jit(solution)/shard_map/ppermute | solution.py:417
  21.6 0.0 collective-permute-start.6
  21.6 0.7 %shard_map.100 = bf16[32,16,256]{2,1,0:T(8,128)(2,1)} custom-call(f32[32,16,256]{2,1,0:T(8,128)S(1)} %get-tuple-element.64.keep, bf16[32,16,256]{2,1,0:T(8,128)(2,1)S(1)} %collective-permute-done.10.sibling), custom_call_target="tpu_custom_call" | custom-call | tf_op jit(solution)/shard_map/pallas_call | solution.py:28
  22.3 8.2 %all-to-all-start = ((bf16[32,16,256]{2,1,0:T(8,128)(2,1)}), bf16[32,16,256]{2,1,0:T(8,128)(2,1)S(1)}, u32[]{:S(2)}, u32[]{:S(2)}) async-start(bf16[32,16,256]{2,1,0:T(8,128)(2,1)} %shard_map.100), calls=%async_computation | async-start | bytes 524288 | tf_op jit(solution)/shard_map/all_to_all | solution.py:432
  30.5 0.0 collective-permute-done.5.from_below
  30.6 2.2 %shard_map.98 = (bf16[4,512,256]{2,1,0:T(8,128)(2,1)S(1)}, bf16[256,512]{1,0:T(8,128)(2,1)S(1)}, bf16[256,512]{1,0:T(8,128)(2,1)S(1)}, bf16[768,512]{1,0:T(8,128...) custom-call(bf16[512,256]{1,0:T(8,128)(2,1)S(1)} %get-tuple-element.39.queries, ...), custom_call_target="tpu_custom_call" | custom-call | flops 2000000000 | bytes 4194304 | tf_op jit(solution)/shard_map/pallas_call | solution.py:28
  32.7 2.7 %collective-permute-start.7 = (bf16[512,256]{1,0:T(8,128)(2,1)S(1)}, bf16[512,256]{1,0:T(8,128)(2,1)S(1)}, u32[]{:S(2)}, u32[]{:S(2)}) collective-permute-start(bf16[512,256]{1,0:T(8,128)(2,1)S(1)} %get-tuple-element.58), channel_id=1, source_target_pairs={{0,1},{1,2},{2,3},{3,0},{4,5},{5,6},{6,7},{7,4},{8,9},{9,10},{10,1... | collective-permute-start | bytes 786440 | tf_op jit(solution)/shard_map/ppermute | solution.py:440
  35.5 3.8 %collective-permute-start.8 = (bf16[256,512]{1,0:T(8,128)(2,1)S(1)}, bf16[256,512]{1,0:T(8,128)(2,1)S(1)}, u32[]{:S(2)}, u32[]{:S(2)}) collective-permute-start(bf16[256,512]{1,0:T(8,128)(2,1)S(1)} %get-tuple-element.62), channel_id=1, source_target_pairs={{0,4},{4,8},{8,12},{12,16},{16,20},{20,24},{24,28},{28,32},{32,36}... | collective-permute-start | bytes 786440 | tf_op jit(solution)/shard_map/ppermute | solution.py:441
  39.3 0.0 collective-permute-start.9
  39.3 3.1 %shard_map.99 = (bf16[512,256]{1,0:T(8,128)(2,1)}, bf16[512,512]{1,0:T(8,128)(2,1)S(1)}) custom-call(bf16[512,256]{1,0:T(8,128)(2,1)S(1)} %get-tuple-element.39.queries, bf16[512,512]{1,0:T(8,128)(2,1)S(1)} %get-tuple-element.42.mine, bf16[768,512]{1,0:T(8,128)(2,1)S(1)} %get-tuple-element.59.edge, f32[2,512]{1,0:T(2,128)S(1)} %get-tuple-element.46.lse, ...), custom_call_target="tpu_custom_call" | custom-call | flops 3000000000 | bytes 6291456 | tf_op jit(solution)/shard_map/pallas_call | solution.py:28
  42.4 0.2 collective-permute-done.8.from_prev
  42.6 5.8 %collective-permute-done.9.from_next = bf16[256,512]{1,0:T(8,128)(2,1)S(1)} collective-permute-done((bf16[256,512]{1,0:T(8,128)(2,1)S(1)}, bf16[256,512]{1,0:T(8,128)(2,1)S(1)}, u32[]{:S(2)}, u32[]{:S(2)}) %collective-permute-start.9) | collective-permute-done | bytes 262176 | tf_op jit(solution)/shard_map/ppermute | solution.py:442
  48.4 1.6 %shard_map.101 = (bf16[512,256]{1,0:T(8,128)(2,1)}, bf16[512,256]{1,0:T(8,128)(2,1)}, bf16[512,256]{1,0:T(8,128)(2,1)}, f32[16,256]{1,0:T(8,128)}) custom-call(f32[512,256]{1,0:T(8,128)S(1)} %get-tuple-element.57.near_out, bf16[512,256]{1,0:T(8,128)(2,1)S(1)} %collective-permute-done.7.last_below, bf16[512,512]{1,0:T(8,128)(2,1)S(1)} %get-tuple-element.61.own, ...), custom_call_target="tpu_custom_call" | custom-call | bytes 4194304 | tf_op jit(solution)/shard_map/pallas_call | solution.py:28
  (12 shorter events, 0.0 us)
Async XLA Ops:
  0.6 10.4 %copy-start = (bf16[1024,256]{1,0:T(8,128)(2,1)S(1)}, bf16[1024,256]{1,0:T(8,128)(2,1)}, u32[]{:S(2)}) copy-start(bf16[1024,256]{1,0:T(8,128)(2,1)} %weight.1) | copy-start | bytes 1572868
  0.6 9.0 %collective-permute-start.2 = (bf16[512,256]{1,0:T(8,128)(2,1)}, bf16[512,256]{1,0:T(8,128)(2,1)S(1)}, u32[]{:S(2)}, u32[]{:S(2)}) collective-permute-start(bf16[512,256]{1,0:T(8,128)(2,1)} %mine.1), channel_id=1, source_target_pairs={{0,1},{1,2},{2,3},{3,0},{4,5},{5,6},{6,7},{7,4},{8,9},{9,10},{10,1... | collective-permute-start | bytes 786440 | tf_op jit(solution)/shard_map/ppermute | solution.py:394
  0.9 0.9 %copy-start.3 = (bf16[512,256]{1,0:T(8,128)(2,1)S(1)}, bf16[512,256]{1,0:T(8,128)(2,1)}, u32[]{:S(2)}) copy-start(bf16[512,256]{1,0:T(8,128)(2,1)} %keys.1) | copy-start | bytes 786436
  1.9 0.9 %copy-start.4 = (bf16[512,256]{1,0:T(8,128)(2,1)S(1)}, bf16[512,256]{1,0:T(8,128)(2,1)}, u32[]{:S(2)}) copy-start(bf16[512,256]{1,0:T(8,128)(2,1)} %values.1) | copy-start | bytes 786436
  3.2 10.1 %collective-permute-start.1 = (bf16[256,512]{1,0:T(8,128)(2,1)S(1)}, bf16[256,512]{1,0:T(8,128)(2,1)S(1)}, u32[]{:S(2)}, u32[]{:S(2)}) collective-permute-start(bf16[256,512]{1,0:T(8,128)(2,1)S(1)} %get-tuple-element.40), channel_id=1, source_target_pairs={{4,0},{8,4},{12,8},{16,12},{20,16},{24,20},{28,24},{32,28},{36,32}... | collective-permute-start | bytes 786440 | tf_op jit(solution)/shard_map/ppermute | solution.py:402
  4.3 9.1 %collective-permute-start = (bf16[256,512]{1,0:T(8,128)(2,1)S(1)}, bf16[256,512]{1,0:T(8,128)(2,1)S(1)}, u32[]{:S(2)}, u32[]{:S(2)}) collective-permute-start(bf16[256,512]{1,0:T(8,128)(2,1)S(1)} %get-tuple-element.38._), channel_id=1, source_target_pairs={{0,4},{4,8},{8,12},{12,16},{16,20},{20,24},{24,28},{28,32},{32,36}... | collective-permute-start | bytes 786440 | tf_op jit(solution)/shard_map/ppermute | solution.py:401
  8.4 6.7 %collective-permute-start.4 = (bf16[512,256]{1,0:T(8,128)(2,1)}, bf16[512,256]{1,0:T(8,128)(2,1)S(1)}, u32[]{:S(2)}, u32[]{:S(2)}) collective-permute-start(bf16[512,256]{1,0:T(8,128)(2,1)} %mine.1), channel_id=1, source_target_pairs={{1,0},{2,1},{3,2},{0,3},{5,4},{6,5},{7,6},{4,7},{9,8},{10,9},{11,1... | collective-permute-start | bytes 786440 | tf_op jit(solution)/shard_map/ppermute | solution.py:395
  9.6 7.9 %collective-permute-start.3 = (bf16[512,256]{1,0:T(8,128)(2,1)S(1)}, bf16[512,256]{1,0:T(8,128)(2,1)S(1)}, u32[]{:S(2)}, u32[]{:S(2)}) collective-permute-start(bf16[512,256]{1,0:T(8,128)(2,1)S(1)} %collective-permute-done.2.below), channel_id=1, source_target_pairs={{0,1},{1,2},{2,3},{3,0},{4,5},{5,6},{6,7},{7,4},{8,9},{9,10},{10,1... | collective-permute-start | bytes 786440 | tf_op jit(solution)/shard_map/ppermute | solution.py:410
  11.1 1.0 %copy-start.1 = (bf16[512,256]{1,0:T(8,128)(2,1)S(1)}, bf16[512,256]{1,0:T(8,128)(2,1)}, u32[]{:S(2)}) copy-start(bf16[512,256]{1,0:T(8,128)(2,1)} %queries.1) | copy-start | bytes 786436
  13.4 1.7 %copy-start.2 = (bf16[512,256]{1,0:T(8,128)(2,1)S(1)}, bf16[512,256]{1,0:T(8,128)(2,1)}, u32[]{:S(2)}) copy-start(bf16[512,256]{1,0:T(8,128)(2,1)} %mine.1) | copy-start | bytes 786436
  18.1 3.5 %collective-permute-start.10 = (bf16[32,16,256]{2,1,0:T(8,128)(2,1)S(1)}, bf16[32,16,256]{2,1,0:T(8,128)(2,1)S(1)}, u32[]{:S(2)}, u32[]{:S(2)}) collective-permute-start(bf16[32,16,256]{2,1,0:T(8,128)(2,1)S(1)} %get-tuple-element.65), channel_id=1, source_target_pairs={{0,4},{4,0},{8,12},{12,8},{16,20},{20,16},{24,28},{28,24},{32,36},... | collective-permute-start | bytes 786440 | tf_op jit(solution)/shard_map/ppermute | solution.py:428
  19.0 11.6 %collective-permute-start.5 = (bf16[512,256]{1,0:T(8,128)(2,1)S(1)}, bf16[512,256]{1,0:T(8,128)(2,1)S(1)}, u32[]{:S(2)}, u32[]{:S(2)}) collective-permute-start(bf16[512,256]{1,0:T(8,128)(2,1)S(1)} %get-tuple-element.54), channel_id=1, source_target_pairs={{0,1},{1,2},{2,3},{3,0},{4,5},{5,6},{6,7},{7,4},{8,9},{9,10},{10,1... | collective-permute-start | bytes 786440 | tf_op jit(solution)/shard_map/ppermute | solution.py:417
  21.6 9.0 %collective-permute-start.6 = (bf16[512,256]{1,0:T(8,128)(2,1)S(1)}, bf16[512,256]{1,0:T(8,128)(2,1)S(1)}, u32[]{:S(2)}, u32[]{:S(2)}) collective-permute-start(bf16[512,256]{1,0:T(8,128)(2,1)S(1)} %get-tuple-element.56), channel_id=1, source_target_pairs={{1,0},{2,1},{3,2},{0,3},{5,4},{6,5},{7,6},{4,7},{9,8},{10,9},{11,1... | collective-permute-start | bytes 786440 | tf_op jit(solution)/shard_map/ppermute | solution.py:418
  22.3 26.0 %all-to-all-start = ((bf16[32,16,256]{2,1,0:T(8,128)(2,1)}), bf16[32,16,256]{2,1,0:T(8,128)(2,1)S(1)}, u32[]{:S(2)}, u32[]{:S(2)}) async-start(bf16[32,16,256]{2,1,0:T(8,128)(2,1)} %shard_map.100), calls=%async_computation | async-start | bytes 524288 | tf_op jit(solution)/shard_map/all_to_all | solution.py:432
  32.7 9.6 %collective-permute-start.7 = (bf16[512,256]{1,0:T(8,128)(2,1)S(1)}, bf16[512,256]{1,0:T(8,128)(2,1)S(1)}, u32[]{:S(2)}, u32[]{:S(2)}) collective-permute-start(bf16[512,256]{1,0:T(8,128)(2,1)S(1)} %get-tuple-element.58), channel_id=1, source_target_pairs={{0,1},{1,2},{2,3},{3,0},{4,5},{5,6},{6,7},{7,4},{8,9},{9,10},{10,1... | collective-permute-start | bytes 786440 | tf_op jit(solution)/shard_map/ppermute | solution.py:440
  35.5 7.1 %collective-permute-start.8 = (bf16[256,512]{1,0:T(8,128)(2,1)S(1)}, bf16[256,512]{1,0:T(8,128)(2,1)S(1)}, u32[]{:S(2)}, u32[]{:S(2)}) collective-permute-start(bf16[256,512]{1,0:T(8,128)(2,1)S(1)} %get-tuple-element.62), channel_id=1, source_target_pairs={{0,4},{4,8},{8,12},{12,16},{16,20},{20,24},{24,28},{28,32},{32,36}... | collective-permute-start | bytes 786440 | tf_op jit(solution)/shard_map/ppermute | solution.py:441
  39.3 9.1 %collective-permute-start.9 = (bf16[256,512]{1,0:T(8,128)(2,1)S(1)}, bf16[256,512]{1,0:T(8,128)(2,1)S(1)}, u32[]{:S(2)}, u32[]{:S(2)}) collective-permute-start(bf16[256,512]{1,0:T(8,128)(2,1)S(1)} %get-tuple-element.63), channel_id=1, source_target_pairs={{4,0},{8,4},{12,8},{16,12},{20,16},{24,20},{28,24},{32,28},{36,32}... | collective-permute-start | bytes 786440 | tf_op jit(solution)/shard_map/ppermute | solution.py:442

commit v3 on v2

--- a/solution.py
+++ b/solution.py
@@ -175,7 +175,7 @@
 
 
 def forward(queries, before, after, weight, tops, totals, sums,
-            attention, lse, own, first_up, second_up, first_down, edge):
+            attention, lse, own, first_ahead, second_ahead, first_behind, edge):
     widen(before, after, edge)
     width = queries.shape[1]
     for head in range(2):
@@ -201,9 +201,14 @@
         return mm(attention[...], weight[pl.ds(start, width), :], NT)
 
     own[...] = partial_to(here).astype(jnp.bfloat16)
-    first_up[...] = partial_to(here + 2).astype(jnp.bfloat16)
-    second_up[...] = partial_to(here + 1).astype(jnp.bfloat16)
-    first_down[...] = partial_to(here + 3).astype(jnp.bfloat16)
+    step = step_ahead()
+    first_ahead[...] = partial_to(here + 2).astype(jnp.bfloat16)
+    second_ahead[...] = partial_to(here + step).astype(jnp.bfloat16)
+    first_behind[...] = partial_to(here + heads - step).astype(jnp.bfloat16)
+
+
+def step_ahead():
+    return jnp.where(on_even(), 1, lax.axis_size("head") - 1)
 
 
 def product_of(shift, cot, attention, weight, keep, send):
@@ -220,11 +225,12 @@
     return mm(cot[...], weight[pl.ds(pl.multiple_of(owner * width, width), width), :], NN)
 
 
-def near_products(mine, below, above, attention, weight, keep, send, part):
+def near_products(mine, behind_cot, ahead_cot, attention, weight, keep, send, part):
     heads = lax.axis_size("head")
+    step = step_ahead()
     part[...] = (product_of(0, mine, attention, weight, keep, send)
-                 + product_of(heads - 1, below, attention, weight, keep, send)
-                 + product_of(1, above, attention, weight, keep, send))
+                 + product_of(heads - step, behind_cot, attention, weight, keep, send)
+                 + product_of(step, ahead_cot, attention, weight, keep, send))
 
 
 def far_products(opposite, attention, weight, near_keep, near_send, part, keep, send, grad_attention, deltas):
@@ -261,10 +267,10 @@
     return pairs
 
 
-def backward(queries, before, after, lse, grad_attention, deltas, second_up, from_below, own, from_above,
-             dscores, to_next, to_prev, edge, send_up, near, total):
-    send_up[...] = (second_up[...].astype(jnp.float32) + from_below[...].astype(jnp.float32)).astype(jnp.bfloat16)
-    near[...] = own[...].astype(jnp.float32) + from_above[...].astype(jnp.float32)
+def backward(queries, before, after, lse, grad_attention, deltas, second_ahead, from_behind, own, from_ahead,
+             dscores, to_next, to_prev, edge, send_ahead, near, total):
+    send_ahead[...] = (second_ahead[...].astype(jnp.float32) + from_behind[...].astype(jnp.float32)).astype(jnp.bfloat16)
+    near[...] = own[...].astype(jnp.float32) + from_ahead[...].astype(jnp.float32)
     widen(before, after, edge)
     width = queries.shape[1]
     for half in range(2):
@@ -334,7 +340,7 @@
         store.wait()
 
 
-def finish(near_out, last_below, own, from_prev, from_next, spread,
+def finish(near_out, last_behind, own, from_prev, from_next, spread,
            output, grad_keys, grad_values, grad_weight,
            output_here, grad_keys_here, grad_values_here, grad_weight_here, spread_here, load_sems, sems):
     loads = in_pieces(spread, spread_here, load_sems)
@@ -349,9 +355,9 @@
         stores.append(copy)
 
     top, bottom = pl.ds(0, 256), pl.ds(256, 256)
-    output_here[top] = (near_out[top] + last_below[top].astype(jnp.float32)).astype(jnp.bfloat16)
+    output_here[top] = (near_out[top] + last_behind[top].astype(jnp.float32)).astype(jnp.bfloat16)
     store(output_here.at[top], output.at[top])
-    output_here[bottom] = (near_out[bottom] + last_below[bottom].astype(jnp.float32)).astype(jnp.bfloat16)
+    output_here[bottom] = (near_out[bottom] + last_behind[bottom].astype(jnp.float32)).astype(jnp.bfloat16)
     store(output_here.at[bottom], output.at[bottom])
     twice = repeat_matrix(64, 2)
     four = repeat_matrix(64, 4)
@@ -384,15 +390,16 @@
     shards = lax.axis_size("seq")
     heads = lax.axis_size("head")
     features = out_weight.shape[0]
-    up = [(i, (i + 1) % heads) for i in range(heads)]
-    down = [(target, source) for source, target in up]
+    ahead = [(place * heads + head, place * heads + (head + (1 if place % 2 == 0 else heads - 1)) % heads)
+             for place in range(shards) for head in range(heads)]
+    behind = [(target, source) for source, target in ahead]
     swap = [(i, i ^ 1) for i in range(shards)]
     onward = [(i, (i + 1) % shards) for i in range(shards)]
     back = [(target, source) for source, target in onward]
     dma = pltpu.SemaphoreType.DMA
 
-    below = lax.ppermute(grad_out, "head", up)
-    above = lax.ppermute(grad_out, "head", down)
+    behind_cot = lax.ppermute(grad_out, ("seq", "head"), ahead)
+    ahead_cot = lax.ppermute(grad_out, ("seq", "head"), behind)
 
     mine, to_next, to_prev = run(
         prepare, (keys, values),
@@ -407,20 +414,20 @@
         forward_own, (queries, mine, to_next),
         [((2, rows), f32), ((2, rows), f32), ((2 * HEAD_DIM, rows), f32)],
         [pltpu.VMEM((256, 2 * width), bf16)], flops=10 ** 9, moved=2 << 20, far_args=(2,))
-    opposite = lax.ppermute(below, "head", up)
-
-    attention, lse, own_out, first_up, second_up, first_down = run(
+    opposite = lax.ppermute(behind_cot, ("seq", "head"), ahead)
+
+    attention, lse, own_out, first_ahead, second_ahead, first_behind = run(
         forward, (queries, before, after, out_weight, tops, totals, sums),
         [((rows, width), bf16), ((2, rows), f32), ((rows, width), bf16), ((rows, width), bf16),
          ((rows, width), bf16), ((rows, width), bf16)],
         [pltpu.VMEM((768, 2 * width), bf16)], flops=10 ** 9, moved=3 << 20)
-    from_below = lax.ppermute(first_up, "head", up)
-    from_above = lax.ppermute(first_down, "head", down)
+    from_behind = lax.ppermute(first_ahead, ("seq", "head"), ahead)
+    from_ahead = lax.ppermute(first_behind, ("seq", "head"), behind)
 
     chunk = features // shards
     shapes = [((shards // 2, chunk, width), f32), ((shards // 2, chunk, width), bf16)]
     keep, send, part = run(
-        near_products, (grad_out, below, above, attention, out_weight), shapes + [((rows, width), f32)],
+        near_products, (grad_out, behind_cot, ahead_cot, attention, out_weight), shapes + [((rows, width), f32)],
         flops=4 * 10 ** 8, moved=1 << 20)
     keep, send, grad_attention, deltas = run(
         far_products, (opposite, attention, out_weight, keep, send, part),
@@ -431,13 +438,13 @@
     groups = [list(range(core, shards, 2)) for core in range(2)]
     spread = lax.all_to_all(pairs, "seq", 0, 0, axis_index_groups=groups)
 
-    dscores, to_next, to_prev, edge, send_up, near_out = run(
+    dscores, to_next, to_prev, edge, send_ahead, near_out = run(
         backward,
-        (queries, before, after, lse, grad_attention, deltas, second_up, from_below, own_out, from_above),
+        (queries, before, after, lse, grad_attention, deltas, second_ahead, from_behind, own_out, from_ahead),
         [((4, 512, 256), bf16), ((256, 2 * width), bf16), ((256, 2 * width), bf16), ((768, 2 * width), bf16),
          ((rows, width), bf16), ((rows, width), f32)],
         [pltpu.VMEM((1536, 2 * width), f32)], flops=2 * 10 ** 9, moved=4 << 20)
-    last_below = lax.ppermute(send_up, "head", up)
+    last_behind = lax.ppermute(send_ahead, ("seq", "head"), ahead)
     grad_before = lax.ppermute(to_next, "seq", onward)
     grad_after = lax.ppermute(to_prev, "seq", back)
     grad_queries, own_grad = run(
@@ -448,7 +455,7 @@
 
     output, grad_keys, grad_values, grad_weight = run(
         finish,
-        (near_out, last_below, own_grad, grad_before, grad_after, spread),
+        (near_out, last_behind, own_grad, grad_before, grad_after, spread),
         [((rows, width), bf16)] * 3 + [((chunk, width), f32)],
         [pltpu.VMEM((rows, width), bf16)] * 3 + [pltpu.VMEM((chunk, width), f32)]
         + [pltpu.VMEM((shards // 2, chunk, width), bf16), dma((PIECES,)), dma((7,))],

time: 50.4 us -> 51.1 us (1.014)
  starting transfers between devices: 26.3 us -> 27 us
    ppermute x1, starting transfers between devices: 3.76 us -> 6.67 us  [local(): grad_before = lax.ppermute(to_next, 'seq', onward)]
    ppermute x6, starting transfers between devices: 8.34 us -> 5.59 us  [the longest x1 2.19 us: local(): from_ahead = lax.ppermute(first_behind, ('seq', 'head'), behind)]
    all_to_all x1, starting transfers between devices: 8.19 us -> 9.56 us  [local(): spread = lax.all_to_all(pairs, 'seq', 0, 0, axis_index_groups=groups)]
    ppermute x1, starting transfers between devices: 0.83 us -> 0.04 us  [local(): half_sum = lax.ppermute(send, 'seq', swap)]
  transfers between devices with their start and end apart: 12 -> 12, of which waited for: 3 -> 4; matrix products, arithmetic and copies ran while one was open for 0% -> 0% of each run, Pallas kernels for 20% -> 20%
where the time goes in v3:
time: 51.1 us; the launch traced here: 50.8 us
  starting transfers between devices  27 us (53%)
  Pallas kernels  12.2 us (24%)
  waiting for transfers between devices  7.79 us (15%)
  local copies, waits for them, and re-layouts  2.85 us (6%)
  between operations  0.95 us (2%)
    pallas_call x10, Pallas kernels, run(): pl.pallas_call(body, in_specs=[FAR if number in far_args else VMEM for nu...  12.2 us
    all_to_all x1, starting transfers between devices, local(): spread = lax.all_to_all(pairs, 'seq', 0, 0, axis_index_groups=groups)  9.56 us
    ppermute x1, starting transfers between devices, local(): grad_before = lax.ppermute(to_next, 'seq', onward)  6.67 us
    ppermute x1, waiting for transfers between devices, local(): grad_after = lax.ppermute(to_prev, 'seq', back)  5.8 us
    ppermute x1, starting transfers between devices, local(): before = lax.ppermute(to_next, 'seq', onward)  4.46 us
    unnamed x10, local copies, waits for them, and re-layouts  2.85 us
    ppermute x1, starting transfers between devices, local(): from_ahead = lax.ppermute(first_behind, ('seq', 'head'), behind)  2.19 us
    ppermute x1, starting transfers between devices, local(): ahead_cot = lax.ppermute(grad_out, ('seq', 'head'), behind)  2.13 us
  transfers between devices with their start and end apart: 12, of which 4 were waited for; matrix products, arithmetic and copies ran while one was open for 0% of the time, Pallas kernels for 20%

profile of v3, /device:TPU:127, one launch (start us, length us, event | category | flops | bytes accessed | tf_op | source)
XLA Modules:
  0.0 50.8 jit_solution(14898745414019417017)
XLA Ops:
  0.6 0.6 %collective-permute-start.2 = (bf16[512,256]{1,0:T(8,128)(2,1)}, bf16[512,256]{1,0:T(8,128)(2,1)S(1)}, u32[]{:S(2)}, u32[]{:S(2)}) collective-permute-start(bf16[512,256]{1,0:T(8,128)(2,1)} %mine.1), channel_id=1, source_target_pairs={{0,1},{1,2},{2,3},{3,0},{4,7},{5,4},{6,5},{7,6},{8,9},{9,10},{10,1... | collective-permute-start | bytes 786440 | tf_op jit(solution)/shard_map/ppermute | solution.py:401
  1.3 0.9 %copy-done.3 = bf16[512,256]{1,0:T(8,128)(2,1)S(1)} copy-done((bf16[512,256]{1,0:T(8,128)(2,1)S(1)}, bf16[512,256]{1,0:T(8,128)(2,1)}, u32[]{:S(2)}) %copy-start.3) | copy-done | bytes 262168
  2.2 0.9 %copy-done.4 = bf16[512,256]{1,0:T(8,128)(2,1)S(1)} copy-done((bf16[512,256]{1,0:T(8,128)(2,1)S(1)}, bf16[512,256]{1,0:T(8,128)(2,1)}, u32[]{:S(2)}) %copy-start.4) | copy-done | bytes 262168
  3.2 0.4 shard_map.92
  3.6 0.7 %collective-permute-start.1 = (bf16[256,512]{1,0:T(8,128)(2,1)S(1)}, bf16[256,512]{1,0:T(8,128)(2,1)S(1)}, u32[]{:S(2)}, u32[]{:S(2)}) collective-permute-start(bf16[256,512]{1,0:T(8,128)(2,1)S(1)} %get-tuple-element.40), channel_id=1, source_target_pairs={{4,0},{8,4},{12,8},{16,12},{20,16},{24,20},{28,24},{32,28},{36,32}... | collective-permute-start | bytes 786440 | tf_op jit(solution)/shard_map/ppermute | solution.py:409
  4.3 4.5 %collective-permute-start = (bf16[256,512]{1,0:T(8,128)(2,1)S(1)}, bf16[256,512]{1,0:T(8,128)(2,1)S(1)}, u32[]{:S(2)}, u32[]{:S(2)}) collective-permute-start(bf16[256,512]{1,0:T(8,128)(2,1)S(1)} %get-tuple-element.38._), channel_id=1, source_target_pairs={{0,4},{4,8},{8,12},{12,16},{16,20},{20,24},{24,28},{28,32},{32,36}... | collective-permute-start | bytes 786440 | tf_op jit(solution)/shard_map/ppermute | solution.py:408
  8.7 2.1 %collective-permute-start.4 = (bf16[512,256]{1,0:T(8,128)(2,1)}, bf16[512,256]{1,0:T(8,128)(2,1)S(1)}, u32[]{:S(2)}, u32[]{:S(2)}) collective-permute-start(bf16[512,256]{1,0:T(8,128)(2,1)} %mine.1), channel_id=1, source_target_pairs={{1,0},{2,1},{3,2},{0,3},{7,4},{4,5},{5,6},{6,7},{9,8},{10,9},{11,1... | collective-permute-start | bytes 786440 | tf_op jit(solution)/shard_map/ppermute | solution.py:402
  10.8 0.0 collective-permute-done.2.behind_cot
  10.8 0.0 collective-permute-start.3
  10.9 0.0 copy-start.1
  10.9 0.9 %copy-done.1 = bf16[512,256]{1,0:T(8,128)(2,1)S(1)} copy-done((bf16[512,256]{1,0:T(8,128)(2,1)S(1)}, bf16[512,256]{1,0:T(8,128)(2,1)}, u32[]{:S(2)}) %copy-start.1) | copy-done | bytes 262168
  11.8 0.1 shard_map.93
  11.9 1.3 %shard_map.94 = (f32[2,512]{1,0:T(2,128)S(1)}, f32[2,512]{1,0:T(2,128)S(1)}, f32[256,512]{1,0:T(8,128)S(1)}) custom-call(bf16[512,256]{1,0:T(8,128)(2,1)S(1)} %get-tuple-element.39.queries, bf16[512,512]{1,0:T(8,128)(2,1)S(1)} %get-tuple-element.42.mine, bf16[256,512]{1,0:T(8,128)(2,1)S(1)} %get-tuple-element.38._), custom_call_target="tpu_custom_call" | custom-call | flops 1000000000 | bytes 2097152 | tf_op jit(solution)/shard_map/pallas_call | solution.py:28
  13.2 0.0 collective-permute-done.1.after
  13.2 0.0 copy-start.2
  13.2 1.7 %shard_map.95 = (bf16[512,256]{1,0:T(8,128)(2,1)S(1)}, f32[2,512]{1,0:T(2,128)S(1)}, bf16[512,256]{1,0:T(8,128)(2,1)S(1)}, bf16[512,256]{1,0:T(8,128)(2,1)S(1)},...) custom-call(bf16[512,256]{1,0:T(8,128)(2,1)S(1)} %get-tuple-element.39.queries, ...), custom_call_target="tpu_custom_call" | custom-call | flops 1000000000 | bytes 3145728 | tf_op jit(solution)/shard_map/pallas_call | solution.py:28
  14.9 1.6 %collective-permute-done.4.ahead_cot = bf16[512,256]{1,0:T(8,128)(2,1)S(1)} collective-permute-done((bf16[512,256]{1,0:T(8,128)(2,1)}, bf16[512,256]{1,0:T(8,128)(2,1)S(1)}, u32[]{:S(2)}, u32[]{:S(2)}) %collective-permute-start.4) | collective-permute-done | bytes 262176 | tf_op jit(solution)/shard_map/ppermute | solution.py:402
  16.5 0.6 %shard_map.96 = (f32[32,16,256]{2,1,0:T(8,128)S(1)}, bf16[32,16,256]{2,1,0:T(8,128)(2,1)S(1)}, f32[512,256]{1,0:T(8,128)S(1)}) custom-call(bf16[512,256]{1,0:T(8,128)(2,1)S(1)} %copy-done.2, bf16[512,256]{1,0:T(8,128)(2,1)S(1)} %collective-permute-done.2.behind_cot, bf16[512,256]{1,0:T(8,128)(2,1)S(1)} %collective-permute-done.4.ahead_cot, ...), custom_call_target="tpu_custom_call" | custom-call | flops 400000000 | bytes 1048576 | tf_op jit(solution)/shard_map/pallas_call | solution.py:28
  17.1 0.2 collective-permute-done.3.opposite
  17.3 0.6 %shard_map.97 = (f32[32,16,256]{2,1,0:T(8,128)S(1)}, bf16[32,16,256]{2,1,0:T(8,128)(2,1)S(1)}, bf16[512,256]{1,0:T(8,128)(2,1)S(1)}, f32[2,512]{1,0:T(2,128)S(1)}) custom-call(bf16[512,256]{1,0:T(8,128)(2,1)S(1)} %collective-permute-done.3.opposite, bf16[512,256]{1,0:T(8,128)(2,1)S(1)} %get-tuple-element.47.attention, ...), custom_call_target="tpu_custom_call" | custom-call | tf_op jit(solution)/shard_map/pallas_call | solution.py:28
  17.8 0.0 collective-permute-start.10
  17.9 0.6 %collective-permute-start.5 = (bf16[512,256]{1,0:T(8,128)(2,1)S(1)}, bf16[512,256]{1,0:T(8,128)(2,1)S(1)}, u32[]{:S(2)}, u32[]{:S(2)}) collective-permute-start(bf16[512,256]{1,0:T(8,128)(2,1)S(1)} %get-tuple-element.54), channel_id=1, source_target_pairs={{0,1},{1,2},{2,3},{3,0},{4,7},{5,4},{6,5},{7,6},{8,9},{9,10},{10,1... | collective-permute-start | bytes 786440 | tf_op jit(solution)/shard_map/ppermute | solution.py:424
  18.5 2.2 %collective-permute-start.6 = (bf16[512,256]{1,0:T(8,128)(2,1)S(1)}, bf16[512,256]{1,0:T(8,128)(2,1)S(1)}, u32[]{:S(2)}, u32[]{:S(2)}) collective-permute-start(bf16[512,256]{1,0:T(8,128)(2,1)S(1)} %get-tuple-element.56), channel_id=1, source_target_pairs={{1,0},{2,1},{3,2},{0,3},{7,4},{4,5},{5,6},{6,7},{9,8},{10,9},{11,1... | collective-permute-start | bytes 786440 | tf_op jit(solution)/shard_map/ppermute | solution.py:425
  20.7 0.7 %shard_map.100 = bf16[32,16,256]{2,1,0:T(8,128)(2,1)} custom-call(f32[32,16,256]{2,1,0:T(8,128)S(1)} %get-tuple-element.64.keep, bf16[32,16,256]{2,1,0:T(8,128)(2,1)S(1)} %collective-permute-done.10.sibling), custom_call_target="tpu_custom_call" | custom-call | tf_op jit(solution)/shard_map/pallas_call | solution.py:28
  21.4 9.6 %all-to-all-start = ((bf16[32,16,256]{2,1,0:T(8,128)(2,1)}), bf16[32,16,256]{2,1,0:T(8,128)(2,1)S(1)}, u32[]{:S(2)}, u32[]{:S(2)}) async-start(bf16[32,16,256]{2,1,0:T(8,128)(2,1)} %shard_map.100), calls=%async_computation | async-start | bytes 524288 | tf_op jit(solution)/shard_map/all_to_all | solution.py:439
  31.0 2.2 %shard_map.98 = (bf16[4,512,256]{2,1,0:T(8,128)(2,1)S(1)}, bf16[256,512]{1,0:T(8,128)(2,1)S(1)}, bf16[256,512]{1,0:T(8,128)(2,1)S(1)}, bf16[768,512]{1,0:T(8,128...) custom-call(bf16[512,256]{1,0:T(8,128)(2,1)S(1)} %get-tuple-element.39.queries, ...), custom_call_target="tpu_custom_call" | custom-call | flops 2000000000 | bytes 4194304 | tf_op jit(solution)/shard_map/pallas_call | solution.py:28
  33.2 0.1 collective-permute-start.7
  33.3 6.7 %collective-permute-start.8 = (bf16[256,512]{1,0:T(8,128)(2,1)S(1)}, bf16[256,512]{1,0:T(8,128)(2,1)S(1)}, u32[]{:S(2)}, u32[]{:S(2)}) collective-permute-start(bf16[256,512]{1,0:T(8,128)(2,1)S(1)} %get-tuple-element.62), channel_id=1, source_target_pairs={{0,4},{4,8},{8,12},{12,16},{16,20},{20,24},{24,28},{28,32},{32,36}... | collective-permute-start | bytes 786440 | tf_op jit(solution)/shard_map/ppermute | solution.py:448
  39.9 3.1 %shard_map.99 = (bf16[512,256]{1,0:T(8,128)(2,1)}, bf16[512,512]{1,0:T(8,128)(2,1)S(1)}) custom-call(bf16[512,256]{1,0:T(8,128)(2,1)S(1)} %get-tuple-element.39.queries, bf16[512,512]{1,0:T(8,128)(2,1)S(1)} %get-tuple-element.42.mine, bf16[768,512]{1,0:T(8,128)(2,1)S(1)} %get-tuple-element.59.edge, f32[2,512]{1,0:T(2,128)S(1)} %get-tuple-element.46.lse, ...), custom_call_target="tpu_custom_call" | custom-call | flops 3000000000 | bytes 6291456 | tf_op jit(solution)/shard_map/pallas_call | solution.py:28
  43.1 0.2 collective-permute-done.8.from_prev
  43.3 5.8 %collective-permute-done.9.from_next = bf16[256,512]{1,0:T(8,128)(2,1)S(1)} collective-permute-done((bf16[256,512]{1,0:T(8,128)(2,1)S(1)}, bf16[256,512]{1,0:T(8,128)(2,1)S(1)}, u32[]{:S(2)}, u32[]{:S(2)}) %collective-permute-start.9) | collective-permute-done | bytes 262176 | tf_op jit(solution)/shard_map/ppermute | solution.py:449
  49.1 1.6 %shard_map.101 = (bf16[512,256]{1,0:T(8,128)(2,1)}, bf16[512,256]{1,0:T(8,128)(2,1)}, bf16[512,256]{1,0:T(8,128)(2,1)}, f32[16,256]{1,0:T(8,128)}) custom-call(f32[512,256]{1,0:T(8,128)S(1)} %get-tuple-element.57.near_out, bf16[512,256]{1,0:T(8,128)(2,1)S(1)} %collective-permute-done.7.last_behind, bf16[512,512]{1,0:T(8,128)(2,1)S(1)} %get-tuple-element.61.own, ...), custom_call_target="tpu_custom_call" | custom-call | bytes 4194304 | tf_op jit(solution)/shard_map/pallas_call | solution.py:28
  (12 shorter events, 0.0 us)
Async XLA Ops:
  0.6 10.2 %copy-start = (bf16[1024,256]{1,0:T(8,128)(2,1)S(1)}, bf16[1024,256]{1,0:T(8,128)(2,1)}, u32[]{:S(2)}) copy-start(bf16[1024,256]{1,0:T(8,128)(2,1)} %weight.1) | copy-start | bytes 1572868
  0.6 10.2 %collective-permute-start.2 = (bf16[512,256]{1,0:T(8,128)(2,1)}, bf16[512,256]{1,0:T(8,128)(2,1)S(1)}, u32[]{:S(2)}, u32[]{:S(2)}) collective-permute-start(bf16[512,256]{1,0:T(8,128)(2,1)} %mine.1), channel_id=1, source_target_pairs={{0,1},{1,2},{2,3},{3,0},{4,7},{5,4},{6,5},{7,6},{8,9},{9,10},{10,1... | collective-permute-start | bytes 786440 | tf_op jit(solution)/shard_map/ppermute | solution.py:401
  1.3 0.9 %copy-start.3 = (bf16[512,256]{1,0:T(8,128)(2,1)S(1)}, bf16[512,256]{1,0:T(8,128)(2,1)}, u32[]{:S(2)}) copy-start(bf16[512,256]{1,0:T(8,128)(2,1)} %keys.1) | copy-start | bytes 786436
  2.2 0.9 %copy-start.4 = (bf16[512,256]{1,0:T(8,128)(2,1)S(1)}, bf16[512,256]{1,0:T(8,128)(2,1)}, u32[]{:S(2)}) copy-start(bf16[512,256]{1,0:T(8,128)(2,1)} %values.1) | copy-start | bytes 786436
  3.6 9.6 %collective-permute-start.1 = (bf16[256,512]{1,0:T(8,128)(2,1)S(1)}, bf16[256,512]{1,0:T(8,128)(2,1)S(1)}, u32[]{:S(2)}, u32[]{:S(2)}) collective-permute-start(bf16[256,512]{1,0:T(8,128)(2,1)S(1)} %get-tuple-element.40), channel_id=1, source_target_pairs={{4,0},{8,4},{12,8},{16,12},{20,16},{24,20},{28,24},{32,28},{36,32}... | collective-permute-start | bytes 786440 | tf_op jit(solution)/shard_map/ppermute | solution.py:409
  4.3 8.9 %collective-permute-start = (bf16[256,512]{1,0:T(8,128)(2,1)S(1)}, bf16[256,512]{1,0:T(8,128)(2,1)S(1)}, u32[]{:S(2)}, u32[]{:S(2)}) collective-permute-start(bf16[256,512]{1,0:T(8,128)(2,1)S(1)} %get-tuple-element.38._), channel_id=1, source_target_pairs={{0,4},{4,8},{8,12},{12,16},{16,20},{20,24},{24,28},{28,32},{32,36}... | collective-permute-start | bytes 786440 | tf_op jit(solution)/shard_map/ppermute | solution.py:408
  8.7 7.8 %collective-permute-start.4 = (bf16[512,256]{1,0:T(8,128)(2,1)}, bf16[512,256]{1,0:T(8,128)(2,1)S(1)}, u32[]{:S(2)}, u32[]{:S(2)}) collective-permute-start(bf16[512,256]{1,0:T(8,128)(2,1)} %mine.1), channel_id=1, source_target_pairs={{1,0},{2,1},{3,2},{0,3},{7,4},{4,5},{5,6},{6,7},{9,8},{10,9},{11,1... | collective-permute-start | bytes 786440 | tf_op jit(solution)/shard_map/ppermute | solution.py:402
  10.8 6.4 %collective-permute-start.3 = (bf16[512,256]{1,0:T(8,128)(2,1)S(1)}, bf16[512,256]{1,0:T(8,128)(2,1)S(1)}, u32[]{:S(2)}, u32[]{:S(2)}) collective-permute-start(bf16[512,256]{1,0:T(8,128)(2,1)S(1)} %collective-permute-done.2.behind_cot), channel_id=1, source_target_pairs={{0,1},{1,2},{2,3},{3,0},{4,7},{5,4},{6,5},{7,6},{8,9},{9,10},{10,1... | collective-permute-start | bytes 786440 | tf_op jit(solution)/shard_map/ppermute | solution.py:417
  10.9 1.0 %copy-start.1 = (bf16[512,256]{1,0:T(8,128)(2,1)S(1)}, bf16[512,256]{1,0:T(8,128)(2,1)}, u32[]{:S(2)}) copy-start(bf16[512,256]{1,0:T(8,128)(2,1)} %queries.1) | copy-start | bytes 786436
  13.2 3.3 %copy-start.2 = (bf16[512,256]{1,0:T(8,128)(2,1)S(1)}, bf16[512,256]{1,0:T(8,128)(2,1)}, u32[]{:S(2)}) copy-start(bf16[512,256]{1,0:T(8,128)(2,1)} %mine.1) | copy-start | bytes 786436
  17.8 2.8 %collective-permute-start.10 = (bf16[32,16,256]{2,1,0:T(8,128)(2,1)S(1)}, bf16[32,16,256]{2,1,0:T(8,128)(2,1)S(1)}, u32[]{:S(2)}, u32[]{:S(2)}) collective-permute-start(bf16[32,16,256]{2,1,0:T(8,128)(2,1)S(1)} %get-tuple-element.65), channel_id=1, source_target_pairs={{0,4},{4,0},{8,12},{12,8},{16,20},{20,16},{24,28},{28,24},{32,36},... | collective-permute-start | bytes 786440 | tf_op jit(solution)/shard_map/ppermute | solution.py:435
  17.9 13.1 %collective-permute-start.5 = (bf16[512,256]{1,0:T(8,128)(2,1)S(1)}, bf16[512,256]{1,0:T(8,128)(2,1)S(1)}, u32[]{:S(2)}, u32[]{:S(2)}) collective-permute-start(bf16[512,256]{1,0:T(8,128)(2,1)S(1)} %get-tuple-element.54), channel_id=1, source_target_pairs={{0,1},{1,2},{2,3},{3,0},{4,7},{5,4},{6,5},{7,6},{8,9},{9,10},{10,1... | collective-permute-start | bytes 786440 | tf_op jit(solution)/shard_map/ppermute | solution.py:424
  18.5 12.5 %collective-permute-start.6 = (bf16[512,256]{1,0:T(8,128)(2,1)S(1)}, bf16[512,256]{1,0:T(8,128)(2,1)S(1)}, u32[]{:S(2)}, u32[]{:S(2)}) collective-permute-start(bf16[512,256]{1,0:T(8,128)(2,1)S(1)} %get-tuple-element.56), channel_id=1, source_target_pairs={{1,0},{2,1},{3,2},{0,3},{7,4},{4,5},{5,6},{6,7},{9,8},{10,9},{11,1... | collective-permute-start | bytes 786440 | tf_op jit(solution)/shard_map/ppermute | solution.py:425
  21.4 27.7 %all-to-all-start = ((bf16[32,16,256]{2,1,0:T(8,128)(2,1)}), bf16[32,16,256]{2,1,0:T(8,128)(2,1)S(1)}, u32[]{:S(2)}, u32[]{:S(2)}) async-start(bf16[32,16,256]{2,1,0:T(8,128)(2,1)} %shard_map.100), calls=%async_computation | async-start | bytes 524288 | tf_op jit(solution)/shard_map/all_to_all | solution.py:439
  33.2 9.9 %collective-permute-start.7 = (bf16[512,256]{1,0:T(8,128)(2,1)S(1)}, bf16[512,256]{1,0:T(8,128)(2,1)S(1)}, u32[]{:S(2)}, u32[]{:S(2)}) collective-permute-start(bf16[512,256]{1,0:T(8,128)(2,1)S(1)} %get-tuple-element.58), channel_id=1, source_target_pairs={{0,1},{1,2},{2,3},{3,0},{4,7},{5,4},{6,5},{7,6},{8,9},{9,10},{10,1... | collective-permute-start | bytes 786440 | tf_op jit(solution)/shard_map/ppermute | solution.py:447
  33.3 10.0 %collective-permute-start.8 = (bf16[256,512]{1,0:T(8,128)(2,1)S(1)}, bf16[256,512]{1,0:T(8,128)(2,1)S(1)}, u32[]{:S(2)}, u32[]{:S(2)}) collective-permute-start(bf16[256,512]{1,0:T(8,128)(2,1)S(1)} %get-tuple-element.62), channel_id=1, source_target_pairs={{0,4},{4,8},{8,12},{12,16},{16,20},{20,24},{24,28},{28,32},{32,36}... | collective-permute-start | bytes 786440 | tf_op jit(solution)/shard_map/ppermute | solution.py:448
  39.9 9.1 %collective-permute-start.9 = (bf16[256,512]{1,0:T(8,128)(2,1)S(1)}, bf16[256,512]{1,0:T(8,128)(2,1)S(1)}, u32[]{:S(2)}, u32[]{:S(2)}) collective-permute-start(bf16[256,512]{1,0:T(8,128)(2,1)S(1)} %get-tuple-element.63), channel_id=1, source_target_pairs={{4,0},{8,4},{12,8},{16,12},{20,16},{24,20},{28,24},{32,28},{36,32}... | collective-permute-start | bytes 786440 | tf_op jit(solution)/shard_map/ppermute | solution.py:449

commit v4 on v2

--- a/solution.py
+++ b/solution.py
@@ -206,31 +206,31 @@
     first_down[...] = partial_to(here + 3).astype(jnp.bfloat16)
 
 
-def product_of(shift, cot, attention, weight, keep, send):
-    heads = lax.axis_size("head")
-    owner = lax.rem(lax.axis_index("head") + shift, heads)
+def owner_of(shift):
+    return lax.rem(lax.axis_index("head") + shift, lax.axis_size("head"))
+
+
+def product_of(shift, place, cot, attention, weight, keep, send):
     even = on_even()
-    groups, rows, width = keep.shape
-    each = groups // heads
+    rows, width = keep.shape[1:]
+    each = cot.shape[1] // (2 * rows)
     chunks = mm(cot[...], attention[...], TN).reshape(each, 2, rows, width)
     first, second = chunks[:, 0], chunks[:, 1]
-    start = owner * each
-    keep[pl.ds(start, each)] = jnp.where(even, first, second)
-    send[pl.ds(start, each)] = jnp.where(even, second, first).astype(jnp.bfloat16)
-    return mm(cot[...], weight[pl.ds(pl.multiple_of(owner * width, width), width), :], NN)
+    span = slice(place * each, place * each + each)
+    keep[span] = jnp.where(even, first, second)
+    send[span] = jnp.where(even, second, first).astype(jnp.bfloat16)
+    return mm(cot[...], weight[pl.ds(pl.multiple_of(owner_of(shift) * width, width), width), :], NN)
 
 
 def near_products(mine, below, above, attention, weight, keep, send, part):
     heads = lax.axis_size("head")
-    part[...] = (product_of(0, mine, attention, weight, keep, send)
-                 + product_of(heads - 1, below, attention, weight, keep, send)
-                 + product_of(1, above, attention, weight, keep, send))
-
-
-def far_products(opposite, attention, weight, near_keep, near_send, part, keep, send, grad_attention, deltas):
-    keep[...] = near_keep[...]
-    send[...] = near_send[...]
-    rounded = (part[...] + product_of(2, opposite, attention, weight, keep, send)).astype(jnp.bfloat16)
+    part[...] = (product_of(0, 0, mine, attention, weight, keep, send)
+                 + product_of(heads - 1, 1, below, attention, weight, keep, send)
+                 + product_of(1, 2, above, attention, weight, keep, send))
+
+
+def far_products(opposite, attention, weight, part, keep, send, grad_attention, deltas):
+    rounded = (part[...] + product_of(2, 0, opposite, attention, weight, keep, send)).astype(jnp.bfloat16)
     grad_attention[...] = rounded
     terms = rounded.astype(jnp.float32) * attention[...].astype(jnp.float32)
     high = terms.astype(jnp.bfloat16)
@@ -241,13 +241,17 @@
         deltas[head:head + 1] = (mm(ones, high[:, cols], NT) + mm(ones, low[:, cols], NT))[0:1]
 
 
-def pair_sum(keep, sibling, pairs, pairs_here, sems):
-    stores = in_pieces(pairs_here, pairs, sems)
-    size = pairs.shape[0] // len(stores)
-    for number, store in enumerate(stores):
-        span = pl.ds(number * size, size)
-        pairs_here[span] = (keep[span] + sibling[span].astype(jnp.float32)).astype(jnp.bfloat16)
-        store.start()
+def pair_sum(near_keep, near_sibling, far_keep, far_sibling, pairs, pairs_here, sems):
+    heads = lax.axis_size("head")
+    each = far_keep.shape[0]
+    stores = []
+    for place, shift in enumerate((0, heads - 1, 1, 2)):
+        keep, sibling = (near_keep, near_sibling) if place < 3 else (far_keep, far_sibling)
+        source = pl.ds(place * each if place < 3 else 0, each)
+        target = pl.ds(owner_of(shift) * each, each)
+        pairs_here[target] = (keep[source] + sibling[source].astype(jnp.float32)).astype(jnp.bfloat16)
+        stores.append(pltpu.make_async_copy(pairs_here.at[target], pairs.at[target], sems.at[place]))
+        stores[-1].start()
     for store in stores:
         store.wait()
 
@@ -418,16 +422,18 @@
     from_above = lax.ppermute(first_down, "head", down)
 
     chunk = features // shards
-    shapes = [((shards // 2, chunk, width), f32), ((shards // 2, chunk, width), bf16)]
-    keep, send, part = run(
-        near_products, (grad_out, below, above, attention, out_weight), shapes + [((rows, width), f32)],
+    each = shards // 2 // heads
+    near_keep, near_send, part = run(
+        near_products, (grad_out, below, above, attention, out_weight),
+        [((3 * each, chunk, width), f32), ((3 * each, chunk, width), bf16), ((rows, width), f32)],
         flops=4 * 10 ** 8, moved=1 << 20)
-    keep, send, grad_attention, deltas = run(
-        far_products, (opposite, attention, out_weight, keep, send, part),
-        shapes + [((rows, width), bf16), ((2, rows), f32)])
-    half_sum = lax.ppermute(send, "seq", swap)
-    pairs, = run(pair_sum, (keep, half_sum), [((shards // 2, chunk, width), bf16)],
-                 [pltpu.VMEM((shards // 2, chunk, width), bf16), dma((PIECES,))], far_outs=(0,))
+    near_sum = lax.ppermute(near_send, "seq", swap)
+    far_keep, far_send, grad_attention, deltas = run(
+        far_products, (opposite, attention, out_weight, part),
+        [((each, chunk, width), f32), ((each, chunk, width), bf16), ((rows, width), bf16), ((2, rows), f32)])
+    far_sum = lax.ppermute(far_send, "seq", swap)
+    pairs, = run(pair_sum, (near_keep, near_sum, far_keep, far_sum), [((shards // 2, chunk, width), bf16)],
+                 [pltpu.VMEM((shards // 2, chunk, width), bf16), dma((4,))], far_outs=(0,))
     groups = [list(range(core, shards, 2)) for core in range(2)]
     spread = lax.all_to_all(pairs, "seq", 0, 0, axis_index_groups=groups)
 

time: 50.4 us -> 51.3 us (1.018)
  starting transfers between devices: 26.3 us -> 23.9 us
  waiting for transfers between devices: 7.88 us -> 10.2 us
  local copies, waits for them, and re-layouts: 2.86 us -> 3.81 us
    ppermute x1, starting transfers between devices: 2.63 us -> 0.26 us  [local(): from_below = lax.ppermute(first_up, 'head', up)]
    ppermute x1, starting transfers between devices: 0.01 us -> 1.28 us  [local(): from_above = lax.ppermute(first_down, 'head', down)]
    ppermute x1 -> x2, waiting for transfers between devices: 0.01 us -> 1.24 us  [the longest x1 1.24 us: local(): far_sum = lax.ppermute(far_send, 'seq', swap)]
    ppermute x1, waiting for transfers between devices: 1.87 us -> 3 us  [local(): opposite = lax.ppermute(below, 'head', up)]
    unnamed x10 -> x14, local copies, waits for them, and re-layouts: 2.86 us -> 3.81 us
    ppermute x1 -> x2, starting transfers between devices: 0.83 us -> 0.12 us  [the longest x1 0.09 us: local(): near_sum = lax.ppermute(near_send, 'seq', swap)]
  transfers between devices with their start and end apart: 12 -> 13, of which waited for: 3 -> 4; matrix products, arithmetic and copies ran while one was open for 0% -> 0% of each run, Pallas kernels for 20% -> 21%
where the time goes in v4:
time: 51.3 us; the launch traced here: 51.1 us
  starting transfers between devices  23.9 us (47%)
  Pallas kernels  12.2 us (24%)
  waiting for transfers between devices  10.2 us (20%)
  local copies, waits for them, and re-layouts  3.81 us (7%)
  between operations  0.96 us (2%)
    pallas_call x10, Pallas kernels, run(): pl.pallas_call(body, in_specs=[FAR if number in far_args else VMEM for nu...  12.2 us
    all_to_all x1, starting transfers between devices, local(): spread = lax.all_to_all(pairs, 'seq', 0, 0, axis_index_groups=groups)  8.07 us
    ppermute x1, waiting for transfers between devices, local(): grad_after = lax.ppermute(to_prev, 'seq', back)  5.8 us
    ppermute x1, starting transfers between devices, local(): before = lax.ppermute(to_next, 'seq', onward)  4.11 us
    unnamed x14, local copies, waits for them, and re-layouts  3.81 us
    ppermute x1, starting transfers between devices, local(): grad_before = lax.ppermute(to_next, 'seq', onward)  3.28 us
    ppermute x1, waiting for transfers between devices, local(): opposite = lax.ppermute(below, 'head', up)  3 us
    ppermute x1, starting transfers between devices, local(): last_below = lax.ppermute(send_up, 'head', up)  2.7 us
  transfers between devices with their start and end apart: 13, of which 4 were waited for; matrix products, arithmetic and copies ran while one was open for 0% of the time, Pallas kernels for 21%

profile of v4, /device:TPU:127, one launch (start us, length us, event | category | flops | bytes accessed | tf_op | source)
XLA Modules:
  0.0 51.1 jit_solution(17335993471803336789)
XLA Ops:
  0.6 0.3 collective-permute-start.2
  0.9 0.9 %copy-done.3 = bf16[512,256]{1,0:T(8,128)(2,1)S(1)} copy-done((bf16[512,256]{1,0:T(8,128)(2,1)S(1)}, bf16[512,256]{1,0:T(8,128)(2,1)}, u32[]{:S(2)}) %copy-start.3) | copy-done | bytes 262168
  1.9 0.9 %copy-done.4 = bf16[512,256]{1,0:T(8,128)(2,1)S(1)} copy-done((bf16[512,256]{1,0:T(8,128)(2,1)S(1)}, bf16[512,256]{1,0:T(8,128)(2,1)}, u32[]{:S(2)}) %copy-start.4) | copy-done | bytes 262168
  2.8 0.4 shard_map.92
  3.2 1.0 %collective-permute-start.1 = (bf16[256,512]{1,0:T(8,128)(2,1)S(1)}, bf16[256,512]{1,0:T(8,128)(2,1)S(1)}, u32[]{:S(2)}, u32[]{:S(2)}) collective-permute-start(bf16[256,512]{1,0:T(8,128)(2,1)S(1)} %get-tuple-element.40), channel_id=1, source_target_pairs={{4,0},{8,4},{12,8},{16,12},{20,16},{24,20},{28,24},{32,28},{36,32}... | collective-permute-start | bytes 786440 | tf_op jit(solution)/shard_map/ppermute | solution.py:406
  4.3 4.1 %collective-permute-start = (bf16[256,512]{1,0:T(8,128)(2,1)S(1)}, bf16[256,512]{1,0:T(8,128)(2,1)S(1)}, u32[]{:S(2)}, u32[]{:S(2)}) collective-permute-start(bf16[256,512]{1,0:T(8,128)(2,1)S(1)} %get-tuple-element.38._), channel_id=1, source_target_pairs={{0,4},{4,8},{8,12},{12,16},{16,20},{20,24},{24,28},{28,32},{32,36}... | collective-permute-start | bytes 786440 | tf_op jit(solution)/shard_map/ppermute | solution.py:405
  8.4 1.3 %collective-permute-start.4 = (bf16[512,256]{1,0:T(8,128)(2,1)}, bf16[512,256]{1,0:T(8,128)(2,1)S(1)}, u32[]{:S(2)}, u32[]{:S(2)}) collective-permute-start(bf16[512,256]{1,0:T(8,128)(2,1)} %mine.1), channel_id=1, source_target_pairs={{1,0},{2,1},{3,2},{0,3},{5,4},{6,5},{7,6},{4,7},{9,8},{10,9},{11,1... | collective-permute-start | bytes 786440 | tf_op jit(solution)/shard_map/ppermute | solution.py:399
  9.6 0.9 %copy-done.1 = bf16[512,256]{1,0:T(8,128)(2,1)S(1)} copy-done((bf16[512,256]{1,0:T(8,128)(2,1)S(1)}, bf16[512,256]{1,0:T(8,128)(2,1)}, u32[]{:S(2)}) %copy-start.1) | copy-done | bytes 262168
  10.6 0.1 shard_map.93
  10.6 1.3 %shard_map.94 = (f32[2,512]{1,0:T(2,128)S(1)}, f32[2,512]{1,0:T(2,128)S(1)}, f32[256,512]{1,0:T(8,128)S(1)}) custom-call(bf16[512,256]{1,0:T(8,128)(2,1)S(1)} %get-tuple-element.39.queries, bf16[512,512]{1,0:T(8,128)(2,1)S(1)} %get-tuple-element.42.mine, bf16[256,512]{1,0:T(8,128)(2,1)S(1)} %get-tuple-element.38._), custom_call_target="tpu_custom_call" | custom-call | flops 1000000000 | bytes 2097152 | tf_op jit(solution)/shard_map/pallas_call | solution.py:28
  11.9 1.5 %collective-permute-start.3 = (bf16[512,256]{1,0:T(8,128)(2,1)S(1)}, bf16[512,256]{1,0:T(8,128)(2,1)S(1)}, u32[]{:S(2)}, u32[]{:S(2)}) collective-permute-start(bf16[512,256]{1,0:T(8,128)(2,1)S(1)} %collective-permute-done.2.below), channel_id=1, source_target_pairs={{0,1},{1,2},{2,3},{3,0},{4,5},{5,6},{6,7},{7,4},{8,9},{9,10},{10,1... | collective-permute-start | bytes 786440 | tf_op jit(solution)/shard_map/ppermute | solution.py:414
  13.4 1.7 %shard_map.95 = (bf16[512,256]{1,0:T(8,128)(2,1)S(1)}, f32[2,512]{1,0:T(2,128)S(1)}, bf16[512,256]{1,0:T(8,128)(2,1)S(1)}, bf16[512,256]{1,0:T(8,128)(2,1)S(1)},...) custom-call(bf16[512,256]{1,0:T(8,128)(2,1)S(1)} %get-tuple-element.39.queries, ...), custom_call_target="tpu_custom_call" | custom-call | flops 1000000000 | bytes 3145728 | tf_op jit(solution)/shard_map/pallas_call | solution.py:28
  15.1 0.0 copy-start.5
  15.1 0.3 collective-permute-start.5
  15.4 1.3 %collective-permute-start.6 = (bf16[512,256]{1,0:T(8,128)(2,1)S(1)}, bf16[512,256]{1,0:T(8,128)(2,1)S(1)}, u32[]{:S(2)}, u32[]{:S(2)}) collective-permute-start(bf16[512,256]{1,0:T(8,128)(2,1)S(1)} %get-tuple-element.54), channel_id=1, source_target_pairs={{1,0},{2,1},{3,2},{0,3},{5,4},{6,5},{7,6},{4,7},{9,8},{10,9},{11,1... | collective-permute-start | bytes 786440 | tf_op jit(solution)/shard_map/ppermute | solution.py:422
  16.7 0.6 %shard_map.96 = (f32[24,16,256]{2,1,0:T(8,128)S(1)}, bf16[24,16,256]{2,1,0:T(8,128)(2,1)S(1)}, f32[512,256]{1,0:T(8,128)S(1)}) custom-call(bf16[512,256]{1,0:T(8,128)(2,1)S(1)} %copy-done.2, bf16[512,256]{1,0:T(8,128)(2,1)S(1)} %collective-permute-done.2.below, bf16[512,256]{1,0:T(8,128)(2,1)S(1)} %collective-permute-done.4.above, ...), custom_call_target="tpu_custom_call" | custom-call | flops 400000000 | bytes 1048576 | tf_op jit(solution)/shard_map/pallas_call | solution.py:28
  17.3 0.1 collective-permute-start.10
  17.4 3.0 %collective-permute-done.3.opposite = bf16[512,256]{1,0:T(8,128)(2,1)S(1)} collective-permute-done((bf16[512,256]{1,0:T(8,128)(2,1)S(1)}, bf16[512,256]{1,0:T(8,128)(2,1)S(1)}, u32[]{:S(2)}, u32[]{:S(2)}) %collective-permute-start.3) | collective-permute-done | bytes 262176 | tf_op jit(solution)/shard_map/ppermute | solution.py:414
  20.4 0.5 %shard_map.97 = (f32[8,16,256]{2,1,0:T(8,128)S(1)}, bf16[8,16,256]{2,1,0:T(8,128)(2,1)S(1)}, bf16[512,256]{1,0:T(8,128)(2,1)S(1)}, f32[2,512]{1,0:T(2,128)S(1)}) custom-call(bf16[512,256]{1,0:T(8,128)(2,1)S(1)} %collective-permute-done.3.opposite, bf16[512,256]{1,0:T(8,128)(2,1)S(1)} %get-tuple-element.47.attention, ...), custom_call_target="tpu_custom_call" | custom-call | tf_op jit(solution)/shard_map/pallas_call | solution.py:28
  20.9 0.0 collective-permute-start.11
  21.0 1.2 %collective-permute-done.11.far_sibling = bf16[8,16,256]{2,1,0:T(8,128)(2,1)S(1)} collective-permute-done((bf16[8,16,256]{2,1,0:T(8,128)(2,1)S(1)}, bf16[8,16,256]{2,1,0:T(8,128)(2,1)S(1)}, u32[]{:S(2)}, u32[]{:S(2)}) %collective-permute-start.11) | collective-permute-done | bytes 65568 | tf_op jit(solution)/shard_map/ppermute | solution.py:434
  22.2 0.7 %shard_map.100 = bf16[32,16,256]{2,1,0:T(8,128)(2,1)} custom-call(f32[24,16,256]{2,1,0:T(8,128)S(1)} %get-tuple-element.62.near_keep, bf16[24,16,256]{2,1,0:T(8,128)(2,1)S(1)} %collective-permute-done.10.near_sibling, f32[8,16,256]{2,1,0:T(8,128)S(1)} %get-tuple-element.64.far_keep, bf16[8,16,256]{2,1,0:T(8,128)(2,1)S(1)} %collective-permute-done.11.far_sibling), custom_call_target="tpu_custom_call" | custom-call | tf_op jit(solution)/shard_map/pallas_call | solution.py:28
  23.0 8.1 %all-to-all-start = ((bf16[32,16,256]{2,1,0:T(8,128)(2,1)}), bf16[32,16,256]{2,1,0:T(8,128)(2,1)S(1)}, u32[]{:S(2)}, u32[]{:S(2)}) async-start(bf16[32,16,256]{2,1,0:T(8,128)(2,1)} %shard_map.100), calls=%async_computation | async-start | bytes 524288 | tf_op jit(solution)/shard_map/all_to_all | solution.py:438
  31.1 0.0 copy-start.6
  31.1 0.9 %copy-done.6 = bf16[512,256]{1,0:T(8,128)(2,1)S(1)} copy-done((bf16[512,256]{1,0:T(8,128)(2,1)S(1)}, bf16[512,256]{1,0:T(8,128)(2,1)}, u32[]{:S(2)}) %copy-start.6) | copy-done | bytes 262168
  32.0 2.2 %shard_map.98 = (bf16[4,512,256]{2,1,0:T(8,128)(2,1)S(1)}, bf16[256,512]{1,0:T(8,128)(2,1)S(1)}, bf16[256,512]{1,0:T(8,128)(2,1)S(1)}, bf16[768,512]{1,0:T(8,128...) custom-call(bf16[512,256]{1,0:T(8,128)(2,1)S(1)} %get-tuple-element.39.queries, ...), custom_call_target="tpu_custom_call" | custom-call | flops 2000000000 | bytes 4194304 | tf_op jit(solution)/shard_map/pallas_call | solution.py:28
  34.2 2.7 %collective-permute-start.7 = (bf16[512,256]{1,0:T(8,128)(2,1)S(1)}, bf16[512,256]{1,0:T(8,128)(2,1)S(1)}, u32[]{:S(2)}, u32[]{:S(2)}) collective-permute-start(bf16[512,256]{1,0:T(8,128)(2,1)S(1)} %get-tuple-element.56), channel_id=1, source_target_pairs={{0,1},{1,2},{2,3},{3,0},{4,5},{5,6},{6,7},{7,4},{8,9},{9,10},{10,1... | collective-permute-start | bytes 786440 | tf_op jit(solution)/shard_map/ppermute | solution.py:446
  36.9 3.3 %collective-permute-start.8 = (bf16[256,512]{1,0:T(8,128)(2,1)S(1)}, bf16[256,512]{1,0:T(8,128)(2,1)S(1)}, u32[]{:S(2)}, u32[]{:S(2)}) collective-permute-start(bf16[256,512]{1,0:T(8,128)(2,1)S(1)} %get-tuple-element.60), channel_id=1, source_target_pairs={{0,4},{4,8},{8,12},{12,16},{16,20},{20,24},{24,28},{28,32},{32,36}... | collective-permute-start | bytes 786440 | tf_op jit(solution)/shard_map/ppermute | solution.py:447
  40.2 3.1 %shard_map.99 = (bf16[512,256]{1,0:T(8,128)(2,1)}, bf16[512,512]{1,0:T(8,128)(2,1)S(1)}) custom-call(bf16[512,256]{1,0:T(8,128)(2,1)S(1)} %get-tuple-element.39.queries, bf16[512,512]{1,0:T(8,128)(2,1)S(1)} %get-tuple-element.42.mine, bf16[768,512]{1,0:T(8,128)(2,1)S(1)} %get-tuple-element.57.edge, f32[2,512]{1,0:T(2,128)S(1)} %get-tuple-element.46.lse, ...), custom_call_target="tpu_custom_call" | custom-call | flops 3000000000 | bytes 6291456 | tf_op jit(solution)/shard_map/pallas_call | solution.py:28
  43.3 0.2 collective-permute-done.8.from_prev
  43.5 5.8 %collective-permute-done.9.from_next = bf16[256,512]{1,0:T(8,128)(2,1)S(1)} collective-permute-done((bf16[256,512]{1,0:T(8,128)(2,1)S(1)}, bf16[256,512]{1,0:T(8,128)(2,1)S(1)}, u32[]{:S(2)}, u32[]{:S(2)}) %collective-permute-start.9) | collective-permute-done | bytes 262176 | tf_op jit(solution)/shard_map/ppermute | solution.py:448
  49.3 1.6 %shard_map.101 = (bf16[512,256]{1,0:T(8,128)(2,1)}, bf16[512,256]{1,0:T(8,128)(2,1)}, bf16[512,256]{1,0:T(8,128)(2,1)}, f32[16,256]{1,0:T(8,128)}) custom-call(f32[512,256]{1,0:T(8,128)S(1)} %get-tuple-element.55.near_out, bf16[512,256]{1,0:T(8,128)(2,1)S(1)} %collective-permute-done.7.last_below, bf16[512,512]{1,0:T(8,128)(2,1)S(1)} %get-tuple-element.59.own, ...), custom_call_target="tpu_custom_call" | custom-call | bytes 4194304 | tf_op jit(solution)/shard_map/pallas_call | solution.py:28
  (18 shorter events, 0.0 us)
Async XLA Ops:
  0.6 9.0 %copy-start = (bf16[1024,256]{1,0:T(8,128)(2,1)S(1)}, bf16[1024,256]{1,0:T(8,128)(2,1)}, u32[]{:S(2)}) copy-start(bf16[1024,256]{1,0:T(8,128)(2,1)} %weight.1) | copy-start | bytes 1572868
  0.6 11.3 %collective-permute-start.2 = (bf16[512,256]{1,0:T(8,128)(2,1)}, bf16[512,256]{1,0:T(8,128)(2,1)S(1)}, u32[]{:S(2)}, u32[]{:S(2)}) collective-permute-start(bf16[512,256]{1,0:T(8,128)(2,1)} %mine.1), channel_id=1, source_target_pairs={{0,1},{1,2},{2,3},{3,0},{4,5},{5,6},{6,7},{7,4},{8,9},{9,10},{10,1... | collective-permute-start | bytes 786440 | tf_op jit(solution)/shard_map/ppermute | solution.py:398
  0.9 0.9 %copy-start.3 = (bf16[512,256]{1,0:T(8,128)(2,1)S(1)}, bf16[512,256]{1,0:T(8,128)(2,1)}, u32[]{:S(2)}) copy-start(bf16[512,256]{1,0:T(8,128)(2,1)} %keys.1) | copy-start | bytes 786436
  1.9 0.9 %copy-start.4 = (bf16[512,256]{1,0:T(8,128)(2,1)S(1)}, bf16[512,256]{1,0:T(8,128)(2,1)}, u32[]{:S(2)}) copy-start(bf16[512,256]{1,0:T(8,128)(2,1)} %values.1) | copy-start | bytes 786436
  3.2 10.2 %collective-permute-start.1 = (bf16[256,512]{1,0:T(8,128)(2,1)S(1)}, bf16[256,512]{1,0:T(8,128)(2,1)S(1)}, u32[]{:S(2)}, u32[]{:S(2)}) collective-permute-start(bf16[256,512]{1,0:T(8,128)(2,1)S(1)} %get-tuple-element.40), channel_id=1, source_target_pairs={{4,0},{8,4},{12,8},{16,12},{20,16},{24,20},{28,24},{32,28},{36,32}... | collective-permute-start | bytes 786440 | tf_op jit(solution)/shard_map/ppermute | solution.py:406
  4.3 9.2 %collective-permute-start = (bf16[256,512]{1,0:T(8,128)(2,1)S(1)}, bf16[256,512]{1,0:T(8,128)(2,1)S(1)}, u32[]{:S(2)}, u32[]{:S(2)}) collective-permute-start(bf16[256,512]{1,0:T(8,128)(2,1)S(1)} %get-tuple-element.38._), channel_id=1, source_target_pairs={{0,4},{4,8},{8,12},{12,16},{16,20},{20,24},{24,28},{28,32},{32,36}... | collective-permute-start | bytes 786440 | tf_op jit(solution)/shard_map/ppermute | solution.py:405
  8.4 8.3 %collective-permute-start.4 = (bf16[512,256]{1,0:T(8,128)(2,1)}, bf16[512,256]{1,0:T(8,128)(2,1)S(1)}, u32[]{:S(2)}, u32[]{:S(2)}) collective-permute-start(bf16[512,256]{1,0:T(8,128)(2,1)} %mine.1), channel_id=1, source_target_pairs={{1,0},{2,1},{3,2},{0,3},{5,4},{6,5},{7,6},{4,7},{9,8},{10,9},{11,1... | collective-permute-start | bytes 786440 | tf_op jit(solution)/shard_map/ppermute | solution.py:399
  9.6 1.0 %copy-start.1 = (bf16[512,256]{1,0:T(8,128)(2,1)S(1)}, bf16[512,256]{1,0:T(8,128)(2,1)}, u32[]{:S(2)}) copy-start(bf16[512,256]{1,0:T(8,128)(2,1)} %queries.1) | copy-start | bytes 786436
  11.9 8.5 %collective-permute-start.3 = (bf16[512,256]{1,0:T(8,128)(2,1)S(1)}, bf16[512,256]{1,0:T(8,128)(2,1)S(1)}, u32[]{:S(2)}, u32[]{:S(2)}) collective-permute-start(bf16[512,256]{1,0:T(8,128)(2,1)S(1)} %collective-permute-done.2.below), channel_id=1, source_target_pairs={{0,1},{1,2},{2,3},{3,0},{4,5},{5,6},{6,7},{7,4},{8,9},{9,10},{10,1... | collective-permute-start | bytes 786440 | tf_op jit(solution)/shard_map/ppermute | solution.py:414
  13.4 3.2 %copy-start.2 = (bf16[512,256]{1,0:T(8,128)(2,1)S(1)}, bf16[512,256]{1,0:T(8,128)(2,1)}, u32[]{:S(2)}) copy-start(bf16[512,256]{1,0:T(8,128)(2,1)} %mine.1) | copy-start | bytes 786436
  15.1 2.2 %copy-start.5 = (bf16[512,256]{1,0:T(8,128)(2,1)}, bf16[512,256]{1,0:T(8,128)(2,1)S(1)}, u32[]{:S(2)}) copy-start(bf16[512,256]{1,0:T(8,128)(2,1)S(1)} %get-tuple-element.51.second_up) | copy-start | bytes 786436
  15.1 15.9 %collective-permute-start.5 = (bf16[512,256]{1,0:T(8,128)(2,1)S(1)}, bf16[512,256]{1,0:T(8,128)(2,1)S(1)}, u32[]{:S(2)}, u32[]{:S(2)}) collective-permute-start(bf16[512,256]{1,0:T(8,128)(2,1)S(1)} %get-tuple-element.52), channel_id=1, source_target_pairs={{0,1},{1,2},{2,3},{3,0},{4,5},{5,6},{6,7},{7,4},{8,9},{9,10},{10,1... | collective-permute-start | bytes 786440 | tf_op jit(solution)/shard_map/ppermute | solution.py:421
  15.4 15.7 %collective-permute-start.6 = (bf16[512,256]{1,0:T(8,128)(2,1)S(1)}, bf16[512,256]{1,0:T(8,128)(2,1)S(1)}, u32[]{:S(2)}, u32[]{:S(2)}) collective-permute-start(bf16[512,256]{1,0:T(8,128)(2,1)S(1)} %get-tuple-element.54), channel_id=1, source_target_pairs={{1,0},{2,1},{3,2},{0,3},{5,4},{6,5},{7,6},{4,7},{9,8},{10,9},{11,1... | collective-permute-start | bytes 786440 | tf_op jit(solution)/shard_map/ppermute | solution.py:422
  17.3 3.7 %collective-permute-start.10 = (bf16[24,16,256]{2,1,0:T(8,128)(2,1)S(1)}, bf16[24,16,256]{2,1,0:T(8,128)(2,1)S(1)}, u32[]{:S(2)}, u32[]{:S(2)}) collective-permute-start(bf16[24,16,256]{2,1,0:T(8,128)(2,1)S(1)} %get-tuple-element.63), channel_id=1, source_target_pairs={{0,4},{4,0},{8,12},{12,8},{16,20},{20,16},{24,28},{28,24},{32,36},... | collective-permute-start | bytes 589832 | tf_op jit(solution)/shard_map/ppermute | solution.py:430
  20.9 1.3 %collective-permute-start.11 = (bf16[8,16,256]{2,1,0:T(8,128)(2,1)S(1)}, bf16[8,16,256]{2,1,0:T(8,128)(2,1)S(1)}, u32[]{:S(2)}, u32[]{:S(2)}) collective-permute-start(bf16[8,16,256]{2,1,0:T(8,128)(2,1)S(1)} %get-tuple-element.65), channel_id=1, source_target_pairs={{0,4},{4,0},{8,12},{12,8},{16,20},{20,16},{24,28},{28,24},{32,36},... | collective-permute-start | bytes 196616 | tf_op jit(solution)/shard_map/ppermute | solution.py:434
  23.0 26.3 %all-to-all-start = ((bf16[32,16,256]{2,1,0:T(8,128)(2,1)}), bf16[32,16,256]{2,1,0:T(8,128)(2,1)S(1)}, u32[]{:S(2)}, u32[]{:S(2)}) async-start(bf16[32,16,256]{2,1,0:T(8,128)(2,1)} %shard_map.100), calls=%async_computation | async-start | bytes 524288 | tf_op jit(solution)/shard_map/all_to_all | solution.py:438
  31.1 1.0 %copy-start.6 = (bf16[512,256]{1,0:T(8,128)(2,1)S(1)}, bf16[512,256]{1,0:T(8,128)(2,1)}, u32[]{:S(2)}) copy-start(bf16[512,256]{1,0:T(8,128)(2,1)} %copy-done.5) | copy-start | bytes 786436
  34.2 9.1 %collective-permute-start.7 = (bf16[512,256]{1,0:T(8,128)(2,1)S(1)}, bf16[512,256]{1,0:T(8,128)(2,1)S(1)}, u32[]{:S(2)}, u32[]{:S(2)}) collective-permute-start(bf16[512,256]{1,0:T(8,128)(2,1)S(1)} %get-tuple-element.56), channel_id=1, source_target_pairs={{0,1},{1,2},{2,3},{3,0},{4,5},{5,6},{6,7},{7,4},{8,9},{9,10},{10,1... | collective-permute-start | bytes 786440 | tf_op jit(solution)/shard_map/ppermute | solution.py:446
  36.9 6.6 %collective-permute-start.8 = (bf16[256,512]{1,0:T(8,128)(2,1)S(1)}, bf16[256,512]{1,0:T(8,128)(2,1)S(1)}, u32[]{:S(2)}, u32[]{:S(2)}) collective-permute-start(bf16[256,512]{1,0:T(8,128)(2,1)S(1)} %get-tuple-element.60), channel_id=1, source_target_pairs={{0,4},{4,8},{8,12},{12,16},{16,20},{20,24},{24,28},{28,32},{32,36}... | collective-permute-start | bytes 786440 | tf_op jit(solution)/shard_map/ppermute | solution.py:447
  40.2 9.1 %collective-permute-start.9 = (bf16[256,512]{1,0:T(8,128)(2,1)S(1)}, bf16[256,512]{1,0:T(8,128)(2,1)S(1)}, u32[]{:S(2)}, u32[]{:S(2)}) collective-permute-start(bf16[256,512]{1,0:T(8,128)(2,1)S(1)} %get-tuple-element.61), channel_id=1, source_target_pairs={{4,0},{8,4},{12,8},{16,12},{20,16},{24,20},{28,24},{32,28},{36,32}... | collective-permute-start | bytes 786440 | tf_op jit(solution)/shard_map/ppermute | solution.py:448

commit v5 on v3

--- a/solution.py
+++ b/solution.py
@@ -201,14 +201,9 @@
         return mm(attention[...], weight[pl.ds(start, width), :], NT)
 
     own[...] = partial_to(here).astype(jnp.bfloat16)
-    step = step_ahead()
     first_ahead[...] = partial_to(here + 2).astype(jnp.bfloat16)
-    second_ahead[...] = partial_to(here + step).astype(jnp.bfloat16)
-    first_behind[...] = partial_to(here + heads - step).astype(jnp.bfloat16)
-
-
-def step_ahead():
-    return jnp.where(on_even(), 1, lax.axis_size("head") - 1)
+    second_ahead[...] = partial_to(here + heads - 1).astype(jnp.bfloat16)
+    first_behind[...] = partial_to(here + 1).astype(jnp.bfloat16)
 
 
 def product_of(shift, cot, attention, weight, keep, send):
@@ -227,10 +222,9 @@
 
 def near_products(mine, behind_cot, ahead_cot, attention, weight, keep, send, part):
     heads = lax.axis_size("head")
-    step = step_ahead()
     part[...] = (product_of(0, mine, attention, weight, keep, send)
-                 + product_of(heads - step, behind_cot, attention, weight, keep, send)
-                 + product_of(step, ahead_cot, attention, weight, keep, send))
+                 + product_of(1, behind_cot, attention, weight, keep, send)
+                 + product_of(heads - 1, ahead_cot, attention, weight, keep, send))
 
 
 def far_products(opposite, attention, weight, near_keep, near_send, part, keep, send, grad_attention, deltas):
@@ -390,16 +384,15 @@
     shards = lax.axis_size("seq")
     heads = lax.axis_size("head")
     features = out_weight.shape[0]
-    ahead = [(place * heads + head, place * heads + (head + (1 if place % 2 == 0 else heads - 1)) % heads)
-             for place in range(shards) for head in range(heads)]
+    ahead = [(i, (i - 1) % heads) for i in range(heads)]
     behind = [(target, source) for source, target in ahead]
     swap = [(i, i ^ 1) for i in range(shards)]
     onward = [(i, (i + 1) % shards) for i in range(shards)]
     back = [(target, source) for source, target in onward]
     dma = pltpu.SemaphoreType.DMA
 
-    behind_cot = lax.ppermute(grad_out, ("seq", "head"), ahead)
-    ahead_cot = lax.ppermute(grad_out, ("seq", "head"), behind)
+    behind_cot = lax.ppermute(grad_out, "head", ahead)
+    ahead_cot = lax.ppermute(grad_out, "head", behind)
 
     mine, to_next, to_prev = run(
         prepare, (keys, values),
@@ -414,15 +407,15 @@
         forward_own, (queries, mine, to_next),
         [((2, rows), f32), ((2, rows), f32), ((2 * HEAD_DIM, rows), f32)],
         [pltpu.VMEM((256, 2 * width), bf16)], flops=10 ** 9, moved=2 << 20, far_args=(2,))
-    opposite = lax.ppermute(behind_cot, ("seq", "head"), ahead)
+    opposite = lax.ppermute(behind_cot, "head", ahead)
 
     attention, lse, own_out, first_ahead, second_ahead, first_behind = run(
         forward, (queries, before, after, out_weight, tops, totals, sums),
         [((rows, width), bf16), ((2, rows), f32), ((rows, width), bf16), ((rows, width), bf16),
          ((rows, width), bf16), ((rows, width), bf16)],
         [pltpu.VMEM((768, 2 * width), bf16)], flops=10 ** 9, moved=3 << 20)
-    from_behind = lax.ppermute(first_ahead, ("seq", "head"), ahead)
-    from_ahead = lax.ppermute(first_behind, ("seq", "head"), behind)
+    from_behind = lax.ppermute(first_ahead, "head", ahead)
+    from_ahead = lax.ppermute(first_behind, "head", behind)
 
     chunk = features // shards
     shapes = [((shards // 2, chunk, width), f32), ((shards // 2, chunk, width), bf16)]
@@ -444,7 +437,7 @@
         [((4, 512, 256), bf16), ((256, 2 * width), bf16), ((256, 2 * width), bf16), ((768, 2 * width), bf16),
          ((rows, width), bf16), ((rows, width), f32)],
         [pltpu.VMEM((1536, 2 * width), f32)], flops=2 * 10 ** 9, moved=4 << 20)
-    last_behind = lax.ppermute(send_ahead, ("seq", "head"), ahead)
+    last_behind = lax.ppermute(send_ahead, "head", ahead)
     grad_before = lax.ppermute(to_next, "seq", onward)
     grad_after = lax.ppermute(to_prev, "seq", back)
     grad_queries, own_grad = run(

time: 51.1 us -> 52.7 us (1.031)
  the two profiles are of different devices: /device:TPU:127 before, /device:TPU:121 now
where the time goes in v5:
time: 52.7 us; the launch traced here: 52.4 us
  starting transfers between devices  29.3 us (56%)
  Pallas kernels  12.2 us (23%)
  waiting for transfers between devices  7.09 us (13%)
  local copies, waits for them, and re-layouts  2.86 us (5%)
  between operations  0.94 us (2%)
    pallas_call x10, Pallas kernels, run(): pl.pallas_call(body, in_specs=[FAR if number in far_args else VMEM for nu...  12.2 us
    all_to_all x1, starting transfers between devices, local(): spread = lax.all_to_all(pairs, 'seq', 0, 0, axis_index_groups=groups)  8.19 us
    ppermute x1, waiting for transfers between devices, local(): grad_after = lax.ppermute(to_prev, 'seq', back)  5.8 us
    ppermute x1, starting transfers between devices, local(): before = lax.ppermute(to_next, 'seq', onward)  4.11 us
    ppermute x1, starting transfers between devices, local(): grad_before = lax.ppermute(to_next, 'seq', onward)  3.76 us
    ppermute x1, starting transfers between devices, local(): from_behind = lax.ppermute(first_ahead, 'head', ahead)  3.43 us
    unnamed x10, local copies, waits for them, and re-layouts  2.86 us
    ppermute x1, starting transfers between devices, local(): last_behind = lax.ppermute(send_ahead, 'head', ahead)  2.75 us
  transfers between devices with their start and end apart: 12, of which 3 were waited for; matrix products, arithmetic and copies ran while one was open for 0% of the time, Pallas kernels for 19%

profile of v5, /device:TPU:121, one launch (start us, length us, event | category | flops | bytes accessed | tf_op | source)
XLA Modules:
  0.0 52.4 jit_solution(11634091738114250273)
XLA Ops:
  0.6 2.6 %collective-permute-start.2 = (bf16[512,256]{1,0:T(8,128)(2,1)}, bf16[512,256]{1,0:T(8,128)(2,1)S(1)}, u32[]{:S(2)}, u32[]{:S(2)}) collective-permute-start(bf16[512,256]{1,0:T(8,128)(2,1)} %mine.1), channel_id=1, source_target_pairs={{0,3},{1,0},{2,1},{3,2},{4,7},{5,4},{6,5},{7,6},{8,11},{9,8},{10,9... | collective-permute-start | bytes 786440 | tf_op jit(solution)/shard_map/ppermute | solution.py:394
  3.2 0.9 %copy-done.3 = bf16[512,256]{1,0:T(8,128)(2,1)S(1)} copy-done((bf16[512,256]{1,0:T(8,128)(2,1)S(1)}, bf16[512,256]{1,0:T(8,128)(2,1)}, u32[]{:S(2)}) %copy-start.3) | copy-done | bytes 262168
  4.1 0.9 %copy-done.4 = bf16[512,256]{1,0:T(8,128)(2,1)S(1)} copy-done((bf16[512,256]{1,0:T(8,128)(2,1)S(1)}, bf16[512,256]{1,0:T(8,128)(2,1)}, u32[]{:S(2)}) %copy-start.4) | copy-done | bytes 262168
  5.1 0.4 shard_map.92
  5.5 1.0 %collective-permute-start.1 = (bf16[256,512]{1,0:T(8,128)(2,1)S(1)}, bf16[256,512]{1,0:T(8,128)(2,1)S(1)}, u32[]{:S(2)}, u32[]{:S(2)}) collective-permute-start(bf16[256,512]{1,0:T(8,128)(2,1)S(1)} %get-tuple-element.40), channel_id=1, source_target_pairs={{4,0},{8,4},{12,8},{16,12},{20,16},{24,20},{28,24},{32,28},{36,32}... | collective-permute-start | bytes 786440 | tf_op jit(solution)/shard_map/ppermute | solution.py:402
  6.5 4.1 %collective-permute-start = (bf16[256,512]{1,0:T(8,128)(2,1)S(1)}, bf16[256,512]{1,0:T(8,128)(2,1)S(1)}, u32[]{:S(2)}, u32[]{:S(2)}) collective-permute-start(bf16[256,512]{1,0:T(8,128)(2,1)S(1)} %get-tuple-element.38._), channel_id=1, source_target_pairs={{0,4},{4,8},{8,12},{12,16},{16,20},{20,24},{24,28},{28,32},{32,36}... | collective-permute-start | bytes 786440 | tf_op jit(solution)/shard_map/ppermute | solution.py:401
  10.6 0.0 collective-permute-start.4
  10.7 0.0 collective-permute-done.2.behind_cot
  10.7 2.7 %collective-permute-start.3 = (bf16[512,256]{1,0:T(8,128)(2,1)S(1)}, bf16[512,256]{1,0:T(8,128)(2,1)S(1)}, u32[]{:S(2)}, u32[]{:S(2)}) collective-permute-start(bf16[512,256]{1,0:T(8,128)(2,1)S(1)} %collective-permute-done.2.behind_cot), channel_id=1, source_target_pairs={{0,3},{1,0},{2,1},{3,2},{4,7},{5,4},{6,5},{7,6},{8,11},{9,8},{10,9... | collective-permute-start | bytes 786440 | tf_op jit(solution)/shard_map/ppermute | solution.py:410
  13.3 0.9 %copy-done.1 = bf16[512,256]{1,0:T(8,128)(2,1)S(1)} copy-done((bf16[512,256]{1,0:T(8,128)(2,1)S(1)}, bf16[512,256]{1,0:T(8,128)(2,1)}, u32[]{:S(2)}) %copy-start.1) | copy-done | bytes 262168
  14.3 0.1 shard_map.93
  14.3 1.3 %shard_map.94 = (f32[2,512]{1,0:T(2,128)S(1)}, f32[2,512]{1,0:T(2,128)S(1)}, f32[256,512]{1,0:T(8,128)S(1)}) custom-call(bf16[512,256]{1,0:T(8,128)(2,1)S(1)} %get-tuple-element.39.queries, bf16[512,512]{1,0:T(8,128)(2,1)S(1)} %get-tuple-element.42.mine, bf16[256,512]{1,0:T(8,128)(2,1)S(1)} %get-tuple-element.38._), custom_call_target="tpu_custom_call" | custom-call | flops 1000000000 | bytes 2097152 | tf_op jit(solution)/shard_map/pallas_call | solution.py:28
  15.6 0.0 collective-permute-done.1.after
  15.7 0.0 copy-start.2
  15.7 1.7 %shard_map.95 = (bf16[512,256]{1,0:T(8,128)(2,1)S(1)}, f32[2,512]{1,0:T(2,128)S(1)}, bf16[512,256]{1,0:T(8,128)(2,1)S(1)}, bf16[512,256]{1,0:T(8,128)(2,1)S(1)},...) custom-call(bf16[512,256]{1,0:T(8,128)(2,1)S(1)} %get-tuple-element.39.queries, ...), custom_call_target="tpu_custom_call" | custom-call | flops 1000000000 | bytes 3145728 | tf_op jit(solution)/shard_map/pallas_call | solution.py:28
  17.3 0.0 collective-permute-done.4.ahead_cot
  17.3 0.6 %shard_map.96 = (f32[32,16,256]{2,1,0:T(8,128)S(1)}, bf16[32,16,256]{2,1,0:T(8,128)(2,1)S(1)}, f32[512,256]{1,0:T(8,128)S(1)}) custom-call(bf16[512,256]{1,0:T(8,128)(2,1)S(1)} %copy-done.2, bf16[512,256]{1,0:T(8,128)(2,1)S(1)} %collective-permute-done.2.behind_cot, bf16[512,256]{1,0:T(8,128)(2,1)S(1)} %collective-permute-done.4.ahead_cot, ...), custom_call_target="tpu_custom_call" | custom-call | flops 400000000 | bytes 1048576 | tf_op jit(solution)/shard_map/pallas_call | solution.py:28
  18.0 1.1 %collective-permute-done.3.opposite = bf16[512,256]{1,0:T(8,128)(2,1)S(1)} collective-permute-done((bf16[512,256]{1,0:T(8,128)(2,1)S(1)}, bf16[512,256]{1,0:T(8,128)(2,1)S(1)}, u32[]{:S(2)}, u32[]{:S(2)}) %collective-permute-start.3) | collective-permute-done | bytes 262176 | tf_op jit(solution)/shard_map/ppermute | solution.py:410
  19.1 0.6 %shard_map.97 = (f32[32,16,256]{2,1,0:T(8,128)S(1)}, bf16[32,16,256]{2,1,0:T(8,128)(2,1)S(1)}, bf16[512,256]{1,0:T(8,128)(2,1)S(1)}, f32[2,512]{1,0:T(2,128)S(1)}) custom-call(bf16[512,256]{1,0:T(8,128)(2,1)S(1)} %collective-permute-done.3.opposite, bf16[512,256]{1,0:T(8,128)(2,1)S(1)} %get-tuple-element.47.attention, ...), custom_call_target="tpu_custom_call" | custom-call | tf_op jit(solution)/shard_map/pallas_call | solution.py:28
  19.6 0.8 %collective-permute-start.10 = (bf16[32,16,256]{2,1,0:T(8,128)(2,1)S(1)}, bf16[32,16,256]{2,1,0:T(8,128)(2,1)S(1)}, u32[]{:S(2)}, u32[]{:S(2)}) collective-permute-start(bf16[32,16,256]{2,1,0:T(8,128)(2,1)S(1)} %get-tuple-element.65), channel_id=1, source_target_pairs={{0,4},{4,0},{8,12},{12,8},{16,20},{20,16},{24,28},{28,24},{32,36},... | collective-permute-start | bytes 786440 | tf_op jit(solution)/shard_map/ppermute | solution.py:428
  20.4 3.4 %collective-permute-start.5 = (bf16[512,256]{1,0:T(8,128)(2,1)S(1)}, bf16[512,256]{1,0:T(8,128)(2,1)S(1)}, u32[]{:S(2)}, u32[]{:S(2)}) collective-permute-start(bf16[512,256]{1,0:T(8,128)(2,1)S(1)} %get-tuple-element.54), channel_id=1, source_target_pairs={{0,3},{1,0},{2,1},{3,2},{4,7},{5,4},{6,5},{7,6},{8,11},{9,8},{10,9... | collective-permute-start | bytes 786440 | tf_op jit(solution)/shard_map/ppermute | solution.py:417
  23.9 0.7 %shard_map.100 = bf16[32,16,256]{2,1,0:T(8,128)(2,1)} custom-call(f32[32,16,256]{2,1,0:T(8,128)S(1)} %get-tuple-element.64.keep, bf16[32,16,256]{2,1,0:T(8,128)(2,1)S(1)} %collective-permute-done.10.sibling), custom_call_target="tpu_custom_call" | custom-call | tf_op jit(solution)/shard_map/pallas_call | solution.py:28
  24.6 8.2 %all-to-all-start = ((bf16[32,16,256]{2,1,0:T(8,128)(2,1)}), bf16[32,16,256]{2,1,0:T(8,128)(2,1)S(1)}, u32[]{:S(2)}, u32[]{:S(2)}) async-start(bf16[32,16,256]{2,1,0:T(8,128)(2,1)} %shard_map.100), calls=%async_computation | async-start | bytes 524288 | tf_op jit(solution)/shard_map/all_to_all | solution.py:432
  32.8 0.0 collective-permute-done.6.from_ahead
  32.8 2.2 %shard_map.98 = (bf16[4,512,256]{2,1,0:T(8,128)(2,1)S(1)}, bf16[256,512]{1,0:T(8,128)(2,1)S(1)}, bf16[256,512]{1,0:T(8,128)(2,1)S(1)}, bf16[768,512]{1,0:T(8,128...) custom-call(bf16[512,256]{1,0:T(8,128)(2,1)S(1)} %get-tuple-element.39.queries, ...), custom_call_target="tpu_custom_call" | custom-call | flops 2000000000 | bytes 4194304 | tf_op jit(solution)/shard_map/pallas_call | solution.py:28
  35.0 2.7 %collective-permute-start.7 = (bf16[512,256]{1,0:T(8,128)(2,1)S(1)}, bf16[512,256]{1,0:T(8,128)(2,1)S(1)}, u32[]{:S(2)}, u32[]{:S(2)}) collective-permute-start(bf16[512,256]{1,0:T(8,128)(2,1)S(1)} %get-tuple-element.58), channel_id=1, source_target_pairs={{0,3},{1,0},{2,1},{3,2},{4,7},{5,4},{6,5},{7,6},{8,11},{9,8},{10,9... | collective-permute-start | bytes 786440 | tf_op jit(solution)/shard_map/ppermute | solution.py:440
  37.8 3.8 %collective-permute-start.8 = (bf16[256,512]{1,0:T(8,128)(2,1)S(1)}, bf16[256,512]{1,0:T(8,128)(2,1)S(1)}, u32[]{:S(2)}, u32[]{:S(2)}) collective-permute-start(bf16[256,512]{1,0:T(8,128)(2,1)S(1)} %get-tuple-element.62), channel_id=1, source_target_pairs={{0,4},{4,8},{8,12},{12,16},{16,20},{20,24},{24,28},{28,32},{32,36}... | collective-permute-start | bytes 786440 | tf_op jit(solution)/shard_map/ppermute | solution.py:441
  41.5 0.0 collective-permute-start.9
  41.5 3.1 %shard_map.99 = (bf16[512,256]{1,0:T(8,128)(2,1)}, bf16[512,512]{1,0:T(8,128)(2,1)S(1)}) custom-call(bf16[512,256]{1,0:T(8,128)(2,1)S(1)} %get-tuple-element.39.queries, bf16[512,512]{1,0:T(8,128)(2,1)S(1)} %get-tuple-element.42.mine, bf16[768,512]{1,0:T(8,128)(2,1)S(1)} %get-tuple-element.59.edge, f32[2,512]{1,0:T(2,128)S(1)} %get-tuple-element.46.lse, ...), custom_call_target="tpu_custom_call" | custom-call | flops 3000000000 | bytes 6291456 | tf_op jit(solution)/shard_map/pallas_call | solution.py:28
  44.7 0.2 collective-permute-done.8.from_prev
  44.9 5.8 %collective-permute-done.9.from_next = bf16[256,512]{1,0:T(8,128)(2,1)S(1)} collective-permute-done((bf16[256,512]{1,0:T(8,128)(2,1)S(1)}, bf16[256,512]{1,0:T(8,128)(2,1)S(1)}, u32[]{:S(2)}, u32[]{:S(2)}) %collective-permute-start.9) | collective-permute-done | bytes 262176 | tf_op jit(solution)/shard_map/ppermute | solution.py:442
  50.7 1.6 %shard_map.101 = (bf16[512,256]{1,0:T(8,128)(2,1)}, bf16[512,256]{1,0:T(8,128)(2,1)}, bf16[512,256]{1,0:T(8,128)(2,1)}, f32[16,256]{1,0:T(8,128)}) custom-call(f32[512,256]{1,0:T(8,128)S(1)} %get-tuple-element.57.near_out, bf16[512,256]{1,0:T(8,128)(2,1)S(1)} %collective-permute-done.7.last_behind, bf16[512,512]{1,0:T(8,128)(2,1)S(1)} %get-tuple-element.61.own, ...), custom_call_target="tpu_custom_call" | custom-call | bytes 4194304 | tf_op jit(solution)/shard_map/pallas_call | solution.py:28
  (12 shorter events, 0.0 us)
Async XLA Ops:
  0.6 12.7 %copy-start = (bf16[1024,256]{1,0:T(8,128)(2,1)S(1)}, bf16[1024,256]{1,0:T(8,128)(2,1)}, u32[]{:S(2)}) copy-start(bf16[1024,256]{1,0:T(8,128)(2,1)} %weight.1) | copy-start | bytes 1572868
  0.6 10.0 %collective-permute-start.2 = (bf16[512,256]{1,0:T(8,128)(2,1)}, bf16[512,256]{1,0:T(8,128)(2,1)S(1)}, u32[]{:S(2)}, u32[]{:S(2)}) collective-permute-start(bf16[512,256]{1,0:T(8,128)(2,1)} %mine.1), channel_id=1, source_target_pairs={{0,3},{1,0},{2,1},{3,2},{4,7},{5,4},{6,5},{7,6},{8,11},{9,8},{10,9... | collective-permute-start | bytes 786440 | tf_op jit(solution)/shard_map/ppermute | solution.py:394
  3.2 0.9 %copy-start.3 = (bf16[512,256]{1,0:T(8,128)(2,1)S(1)}, bf16[512,256]{1,0:T(8,128)(2,1)}, u32[]{:S(2)}) copy-start(bf16[512,256]{1,0:T(8,128)(2,1)} %keys.1) | copy-start | bytes 786436
  4.1 0.9 %copy-start.4 = (bf16[512,256]{1,0:T(8,128)(2,1)S(1)}, bf16[512,256]{1,0:T(8,128)(2,1)}, u32[]{:S(2)}) copy-start(bf16[512,256]{1,0:T(8,128)(2,1)} %values.1) | copy-start | bytes 786436
  5.5 10.1 %collective-permute-start.1 = (bf16[256,512]{1,0:T(8,128)(2,1)S(1)}, bf16[256,512]{1,0:T(8,128)(2,1)S(1)}, u32[]{:S(2)}, u32[]{:S(2)}) collective-permute-start(bf16[256,512]{1,0:T(8,128)(2,1)S(1)} %get-tuple-element.40), channel_id=1, source_target_pairs={{4,0},{8,4},{12,8},{16,12},{20,16},{24,20},{28,24},{32,28},{36,32}... | collective-permute-start | bytes 786440 | tf_op jit(solution)/shard_map/ppermute | solution.py:402
  6.5 9.1 %collective-permute-start = (bf16[256,512]{1,0:T(8,128)(2,1)S(1)}, bf16[256,512]{1,0:T(8,128)(2,1)S(1)}, u32[]{:S(2)}, u32[]{:S(2)}) collective-permute-start(bf16[256,512]{1,0:T(8,128)(2,1)S(1)} %get-tuple-element.38._), channel_id=1, source_target_pairs={{0,4},{4,8},{8,12},{12,16},{16,20},{20,24},{24,28},{28,32},{32,36}... | collective-permute-start | bytes 786440 | tf_op jit(solution)/shard_map/ppermute | solution.py:401
  10.6 6.7 %collective-permute-start.4 = (bf16[512,256]{1,0:T(8,128)(2,1)}, bf16[512,256]{1,0:T(8,128)(2,1)S(1)}, u32[]{:S(2)}, u32[]{:S(2)}) collective-permute-start(bf16[512,256]{1,0:T(8,128)(2,1)} %mine.1), channel_id=1, source_target_pairs={{3,0},{0,1},{1,2},{2,3},{7,4},{4,5},{5,6},{6,7},{11,8},{8,9},{9,10... | collective-permute-start | bytes 786440 | tf_op jit(solution)/shard_map/ppermute | solution.py:395
  10.7 8.4 %collective-permute-start.3 = (bf16[512,256]{1,0:T(8,128)(2,1)S(1)}, bf16[512,256]{1,0:T(8,128)(2,1)S(1)}, u32[]{:S(2)}, u32[]{:S(2)}) collective-permute-start(bf16[512,256]{1,0:T(8,128)(2,1)S(1)} %collective-permute-done.2.behind_cot), channel_id=1, source_target_pairs={{0,3},{1,0},{2,1},{3,2},{4,7},{5,4},{6,5},{7,6},{8,11},{9,8},{10,9... | collective-permute-start | bytes 786440 | tf_op jit(solution)/shard_map/ppermute | solution.py:410
  13.3 1.0 %copy-start.1 = (bf16[512,256]{1,0:T(8,128)(2,1)S(1)}, bf16[512,256]{1,0:T(8,128)(2,1)}, u32[]{:S(2)}) copy-start(bf16[512,256]{1,0:T(8,128)(2,1)} %queries.1) | copy-start | bytes 786436
  15.7 1.7 %copy-start.2 = (bf16[512,256]{1,0:T(8,128)(2,1)S(1)}, bf16[512,256]{1,0:T(8,128)(2,1)}, u32[]{:S(2)}) copy-start(bf16[512,256]{1,0:T(8,128)(2,1)} %mine.1) | copy-start | bytes 786436
  19.6 4.3 %collective-permute-start.10 = (bf16[32,16,256]{2,1,0:T(8,128)(2,1)S(1)}, bf16[32,16,256]{2,1,0:T(8,128)(2,1)S(1)}, u32[]{:S(2)}, u32[]{:S(2)}) collective-permute-start(bf16[32,16,256]{2,1,0:T(8,128)(2,1)S(1)} %get-tuple-element.65), channel_id=1, source_target_pairs={{0,4},{4,0},{8,12},{12,8},{16,20},{20,16},{24,28},{28,24},{32,36},... | collective-permute-start | bytes 786440 | tf_op jit(solution)/shard_map/ppermute | solution.py:428
  20.4 12.4 %collective-permute-start.5 = (bf16[512,256]{1,0:T(8,128)(2,1)S(1)}, bf16[512,256]{1,0:T(8,128)(2,1)S(1)}, u32[]{:S(2)}, u32[]{:S(2)}) collective-permute-start(bf16[512,256]{1,0:T(8,128)(2,1)S(1)} %get-tuple-element.54), channel_id=1, source_target_pairs={{0,3},{1,0},{2,1},{3,2},{4,7},{5,4},{6,5},{7,6},{8,11},{9,8},{10,9... | collective-permute-start | bytes 786440 | tf_op jit(solution)/shard_map/ppermute | solution.py:417
  23.9 9.0 %collective-permute-start.6 = (bf16[512,256]{1,0:T(8,128)(2,1)S(1)}, bf16[512,256]{1,0:T(8,128)(2,1)S(1)}, u32[]{:S(2)}, u32[]{:S(2)}) collective-permute-start(bf16[512,256]{1,0:T(8,128)(2,1)S(1)} %get-tuple-element.56), channel_id=1, source_target_pairs={{3,0},{0,1},{1,2},{2,3},{7,4},{4,5},{5,6},{6,7},{11,8},{8,9},{9,10... | collective-permute-start | bytes 786440 | tf_op jit(solution)/shard_map/ppermute | solution.py:418
  24.6 26.0 %all-to-all-start = ((bf16[32,16,256]{2,1,0:T(8,128)(2,1)}), bf16[32,16,256]{2,1,0:T(8,128)(2,1)S(1)}, u32[]{:S(2)}, u32[]{:S(2)}) async-start(bf16[32,16,256]{2,1,0:T(8,128)(2,1)} %shard_map.100), calls=%async_computation | async-start | bytes 524288 | tf_op jit(solution)/shard_map/all_to_all | solution.py:432
  35.0 9.6 %collective-permute-start.7 = (bf16[512,256]{1,0:T(8,128)(2,1)S(1)}, bf16[512,256]{1,0:T(8,128)(2,1)S(1)}, u32[]{:S(2)}, u32[]{:S(2)}) collective-permute-start(bf16[512,256]{1,0:T(8,128)(2,1)S(1)} %get-tuple-element.58), channel_id=1, source_target_pairs={{0,3},{1,0},{2,1},{3,2},{4,7},{5,4},{6,5},{7,6},{8,11},{9,8},{10,9... | collective-permute-start | bytes 786440 | tf_op jit(solution)/shard_map/ppermute | solution.py:440
  37.8 7.1 %collective-permute-start.8 = (bf16[256,512]{1,0:T(8,128)(2,1)S(1)}, bf16[256,512]{1,0:T(8,128)(2,1)S(1)}, u32[]{:S(2)}, u32[]{:S(2)}) collective-permute-start(bf16[256,512]{1,0:T(8,128)(2,1)S(1)} %get-tuple-element.62), channel_id=1, source_target_pairs={{0,4},{4,8},{8,12},{12,16},{16,20},{20,24},{24,28},{28,32},{32,36}... | collective-permute-start | bytes 786440 | tf_op jit(solution)/shard_map/ppermute | solution.py:441
  41.5 9.1 %collective-permute-start.9 = (bf16[256,512]{1,0:T(8,128)(2,1)S(1)}, bf16[256,512]{1,0:T(8,128)(2,1)S(1)}, u32[]{:S(2)}, u32[]{:S(2)}) collective-permute-start(bf16[256,512]{1,0:T(8,128)(2,1)S(1)} %get-tuple-element.63), channel_id=1, source_target_pairs={{4,0},{8,4},{12,8},{16,12},{20,16},{24,20},{28,24},{32,28},{36,32}... | collective-permute-start | bytes 786440 | tf_op jit(solution)/shard_map/ppermute | solution.py:442

commit v6 on v2

--- a/solution.py
+++ b/solution.py
@@ -220,11 +220,11 @@
     return mm(cot[...], weight[pl.ds(pl.multiple_of(owner * width, width), width), :], NN)
 
 
-def near_products(mine, below, above, attention, weight, keep, send, part):
+def near_products(mine, first_cot, second_cot, attention, weight, keep, send, part):
     heads = lax.axis_size("head")
     part[...] = (product_of(0, mine, attention, weight, keep, send)
-                 + product_of(heads - 1, below, attention, weight, keep, send)
-                 + product_of(1, above, attention, weight, keep, send))
+                 + product_of(1, first_cot, attention, weight, keep, send)
+                 + product_of(heads - 1, second_cot, attention, weight, keep, send))
 
 
 def far_products(opposite, attention, weight, near_keep, near_send, part, keep, send, grad_attention, deltas):
@@ -391,8 +391,8 @@
     back = [(target, source) for source, target in onward]
     dma = pltpu.SemaphoreType.DMA
 
-    below = lax.ppermute(grad_out, "head", up)
-    above = lax.ppermute(grad_out, "head", down)
+    first_cot = lax.ppermute(grad_out, "head", down)
+    second_cot = lax.ppermute(grad_out, "head", up)
 
     mine, to_next, to_prev = run(
         prepare, (keys, values),
@@ -407,7 +407,7 @@
         forward_own, (queries, mine, to_next),
         [((2, rows), f32), ((2, rows), f32), ((2 * HEAD_DIM, rows), f32)],
         [pltpu.VMEM((256, 2 * width), bf16)], flops=10 ** 9, moved=2 << 20, far_args=(2,))
-    opposite = lax.ppermute(below, "head", up)
+    opposite = lax.ppermute(first_cot, "head", down)
 
     attention, lse, own_out, first_up, second_up, first_down = run(
         forward, (queries, before, after, out_weight, tops, totals, sums),
@@ -420,7 +420,7 @@
     chunk = features // shards
     shapes = [((shards // 2, chunk, width), f32), ((shards // 2, chunk, width), bf16)]
     keep, send, part = run(
-        near_products, (grad_out, below, above, attention, out_weight), shapes + [((rows, width), f32)],
+        near_products, (grad_out, first_cot, second_cot, attention, out_weight), shapes + [((rows, width), f32)],
         flops=4 * 10 ** 8, moved=1 << 20)
     keep, send, grad_attention, deltas = run(
         far_products, (opposite, attention, out_weight, keep, send, part),

time: 50.4 us -> 50.4 us (level)
  starting transfers between devices: 26.3 us -> 23.2 us
  waiting for transfers between devices: 7.88 us -> 10.5 us
    ppermute x1, starting transfers between devices: 2.63 us -> 0.01 us  [local(): from_below = lax.ppermute(first_up, 'head', up)]
    ppermute x3, waiting for transfers between devices: 1.87 us -> 4.49 us  [the longest x1 4.48 us: local(): opposite = lax.ppermute(first_cot, 'head', down)]
    ppermute x1, starting transfers between devices: 0.01 us -> 1.48 us  [local(): from_above = lax.ppermute(first_down, 'head', down)]
    ppermute x1, starting transfers between devices: 2.75 us -> 1.28 us  [local(): last_below = lax.ppermute(send_up, 'head', up)]
where the time goes in v6:
time: 50.4 us; the launch traced here: 49.7 us
  starting transfers between devices  23.2 us (46%)
  Pallas kernels  12.2 us (24%)
  waiting for transfers between devices  10.5 us (21%)
  local copies, waits for them, and re-layouts  2.85 us (6%)
  between operations  0.95 us (2%)
    pallas_call x10, Pallas kernels, run(): pl.pallas_call(body, in_specs=[FAR if number in far_args else VMEM for nu...  12.2 us
    all_to_all x1, starting transfers between devices, local(): spread = lax.all_to_all(pairs, 'seq', 0, 0, axis_index_groups=groups)  8.19 us
    ppermute x1, waiting for transfers between devices, local(): grad_after = lax.ppermute(to_prev, 'seq', back)  5.8 us
    ppermute x1, waiting for transfers between devices, local(): opposite = lax.ppermute(first_cot, 'head', down)  4.48 us
    ppermute x1, starting transfers between devices, local(): before = lax.ppermute(to_next, 'seq', onward)  4.11 us
    ppermute x1, starting transfers between devices, local(): grad_before = lax.ppermute(to_next, 'seq', onward)  3.58 us
    unnamed x10, local copies, waits for them, and re-layouts  2.85 us
    ppermute x1, starting transfers between devices, local(): second_cot = lax.ppermute(grad_out, 'head', up)  2.13 us
  transfers between devices with their start and end apart: 12, of which 3 were waited for; matrix products, arithmetic and copies ran while one was open for 0% of the time, Pallas kernels for 20%

profile of v6, /device:TPU:127, one launch (start us, length us, event | category | flops | bytes accessed | tf_op | source)
XLA Modules:
  0.0 49.7 jit_solution(2762787198900348840)
XLA Ops:
  0.6 0.6 %collective-permute-start.2 = (bf16[512,256]{1,0:T(8,128)(2,1)}, bf16[512,256]{1,0:T(8,128)(2,1)S(1)}, u32[]{:S(2)}, u32[]{:S(2)}) collective-permute-start(bf16[512,256]{1,0:T(8,128)(2,1)} %mine.1), channel_id=1, source_target_pairs={{1,0},{2,1},{3,2},{0,3},{5,4},{6,5},{7,6},{4,7},{9,8},{10,9},{11,1... | collective-permute-start | bytes 786440 | tf_op jit(solution)/shard_map/ppermute | solution.py:394
  1.3 0.9 %copy-done.3 = bf16[512,256]{1,0:T(8,128)(2,1)S(1)} copy-done((bf16[512,256]{1,0:T(8,128)(2,1)S(1)}, bf16[512,256]{1,0:T(8,128)(2,1)}, u32[]{:S(2)}) %copy-start.3) | copy-done | bytes 262168
  2.2 0.9 %copy-done.4 = bf16[512,256]{1,0:T(8,128)(2,1)S(1)} copy-done((bf16[512,256]{1,0:T(8,128)(2,1)S(1)}, bf16[512,256]{1,0:T(8,128)(2,1)}, u32[]{:S(2)}) %copy-start.4) | copy-done | bytes 262168
  3.2 0.4 shard_map.92
  3.6 1.0 %collective-permute-start.1 = (bf16[256,512]{1,0:T(8,128)(2,1)S(1)}, bf16[256,512]{1,0:T(8,128)(2,1)S(1)}, u32[]{:S(2)}, u32[]{:S(2)}) collective-permute-start(bf16[256,512]{1,0:T(8,128)(2,1)S(1)} %get-tuple-element.40), channel_id=1, source_target_pairs={{4,0},{8,4},{12,8},{16,12},{20,16},{24,20},{28,24},{32,28},{36,32}... | collective-permute-start | bytes 786440 | tf_op jit(solution)/shard_map/ppermute | solution.py:402
  4.6 4.1 %collective-permute-start = (bf16[256,512]{1,0:T(8,128)(2,1)S(1)}, bf16[256,512]{1,0:T(8,128)(2,1)S(1)}, u32[]{:S(2)}, u32[]{:S(2)}) collective-permute-start(bf16[256,512]{1,0:T(8,128)(2,1)S(1)} %get-tuple-element.38._), channel_id=1, source_target_pairs={{0,4},{4,8},{8,12},{12,16},{16,20},{20,24},{24,28},{28,32},{32,36}... | collective-permute-start | bytes 786440 | tf_op jit(solution)/shard_map/ppermute | solution.py:401
  8.7 2.1 %collective-permute-start.4 = (bf16[512,256]{1,0:T(8,128)(2,1)}, bf16[512,256]{1,0:T(8,128)(2,1)S(1)}, u32[]{:S(2)}, u32[]{:S(2)}) collective-permute-start(bf16[512,256]{1,0:T(8,128)(2,1)} %mine.1), channel_id=1, source_target_pairs={{0,1},{1,2},{2,3},{3,0},{4,5},{5,6},{6,7},{7,4},{8,9},{9,10},{10,1... | collective-permute-start | bytes 786440 | tf_op jit(solution)/shard_map/ppermute | solution.py:395
  10.8 0.0 collective-permute-done.2.first_cot
  10.8 0.0 collective-permute-start.3
  10.9 0.0 copy-start.1
  10.9 0.9 %copy-done.1 = bf16[512,256]{1,0:T(8,128)(2,1)S(1)} copy-done((bf16[512,256]{1,0:T(8,128)(2,1)S(1)}, bf16[512,256]{1,0:T(8,128)(2,1)}, u32[]{:S(2)}) %copy-start.1) | copy-done | bytes 262168
  11.8 0.1 shard_map.93
  11.9 1.3 %shard_map.94 = (f32[2,512]{1,0:T(2,128)S(1)}, f32[2,512]{1,0:T(2,128)S(1)}, f32[256,512]{1,0:T(8,128)S(1)}) custom-call(bf16[512,256]{1,0:T(8,128)(2,1)S(1)} %get-tuple-element.39.queries, bf16[512,512]{1,0:T(8,128)(2,1)S(1)} %get-tuple-element.42.mine, bf16[256,512]{1,0:T(8,128)(2,1)S(1)} %get-tuple-element.38._), custom_call_target="tpu_custom_call" | custom-call | flops 1000000000 | bytes 2097152 | tf_op jit(solution)/shard_map/pallas_call | solution.py:28
  13.2 0.0 collective-permute-done.1.after
  13.2 0.0 collective-permute-done.before
  13.2 0.0 copy-start.2
  13.2 1.7 %shard_map.95 = (bf16[512,256]{1,0:T(8,128)(2,1)S(1)}, f32[2,512]{1,0:T(2,128)S(1)}, bf16[512,256]{1,0:T(8,128)(2,1)S(1)}, bf16[512,256]{1,0:T(8,128)(2,1)S(1)},...) custom-call(bf16[512,256]{1,0:T(8,128)(2,1)S(1)} %get-tuple-element.39.queries, ...), custom_call_target="tpu_custom_call" | custom-call | flops 1000000000 | bytes 3145728 | tf_op jit(solution)/shard_map/pallas_call | solution.py:28
  14.9 0.6 %shard_map.96 = (f32[32,16,256]{2,1,0:T(8,128)S(1)}, bf16[32,16,256]{2,1,0:T(8,128)(2,1)S(1)}, f32[512,256]{1,0:T(8,128)S(1)}) custom-call(bf16[512,256]{1,0:T(8,128)(2,1)S(1)} %copy-done.2, bf16[512,256]{1,0:T(8,128)(2,1)S(1)} %collective-permute-done.2.first_cot, bf16[512,256]{1,0:T(8,128)(2,1)S(1)} %collective-permute-done.4.second_cot, ...), custom_call_target="tpu_custom_call" | custom-call | flops 400000000 | bytes 1048576 | tf_op jit(solution)/shard_map/pallas_call | solution.py:28
  15.5 4.5 %collective-permute-done.3.opposite = bf16[512,256]{1,0:T(8,128)(2,1)S(1)} collective-permute-done((bf16[512,256]{1,0:T(8,128)(2,1)S(1)}, bf16[512,256]{1,0:T(8,128)(2,1)S(1)}, u32[]{:S(2)}, u32[]{:S(2)}) %collective-permute-start.3) | collective-permute-done | bytes 262176 | tf_op jit(solution)/shard_map/ppermute | solution.py:410
  20.0 0.6 %shard_map.97 = (f32[32,16,256]{2,1,0:T(8,128)S(1)}, bf16[32,16,256]{2,1,0:T(8,128)(2,1)S(1)}, bf16[512,256]{1,0:T(8,128)(2,1)S(1)}, f32[2,512]{1,0:T(2,128)S(1)}) custom-call(bf16[512,256]{1,0:T(8,128)(2,1)S(1)} %collective-permute-done.3.opposite, bf16[512,256]{1,0:T(8,128)(2,1)S(1)} %get-tuple-element.47.attention, ...), custom_call_target="tpu_custom_call" | custom-call | tf_op jit(solution)/shard_map/pallas_call | solution.py:28
  20.6 0.8 %collective-permute-start.10 = (bf16[32,16,256]{2,1,0:T(8,128)(2,1)S(1)}, bf16[32,16,256]{2,1,0:T(8,128)(2,1)S(1)}, u32[]{:S(2)}, u32[]{:S(2)}) collective-permute-start(bf16[32,16,256]{2,1,0:T(8,128)(2,1)S(1)} %get-tuple-element.65), channel_id=1, source_target_pairs={{0,4},{4,0},{8,12},{12,8},{16,20},{20,16},{24,28},{28,24},{32,36},... | collective-permute-start | bytes 786440 | tf_op jit(solution)/shard_map/ppermute | solution.py:428
  21.4 1.5 %collective-permute-start.6 = (bf16[512,256]{1,0:T(8,128)(2,1)S(1)}, bf16[512,256]{1,0:T(8,128)(2,1)S(1)}, u32[]{:S(2)}, u32[]{:S(2)}) collective-permute-start(bf16[512,256]{1,0:T(8,128)(2,1)S(1)} %get-tuple-element.56), channel_id=1, source_target_pairs={{1,0},{2,1},{3,2},{0,3},{5,4},{6,5},{7,6},{4,7},{9,8},{10,9},{11,1... | collective-permute-start | bytes 786440 | tf_op jit(solution)/shard_map/ppermute | solution.py:418
  22.9 0.0 collective-permute-done.10.sibling
  22.9 0.7 %shard_map.100 = bf16[32,16,256]{2,1,0:T(8,128)(2,1)} custom-call(f32[32,16,256]{2,1,0:T(8,128)S(1)} %get-tuple-element.64.keep, bf16[32,16,256]{2,1,0:T(8,128)(2,1)S(1)} %collective-permute-done.10.sibling), custom_call_target="tpu_custom_call" | custom-call | tf_op jit(solution)/shard_map/pallas_call | solution.py:28
  23.6 8.2 %all-to-all-start = ((bf16[32,16,256]{2,1,0:T(8,128)(2,1)}), bf16[32,16,256]{2,1,0:T(8,128)(2,1)S(1)}, u32[]{:S(2)}, u32[]{:S(2)}) async-start(bf16[32,16,256]{2,1,0:T(8,128)(2,1)} %shard_map.100), calls=%async_computation | async-start | bytes 524288 | tf_op jit(solution)/shard_map/all_to_all | solution.py:432
  31.8 2.2 %shard_map.98 = (bf16[4,512,256]{2,1,0:T(8,128)(2,1)S(1)}, bf16[256,512]{1,0:T(8,128)(2,1)S(1)}, bf16[256,512]{1,0:T(8,128)(2,1)S(1)}, bf16[768,512]{1,0:T(8,128...) custom-call(bf16[512,256]{1,0:T(8,128)(2,1)S(1)} %get-tuple-element.39.queries, ...), custom_call_target="tpu_custom_call" | custom-call | flops 2000000000 | bytes 4194304 | tf_op jit(solution)/shard_map/pallas_call | solution.py:28
  34.0 1.3 %collective-permute-start.7 = (bf16[512,256]{1,0:T(8,128)(2,1)S(1)}, bf16[512,256]{1,0:T(8,128)(2,1)S(1)}, u32[]{:S(2)}, u32[]{:S(2)}) collective-permute-start(bf16[512,256]{1,0:T(8,128)(2,1)S(1)} %get-tuple-element.58), channel_id=1, source_target_pairs={{0,1},{1,2},{2,3},{3,0},{4,5},{5,6},{6,7},{7,4},{8,9},{9,10},{10,1... | collective-permute-start | bytes 786440 | tf_op jit(solution)/shard_map/ppermute | solution.py:440
  35.3 3.6 %collective-permute-start.8 = (bf16[256,512]{1,0:T(8,128)(2,1)S(1)}, bf16[256,512]{1,0:T(8,128)(2,1)S(1)}, u32[]{:S(2)}, u32[]{:S(2)}) collective-permute-start(bf16[256,512]{1,0:T(8,128)(2,1)S(1)} %get-tuple-element.62), channel_id=1, source_target_pairs={{0,4},{4,8},{8,12},{12,16},{16,20},{20,24},{24,28},{28,32},{32,36}... | collective-permute-start | bytes 786440 | tf_op jit(solution)/shard_map/ppermute | solution.py:441
  38.9 3.1 %shard_map.99 = (bf16[512,256]{1,0:T(8,128)(2,1)}, bf16[512,512]{1,0:T(8,128)(2,1)S(1)}) custom-call(bf16[512,256]{1,0:T(8,128)(2,1)S(1)} %get-tuple-element.39.queries, bf16[512,512]{1,0:T(8,128)(2,1)S(1)} %get-tuple-element.42.mine, bf16[768,512]{1,0:T(8,128)(2,1)S(1)} %get-tuple-element.59.edge, f32[2,512]{1,0:T(2,128)S(1)} %get-tuple-element.46.lse, ...), custom_call_target="tpu_custom_call" | custom-call | flops 3000000000 | bytes 6291456 | tf_op jit(solution)/shard_map/pallas_call | solution.py:28
  42.0 0.2 collective-permute-done.8.from_prev
  42.2 5.8 %collective-permute-done.9.from_next = bf16[256,512]{1,0:T(8,128)(2,1)S(1)} collective-permute-done((bf16[256,512]{1,0:T(8,128)(2,1)S(1)}, bf16[256,512]{1,0:T(8,128)(2,1)S(1)}, u32[]{:S(2)}, u32[]{:S(2)}) %collective-permute-start.9) | collective-permute-done | bytes 262176 | tf_op jit(solution)/shard_map/ppermute | solution.py:442
  48.0 1.6 %shard_map.101 = (bf16[512,256]{1,0:T(8,128)(2,1)}, bf16[512,256]{1,0:T(8,128)(2,1)}, bf16[512,256]{1,0:T(8,128)(2,1)}, f32[16,256]{1,0:T(8,128)}) custom-call(f32[512,256]{1,0:T(8,128)S(1)} %get-tuple-element.57.near_out, bf16[512,256]{1,0:T(8,128)(2,1)S(1)} %collective-permute-done.7.last_below, bf16[512,512]{1,0:T(8,128)(2,1)S(1)} %get-tuple-element.61.own, ...), custom_call_target="tpu_custom_call" | custom-call | bytes 4194304 | tf_op jit(solution)/shard_map/pallas_call | solution.py:28
  (12 shorter events, 0.0 us)
Async XLA Ops:
  0.6 10.2 %copy-start = (bf16[1024,256]{1,0:T(8,128)(2,1)S(1)}, bf16[1024,256]{1,0:T(8,128)(2,1)}, u32[]{:S(2)}) copy-start(bf16[1024,256]{1,0:T(8,128)(2,1)} %weight.1) | copy-start | bytes 1572868
  0.6 10.2 %collective-permute-start.2 = (bf16[512,256]{1,0:T(8,128)(2,1)}, bf16[512,256]{1,0:T(8,128)(2,1)S(1)}, u32[]{:S(2)}, u32[]{:S(2)}) collective-permute-start(bf16[512,256]{1,0:T(8,128)(2,1)} %mine.1), channel_id=1, source_target_pairs={{1,0},{2,1},{3,2},{0,3},{5,4},{6,5},{7,6},{4,7},{9,8},{10,9},{11,1... | collective-permute-start | bytes 786440 | tf_op jit(solution)/shard_map/ppermute | solution.py:394
  1.3 0.9 %copy-start.3 = (bf16[512,256]{1,0:T(8,128)(2,1)S(1)}, bf16[512,256]{1,0:T(8,128)(2,1)}, u32[]{:S(2)}) copy-start(bf16[512,256]{1,0:T(8,128)(2,1)} %keys.1) | copy-start | bytes 786436
  2.2 0.9 %copy-start.4 = (bf16[512,256]{1,0:T(8,128)(2,1)S(1)}, bf16[512,256]{1,0:T(8,128)(2,1)}, u32[]{:S(2)}) copy-start(bf16[512,256]{1,0:T(8,128)(2,1)} %values.1) | copy-start | bytes 786436
  3.6 9.6 %collective-permute-start.1 = (bf16[256,512]{1,0:T(8,128)(2,1)S(1)}, bf16[256,512]{1,0:T(8,128)(2,1)S(1)}, u32[]{:S(2)}, u32[]{:S(2)}) collective-permute-start(bf16[256,512]{1,0:T(8,128)(2,1)S(1)} %get-tuple-element.40), channel_id=1, source_target_pairs={{4,0},{8,4},{12,8},{16,12},{20,16},{24,20},{28,24},{32,28},{36,32}... | collective-permute-start | bytes 786440 | tf_op jit(solution)/shard_map/ppermute | solution.py:402
  4.6 8.6 %collective-permute-start = (bf16[256,512]{1,0:T(8,128)(2,1)S(1)}, bf16[256,512]{1,0:T(8,128)(2,1)S(1)}, u32[]{:S(2)}, u32[]{:S(2)}) collective-permute-start(bf16[256,512]{1,0:T(8,128)(2,1)S(1)} %get-tuple-element.38._), channel_id=1, source_target_pairs={{0,4},{4,8},{8,12},{12,16},{16,20},{20,24},{24,28},{28,32},{32,36}... | collective-permute-start | bytes 786440 | tf_op jit(solution)/shard_map/ppermute | solution.py:401
  8.7 6.1 %collective-permute-start.4 = (bf16[512,256]{1,0:T(8,128)(2,1)}, bf16[512,256]{1,0:T(8,128)(2,1)S(1)}, u32[]{:S(2)}, u32[]{:S(2)}) collective-permute-start(bf16[512,256]{1,0:T(8,128)(2,1)} %mine.1), channel_id=1, source_target_pairs={{0,1},{1,2},{2,3},{3,0},{4,5},{5,6},{6,7},{7,4},{8,9},{9,10},{10,1... | collective-permute-start | bytes 786440 | tf_op jit(solution)/shard_map/ppermute | solution.py:395
  10.8 9.1 %collective-permute-start.3 = (bf16[512,256]{1,0:T(8,128)(2,1)S(1)}, bf16[512,256]{1,0:T(8,128)(2,1)S(1)}, u32[]{:S(2)}, u32[]{:S(2)}) collective-permute-start(bf16[512,256]{1,0:T(8,128)(2,1)S(1)} %collective-permute-done.2.first_cot), channel_id=1, source_target_pairs={{1,0},{2,1},{3,2},{0,3},{5,4},{6,5},{7,6},{4,7},{9,8},{10,9},{11,1... | collective-permute-start | bytes 786440 | tf_op jit(solution)/shard_map/ppermute | solution.py:410
  10.9 1.0 %copy-start.1 = (bf16[512,256]{1,0:T(8,128)(2,1)S(1)}, bf16[512,256]{1,0:T(8,128)(2,1)}, u32[]{:S(2)}) copy-start(bf16[512,256]{1,0:T(8,128)(2,1)} %queries.1) | copy-start | bytes 786436
  13.2 1.7 %copy-start.2 = (bf16[512,256]{1,0:T(8,128)(2,1)S(1)}, bf16[512,256]{1,0:T(8,128)(2,1)}, u32[]{:S(2)}) copy-start(bf16[512,256]{1,0:T(8,128)(2,1)} %mine.1) | copy-start | bytes 786436
  20.6 2.3 %collective-permute-start.10 = (bf16[32,16,256]{2,1,0:T(8,128)(2,1)S(1)}, bf16[32,16,256]{2,1,0:T(8,128)(2,1)S(1)}, u32[]{:S(2)}, u32[]{:S(2)}) collective-permute-start(bf16[32,16,256]{2,1,0:T(8,128)(2,1)S(1)} %get-tuple-element.65), channel_id=1, source_target_pairs={{0,4},{4,0},{8,12},{12,8},{16,20},{20,16},{24,28},{28,24},{32,36},... | collective-permute-start | bytes 786440 | tf_op jit(solution)/shard_map/ppermute | solution.py:428
  21.4 10.4 %collective-permute-start.5 = (bf16[512,256]{1,0:T(8,128)(2,1)S(1)}, bf16[512,256]{1,0:T(8,128)(2,1)S(1)}, u32[]{:S(2)}, u32[]{:S(2)}) collective-permute-start(bf16[512,256]{1,0:T(8,128)(2,1)S(1)} %get-tuple-element.54), channel_id=1, source_target_pairs={{0,1},{1,2},{2,3},{3,0},{4,5},{5,6},{6,7},{7,4},{8,9},{9,10},{10,1... | collective-permute-start | bytes 786440 | tf_op jit(solution)/shard_map/ppermute | solution.py:417
  21.4 10.4 %collective-permute-start.6 = (bf16[512,256]{1,0:T(8,128)(2,1)S(1)}, bf16[512,256]{1,0:T(8,128)(2,1)S(1)}, u32[]{:S(2)}, u32[]{:S(2)}) collective-permute-start(bf16[512,256]{1,0:T(8,128)(2,1)S(1)} %get-tuple-element.56), channel_id=1, source_target_pairs={{1,0},{2,1},{3,2},{0,3},{5,4},{6,5},{7,6},{4,7},{9,8},{10,9},{11,1... | collective-permute-start | bytes 786440 | tf_op jit(solution)/shard_map/ppermute | solution.py:418
  23.6 24.4 %all-to-all-start = ((bf16[32,16,256]{2,1,0:T(8,128)(2,1)}), bf16[32,16,256]{2,1,0:T(8,128)(2,1)S(1)}, u32[]{:S(2)}, u32[]{:S(2)}) async-start(bf16[32,16,256]{2,1,0:T(8,128)(2,1)} %shard_map.100), calls=%async_computation | async-start | bytes 524288 | tf_op jit(solution)/shard_map/all_to_all | solution.py:432
  34.0 8.0 %collective-permute-start.7 = (bf16[512,256]{1,0:T(8,128)(2,1)S(1)}, bf16[512,256]{1,0:T(8,128)(2,1)S(1)}, u32[]{:S(2)}, u32[]{:S(2)}) collective-permute-start(bf16[512,256]{1,0:T(8,128)(2,1)S(1)} %get-tuple-element.58), channel_id=1, source_target_pairs={{0,1},{1,2},{2,3},{3,0},{4,5},{5,6},{6,7},{7,4},{8,9},{9,10},{10,1... | collective-permute-start | bytes 786440 | tf_op jit(solution)/shard_map/ppermute | solution.py:440
  35.3 6.9 %collective-permute-start.8 = (bf16[256,512]{1,0:T(8,128)(2,1)S(1)}, bf16[256,512]{1,0:T(8,128)(2,1)S(1)}, u32[]{:S(2)}, u32[]{:S(2)}) collective-permute-start(bf16[256,512]{1,0:T(8,128)(2,1)S(1)} %get-tuple-element.62), channel_id=1, source_target_pairs={{0,4},{4,8},{8,12},{12,16},{16,20},{20,24},{24,28},{28,32},{32,36}... | collective-permute-start | bytes 786440 | tf_op jit(solution)/shard_map/ppermute | solution.py:441
  38.9 9.1 %collective-permute-start.9 = (bf16[256,512]{1,0:T(8,128)(2,1)S(1)}, bf16[256,512]{1,0:T(8,128)(2,1)S(1)}, u32[]{:S(2)}, u32[]{:S(2)}) collective-permute-start(bf16[256,512]{1,0:T(8,128)(2,1)S(1)} %get-tuple-element.63), channel_id=1, source_target_pairs={{4,0},{8,4},{12,8},{16,12},{20,16},{24,20},{28,24},{32,28},{36,32}... | collective-permute-start | bytes 786440 | tf_op jit(solution)/shard_map/ppermute | solution.py:442

commit v7 on v6

--- a/solution.py
+++ b/solution.py
@@ -175,7 +175,7 @@
 
 
 def forward(queries, before, after, weight, tops, totals, sums,
-            attention, lse, own, first_up, second_up, first_down, edge):
+            attention, residue, lse, own, first_up, second_up, first_down, edge):
     widen(before, after, edge)
     width = queries.shape[1]
     for head in range(2):
@@ -192,7 +192,9 @@
             total = total + scale * totals[head:head + 1, span]
             lse[head:head + 1, span] = top + jnp.log2(total)
             result = ((summed + scale * sums[head * 128:head * 128 + 128, span]) / total).T
-            attention[span, cols] = result.astype(jnp.bfloat16)
+            rounded = result.astype(jnp.bfloat16)
+            attention[span, cols] = rounded
+            residue[span, cols] = (result - rounded.astype(jnp.float32)).astype(jnp.bfloat16)
     heads = lax.axis_size("head")
     here = lax.axis_index("head")
 
@@ -227,18 +229,20 @@
                  + product_of(heads - 1, second_cot, attention, weight, keep, send))
 
 
-def far_products(opposite, attention, weight, near_keep, near_send, part, keep, send, grad_attention, deltas):
+def far_products(opposite, attention, residue, weight, near_keep, near_send, part, keep, send, grad_attention, deltas):
     keep[...] = near_keep[...]
     send[...] = near_send[...]
     rounded = (part[...] + product_of(2, opposite, attention, weight, keep, send)).astype(jnp.bfloat16)
     grad_attention[...] = rounded
-    terms = rounded.astype(jnp.float32) * attention[...].astype(jnp.float32)
-    high = terms.astype(jnp.bfloat16)
-    low = (terms - high.astype(jnp.float32)).astype(jnp.bfloat16)
+    terms = rounded.astype(jnp.float32) * (attention[...].astype(jnp.float32) + residue[...].astype(jnp.float32))
     ones = jnp.ones((16, HEAD_DIM), jnp.bfloat16)
+    sums = [jnp.zeros((16, terms.shape[0]), jnp.float32)] * 2
+    for _ in range(3):
+        part_of = terms.astype(jnp.bfloat16)
+        terms = terms - part_of.astype(jnp.float32)
+        sums = [sums[head] + mm(ones, part_of[:, head * HEAD_DIM:head * HEAD_DIM + HEAD_DIM], NT) for head in range(2)]
     for head in range(2):
-        cols = slice(head * HEAD_DIM, head * HEAD_DIM + HEAD_DIM)
-        deltas[head:head + 1] = (mm(ones, high[:, cols], NT) + mm(ones, low[:, cols], NT))[0:1]
+        deltas[head:head + 1] = sums[head][0:1]
 
 
 def pair_sum(keep, sibling, pairs, pairs_here, sems):
@@ -409,9 +413,9 @@
         [pltpu.VMEM((256, 2 * width), bf16)], flops=10 ** 9, moved=2 << 20, far_args=(2,))
     opposite = lax.ppermute(first_cot, "head", down)
 
-    attention, lse, own_out, first_up, second_up, first_down = run(
+    attention, residue, lse, own_out, first_up, second_up, first_down = run(
         forward, (queries, before, after, out_weight, tops, totals, sums),
-        [((rows, width), bf16), ((2, rows), f32), ((rows, width), bf16), ((rows, width), bf16),
+        [((rows, width), bf16), ((rows, width), bf16), ((2, rows), f32), ((rows, width), bf16), ((rows, width), bf16),
          ((rows, width), bf16), ((rows, width), bf16)],
         [pltpu.VMEM((768, 2 * width), bf16)], flops=10 ** 9, moved=3 << 20)
     from_below = lax.ppermute(first_up, "head", up)
@@ -423,7 +427,7 @@
         near_products, (grad_out, first_cot, second_cot, attention, out_weight), shapes + [((rows, width), f32)],
         flops=4 * 10 ** 8, moved=1 << 20)
     keep, send, grad_attention, deltas = run(
-        far_products, (opposite, attention, out_weight, keep, send, part),
+        far_products, (opposite, attention, residue, out_weight, keep, send, part),
         shapes + [((rows, width), bf16), ((2, rows), f32)])
     half_sum = lax.ppermute(send, "seq", swap)
     pairs, = run(pair_sum, (keep, half_sum), [((shards // 2, chunk, width), bf16)],

time: 50.4 us -> 50.5 us (level)
  no operation moved by 1% of the time
where the time goes in v7:
time: 50.5 us; the launch traced here: 49.8 us
  starting transfers between devices  23.3 us (46%)
  Pallas kernels  12.3 us (24%)
  waiting for transfers between devices  10.5 us (21%)
  local copies, waits for them, and re-layouts  2.85 us (6%)
  between operations  0.95 us (2%)
    pallas_call x10, Pallas kernels, run(): pl.pallas_call(body, in_specs=[FAR if number in far_args else VMEM for nu...  12.3 us
    all_to_all x1, starting transfers between devices, local(): spread = lax.all_to_all(pairs, 'seq', 0, 0, axis_index_groups=groups)  8.19 us
    ppermute x1, waiting for transfers between devices, local(): grad_after = lax.ppermute(to_prev, 'seq', back)  5.8 us
    ppermute x1, waiting for transfers between devices, local(): opposite = lax.ppermute(first_cot, 'head', down)  4.44 us
    ppermute x1, starting transfers between devices, local(): before = lax.ppermute(to_next, 'seq', onward)  4.11 us
    ppermute x1, starting transfers between devices, local(): grad_before = lax.ppermute(to_next, 'seq', onward)  3.58 us
    unnamed x10, local copies, waits for them, and re-layouts  2.85 us
    ppermute x1, starting transfers between devices, local(): second_cot = lax.ppermute(grad_out, 'head', up)  2.13 us
  transfers between devices with their start and end apart: 12, of which 3 were waited for; matrix products, arithmetic and copies ran while one was open for 0% of the time, Pallas kernels for 20%

profile of v7, /device:TPU:127, one launch (start us, length us, event | category | flops | bytes accessed | tf_op | source)
XLA Modules:
  0.0 49.8 jit_solution(16066342825339241024)
XLA Ops:
  0.6 0.6 %collective-permute-start.2 = (bf16[512,256]{1,0:T(8,128)(2,1)}, bf16[512,256]{1,0:T(8,128)(2,1)S(1)}, u32[]{:S(2)}, u32[]{:S(2)}) collective-permute-start(bf16[512,256]{1,0:T(8,128)(2,1)} %mine.1), channel_id=1, source_target_pairs={{1,0},{2,1},{3,2},{0,3},{5,4},{6,5},{7,6},{4,7},{9,8},{10,9},{11,1... | collective-permute-start | bytes 786440 | tf_op jit(solution)/shard_map/ppermute | solution.py:398
  1.3 0.9 %copy-done.3 = bf16[512,256]{1,0:T(8,128)(2,1)S(1)} copy-done((bf16[512,256]{1,0:T(8,128)(2,1)S(1)}, bf16[512,256]{1,0:T(8,128)(2,1)}, u32[]{:S(2)}) %copy-start.3) | copy-done | bytes 262168
  2.2 0.9 %copy-done.4 = bf16[512,256]{1,0:T(8,128)(2,1)S(1)} copy-done((bf16[512,256]{1,0:T(8,128)(2,1)S(1)}, bf16[512,256]{1,0:T(8,128)(2,1)}, u32[]{:S(2)}) %copy-start.4) | copy-done | bytes 262168
  3.2 0.4 shard_map.92
  3.6 1.0 %collective-permute-start.1 = (bf16[256,512]{1,0:T(8,128)(2,1)S(1)}, bf16[256,512]{1,0:T(8,128)(2,1)S(1)}, u32[]{:S(2)}, u32[]{:S(2)}) collective-permute-start(bf16[256,512]{1,0:T(8,128)(2,1)S(1)} %get-tuple-element.41), channel_id=1, source_target_pairs={{4,0},{8,4},{12,8},{16,12},{20,16},{24,20},{28,24},{32,28},{36,32}... | collective-permute-start | bytes 786440 | tf_op jit(solution)/shard_map/ppermute | solution.py:406
  4.6 4.1 %collective-permute-start = (bf16[256,512]{1,0:T(8,128)(2,1)S(1)}, bf16[256,512]{1,0:T(8,128)(2,1)S(1)}, u32[]{:S(2)}, u32[]{:S(2)}) collective-permute-start(bf16[256,512]{1,0:T(8,128)(2,1)S(1)} %get-tuple-element.39._), channel_id=1, source_target_pairs={{0,4},{4,8},{8,12},{12,16},{16,20},{20,24},{24,28},{28,32},{32,36}... | collective-permute-start | bytes 786440 | tf_op jit(solution)/shard_map/ppermute | solution.py:405
  8.7 2.1 %collective-permute-start.4 = (bf16[512,256]{1,0:T(8,128)(2,1)}, bf16[512,256]{1,0:T(8,128)(2,1)S(1)}, u32[]{:S(2)}, u32[]{:S(2)}) collective-permute-start(bf16[512,256]{1,0:T(8,128)(2,1)} %mine.1), channel_id=1, source_target_pairs={{0,1},{1,2},{2,3},{3,0},{4,5},{5,6},{6,7},{7,4},{8,9},{9,10},{10,1... | collective-permute-start | bytes 786440 | tf_op jit(solution)/shard_map/ppermute | solution.py:399
  10.8 0.0 collective-permute-done.2.first_cot
  10.8 0.0 collective-permute-start.3
  10.9 0.0 copy-start.1
  10.9 0.9 %copy-done.1 = bf16[512,256]{1,0:T(8,128)(2,1)S(1)} copy-done((bf16[512,256]{1,0:T(8,128)(2,1)S(1)}, bf16[512,256]{1,0:T(8,128)(2,1)}, u32[]{:S(2)}) %copy-start.1) | copy-done | bytes 262168
  11.8 0.1 shard_map.93
  11.9 1.3 %shard_map.94 = (f32[2,512]{1,0:T(2,128)S(1)}, f32[2,512]{1,0:T(2,128)S(1)}, f32[256,512]{1,0:T(8,128)S(1)}) custom-call(bf16[512,256]{1,0:T(8,128)(2,1)S(1)} %get-tuple-element.40.queries, bf16[512,512]{1,0:T(8,128)(2,1)S(1)} %get-tuple-element.43.mine, bf16[256,512]{1,0:T(8,128)(2,1)S(1)} %get-tuple-element.39._), custom_call_target="tpu_custom_call" | custom-call | flops 1000000000 | bytes 2097152 | tf_op jit(solution)/shard_map/pallas_call | solution.py:28
  13.2 0.0 collective-permute-done.1.after
  13.2 0.0 collective-permute-done.before
  13.2 0.0 copy-start.2
  13.2 1.7 %shard_map.95 = (bf16[512,256]{1,0:T(8,128)(2,1)S(1)}, bf16[512,256]{1,0:T(8,128)(2,1)S(1)}, f32[2,512]{1,0:T(2,128)S(1)}, bf16[512,256]{1,0:T(8,128)(2,1)S(1)},...) custom-call(bf16[512,256]{1,0:T(8,128)(2,1)S(1)} %get-tuple-element.40.queries, ...), custom_call_target="tpu_custom_call" | custom-call | flops 1000000000 | bytes 3145728 | tf_op jit(solution)/shard_map/pallas_call | solution.py:28
  14.9 0.0 collective-permute-done.4.second_cot
  14.9 0.6 %shard_map.96 = (f32[32,16,256]{2,1,0:T(8,128)S(1)}, bf16[32,16,256]{2,1,0:T(8,128)(2,1)S(1)}, f32[512,256]{1,0:T(8,128)S(1)}) custom-call(bf16[512,256]{1,0:T(8,128)(2,1)S(1)} %copy-done.2, bf16[512,256]{1,0:T(8,128)(2,1)S(1)} %collective-permute-done.2.first_cot, bf16[512,256]{1,0:T(8,128)(2,1)S(1)} %collective-permute-done.4.second_cot, ...), custom_call_target="tpu_custom_call" | custom-call | flops 400000000 | bytes 1048576 | tf_op jit(solution)/shard_map/pallas_call | solution.py:28
  15.6 4.4 %collective-permute-done.3.opposite = bf16[512,256]{1,0:T(8,128)(2,1)S(1)} collective-permute-done((bf16[512,256]{1,0:T(8,128)(2,1)S(1)}, bf16[512,256]{1,0:T(8,128)(2,1)S(1)}, u32[]{:S(2)}, u32[]{:S(2)}) %collective-permute-start.3) | collective-permute-done | bytes 262176 | tf_op jit(solution)/shard_map/ppermute | solution.py:414
  20.0 0.6 %shard_map.97 = (f32[32,16,256]{2,1,0:T(8,128)S(1)}, bf16[32,16,256]{2,1,0:T(8,128)(2,1)S(1)}, bf16[512,256]{1,0:T(8,128)(2,1)S(1)}, f32[2,512]{1,0:T(2,128)S(1)}) custom-call(bf16[512,256]{1,0:T(8,128)(2,1)S(1)} %collective-permute-done.3.opposite, bf16[512,256]{1,0:T(8,128)(2,1)S(1)} %get-tuple-element.48.attention, ...), custom_call_target="tpu_custom_call" | custom-call | tf_op jit(solution)/shard_map/pallas_call | solution.py:28
  20.6 0.9 %collective-permute-start.10 = (bf16[32,16,256]{2,1,0:T(8,128)(2,1)S(1)}, bf16[32,16,256]{2,1,0:T(8,128)(2,1)S(1)}, u32[]{:S(2)}, u32[]{:S(2)}) collective-permute-start(bf16[32,16,256]{2,1,0:T(8,128)(2,1)S(1)} %get-tuple-element.67), channel_id=1, source_target_pairs={{0,4},{4,0},{8,12},{12,8},{16,20},{20,16},{24,28},{28,24},{32,36},... | collective-permute-start | bytes 786440 | tf_op jit(solution)/shard_map/ppermute | solution.py:432
  21.5 1.5 %collective-permute-start.6 = (bf16[512,256]{1,0:T(8,128)(2,1)S(1)}, bf16[512,256]{1,0:T(8,128)(2,1)S(1)}, u32[]{:S(2)}, u32[]{:S(2)}) collective-permute-start(bf16[512,256]{1,0:T(8,128)(2,1)S(1)} %get-tuple-element.58), channel_id=1, source_target_pairs={{1,0},{2,1},{3,2},{0,3},{5,4},{6,5},{7,6},{4,7},{9,8},{10,9},{11,1... | collective-permute-start | bytes 786440 | tf_op jit(solution)/shard_map/ppermute | solution.py:422
  23.0 0.7 %shard_map.100 = bf16[32,16,256]{2,1,0:T(8,128)(2,1)} custom-call(f32[32,16,256]{2,1,0:T(8,128)S(1)} %get-tuple-element.66.keep, bf16[32,16,256]{2,1,0:T(8,128)(2,1)S(1)} %collective-permute-done.10.sibling), custom_call_target="tpu_custom_call" | custom-call | tf_op jit(solution)/shard_map/pallas_call | solution.py:28
  23.7 8.2 %all-to-all-start = ((bf16[32,16,256]{2,1,0:T(8,128)(2,1)}), bf16[32,16,256]{2,1,0:T(8,128)(2,1)S(1)}, u32[]{:S(2)}, u32[]{:S(2)}) async-start(bf16[32,16,256]{2,1,0:T(8,128)(2,1)} %shard_map.100), calls=%async_computation | async-start | bytes 524288 | tf_op jit(solution)/shard_map/all_to_all | solution.py:436
  31.9 2.2 %shard_map.98 = (bf16[4,512,256]{2,1,0:T(8,128)(2,1)S(1)}, bf16[256,512]{1,0:T(8,128)(2,1)S(1)}, bf16[256,512]{1,0:T(8,128)(2,1)S(1)}, bf16[768,512]{1,0:T(8,128...) custom-call(bf16[512,256]{1,0:T(8,128)(2,1)S(1)} %get-tuple-element.40.queries, ...), custom_call_target="tpu_custom_call" | custom-call | flops 2000000000 | bytes 4194304 | tf_op jit(solution)/shard_map/pallas_call | solution.py:28
  34.1 1.3 %collective-permute-start.7 = (bf16[512,256]{1,0:T(8,128)(2,1)S(1)}, bf16[512,256]{1,0:T(8,128)(2,1)S(1)}, u32[]{:S(2)}, u32[]{:S(2)}) collective-permute-start(bf16[512,256]{1,0:T(8,128)(2,1)S(1)} %get-tuple-element.60), channel_id=1, source_target_pairs={{0,1},{1,2},{2,3},{3,0},{4,5},{5,6},{6,7},{7,4},{8,9},{9,10},{10,1... | collective-permute-start | bytes 786440 | tf_op jit(solution)/shard_map/ppermute | solution.py:444
  35.4 3.6 %collective-permute-start.8 = (bf16[256,512]{1,0:T(8,128)(2,1)S(1)}, bf16[256,512]{1,0:T(8,128)(2,1)S(1)}, u32[]{:S(2)}, u32[]{:S(2)}) collective-permute-start(bf16[256,512]{1,0:T(8,128)(2,1)S(1)} %get-tuple-element.64), channel_id=1, source_target_pairs={{0,4},{4,8},{8,12},{12,16},{16,20},{20,24},{24,28},{28,32},{32,36}... | collective-permute-start | bytes 786440 | tf_op jit(solution)/shard_map/ppermute | solution.py:445
  39.0 3.1 %shard_map.99 = (bf16[512,256]{1,0:T(8,128)(2,1)}, bf16[512,512]{1,0:T(8,128)(2,1)S(1)}) custom-call(bf16[512,256]{1,0:T(8,128)(2,1)S(1)} %get-tuple-element.40.queries, bf16[512,512]{1,0:T(8,128)(2,1)S(1)} %get-tuple-element.43.mine, bf16[768,512]{1,0:T(8,128)(2,1)S(1)} %get-tuple-element.61.edge, f32[2,512]{1,0:T(2,128)S(1)} %get-tuple-element.47.lse, ...), custom_call_target="tpu_custom_call" | custom-call | flops 3000000000 | bytes 6291456 | tf_op jit(solution)/shard_map/pallas_call | solution.py:28
  42.1 0.2 collective-permute-done.8.from_prev
  42.3 5.8 %collective-permute-done.9.from_next = bf16[256,512]{1,0:T(8,128)(2,1)S(1)} collective-permute-done((bf16[256,512]{1,0:T(8,128)(2,1)S(1)}, bf16[256,512]{1,0:T(8,128)(2,1)S(1)}, u32[]{:S(2)}, u32[]{:S(2)}) %collective-permute-start.9) | collective-permute-done | bytes 262176 | tf_op jit(solution)/shard_map/ppermute | solution.py:446
  48.1 1.6 %shard_map.101 = (bf16[512,256]{1,0:T(8,128)(2,1)}, bf16[512,256]{1,0:T(8,128)(2,1)}, bf16[512,256]{1,0:T(8,128)(2,1)}, f32[16,256]{1,0:T(8,128)}) custom-call(f32[512,256]{1,0:T(8,128)S(1)} %get-tuple-element.59.near_out, bf16[512,256]{1,0:T(8,128)(2,1)S(1)} %collective-permute-done.7.last_below, bf16[512,512]{1,0:T(8,128)(2,1)S(1)} %get-tuple-element.63.own, ...), custom_call_target="tpu_custom_call" | custom-call | bytes 4194304 | tf_op jit(solution)/shard_map/pallas_call | solution.py:28
  (12 shorter events, 0.0 us)
Async XLA Ops:
  0.6 10.2 %copy-start = (bf16[1024,256]{1,0:T(8,128)(2,1)S(1)}, bf16[1024,256]{1,0:T(8,128)(2,1)}, u32[]{:S(2)}) copy-start(bf16[1024,256]{1,0:T(8,128)(2,1)} %weight.1) | copy-start | bytes 1572868
  0.6 10.2 %collective-permute-start.2 = (bf16[512,256]{1,0:T(8,128)(2,1)}, bf16[512,256]{1,0:T(8,128)(2,1)S(1)}, u32[]{:S(2)}, u32[]{:S(2)}) collective-permute-start(bf16[512,256]{1,0:T(8,128)(2,1)} %mine.1), channel_id=1, source_target_pairs={{1,0},{2,1},{3,2},{0,3},{5,4},{6,5},{7,6},{4,7},{9,8},{10,9},{11,1... | collective-permute-start | bytes 786440 | tf_op jit(solution)/shard_map/ppermute | solution.py:398
  1.3 0.9 %copy-start.3 = (bf16[512,256]{1,0:T(8,128)(2,1)S(1)}, bf16[512,256]{1,0:T(8,128)(2,1)}, u32[]{:S(2)}) copy-start(bf16[512,256]{1,0:T(8,128)(2,1)} %keys.1) | copy-start | bytes 786436
  2.2 0.9 %copy-start.4 = (bf16[512,256]{1,0:T(8,128)(2,1)S(1)}, bf16[512,256]{1,0:T(8,128)(2,1)}, u32[]{:S(2)}) copy-start(bf16[512,256]{1,0:T(8,128)(2,1)} %values.1) | copy-start | bytes 786436
  3.6 9.6 %collective-permute-start.1 = (bf16[256,512]{1,0:T(8,128)(2,1)S(1)}, bf16[256,512]{1,0:T(8,128)(2,1)S(1)}, u32[]{:S(2)}, u32[]{:S(2)}) collective-permute-start(bf16[256,512]{1,0:T(8,128)(2,1)S(1)} %get-tuple-element.41), channel_id=1, source_target_pairs={{4,0},{8,4},{12,8},{16,12},{20,16},{24,20},{28,24},{32,28},{36,32}... | collective-permute-start | bytes 786440 | tf_op jit(solution)/shard_map/ppermute | solution.py:406
  4.6 8.6 %collective-permute-start = (bf16[256,512]{1,0:T(8,128)(2,1)S(1)}, bf16[256,512]{1,0:T(8,128)(2,1)S(1)}, u32[]{:S(2)}, u32[]{:S(2)}) collective-permute-start(bf16[256,512]{1,0:T(8,128)(2,1)S(1)} %get-tuple-element.39._), channel_id=1, source_target_pairs={{0,4},{4,8},{8,12},{12,16},{16,20},{20,24},{24,28},{28,32},{32,36}... | collective-permute-start | bytes 786440 | tf_op jit(solution)/shard_map/ppermute | solution.py:405
  8.7 6.2 %collective-permute-start.4 = (bf16[512,256]{1,0:T(8,128)(2,1)}, bf16[512,256]{1,0:T(8,128)(2,1)S(1)}, u32[]{:S(2)}, u32[]{:S(2)}) collective-permute-start(bf16[512,256]{1,0:T(8,128)(2,1)} %mine.1), channel_id=1, source_target_pairs={{0,1},{1,2},{2,3},{3,0},{4,5},{5,6},{6,7},{7,4},{8,9},{9,10},{10,1... | collective-permute-start | bytes 786440 | tf_op jit(solution)/shard_map/ppermute | solution.py:399
  10.8 9.1 %collective-permute-start.3 = (bf16[512,256]{1,0:T(8,128)(2,1)S(1)}, bf16[512,256]{1,0:T(8,128)(2,1)S(1)}, u32[]{:S(2)}, u32[]{:S(2)}) collective-permute-start(bf16[512,256]{1,0:T(8,128)(2,1)S(1)} %collective-permute-done.2.first_cot), channel_id=1, source_target_pairs={{1,0},{2,1},{3,2},{0,3},{5,4},{6,5},{7,6},{4,7},{9,8},{10,9},{11,1... | collective-permute-start | bytes 786440 | tf_op jit(solution)/shard_map/ppermute | solution.py:414
  10.9 1.0 %copy-start.1 = (bf16[512,256]{1,0:T(8,128)(2,1)S(1)}, bf16[512,256]{1,0:T(8,128)(2,1)}, u32[]{:S(2)}) copy-start(bf16[512,256]{1,0:T(8,128)(2,1)} %queries.1) | copy-start | bytes 786436
  13.2 1.7 %copy-start.2 = (bf16[512,256]{1,0:T(8,128)(2,1)S(1)}, bf16[512,256]{1,0:T(8,128)(2,1)}, u32[]{:S(2)}) copy-start(bf16[512,256]{1,0:T(8,128)(2,1)} %mine.1) | copy-start | bytes 786436
  20.6 2.3 %collective-permute-start.10 = (bf16[32,16,256]{2,1,0:T(8,128)(2,1)S(1)}, bf16[32,16,256]{2,1,0:T(8,128)(2,1)S(1)}, u32[]{:S(2)}, u32[]{:S(2)}) collective-permute-start(bf16[32,16,256]{2,1,0:T(8,128)(2,1)S(1)} %get-tuple-element.67), channel_id=1, source_target_pairs={{0,4},{4,0},{8,12},{12,8},{16,20},{20,16},{24,28},{28,24},{32,36},... | collective-permute-start | bytes 786440 | tf_op jit(solution)/shard_map/ppermute | solution.py:432
  21.5 10.4 %collective-permute-start.5 = (bf16[512,256]{1,0:T(8,128)(2,1)S(1)}, bf16[512,256]{1,0:T(8,128)(2,1)S(1)}, u32[]{:S(2)}, u32[]{:S(2)}) collective-permute-start(bf16[512,256]{1,0:T(8,128)(2,1)S(1)} %get-tuple-element.56), channel_id=1, source_target_pairs={{0,1},{1,2},{2,3},{3,0},{4,5},{5,6},{6,7},{7,4},{8,9},{9,10},{10,1... | collective-permute-start | bytes 786440 | tf_op jit(solution)/shard_map/ppermute | solution.py:421
  21.5 10.4 %collective-permute-start.6 = (bf16[512,256]{1,0:T(8,128)(2,1)S(1)}, bf16[512,256]{1,0:T(8,128)(2,1)S(1)}, u32[]{:S(2)}, u32[]{:S(2)}) collective-permute-start(bf16[512,256]{1,0:T(8,128)(2,1)S(1)} %get-tuple-element.58), channel_id=1, source_target_pairs={{1,0},{2,1},{3,2},{0,3},{5,4},{6,5},{7,6},{4,7},{9,8},{10,9},{11,1... | collective-permute-start | bytes 786440 | tf_op jit(solution)/shard_map/ppermute | solution.py:422
  23.7 24.4 %all-to-all-start = ((bf16[32,16,256]{2,1,0:T(8,128)(2,1)}), bf16[32,16,256]{2,1,0:T(8,128)(2,1)S(1)}, u32[]{:S(2)}, u32[]{:S(2)}) async-start(bf16[32,16,256]{2,1,0:T(8,128)(2,1)} %shard_map.100), calls=%async_computation | async-start | bytes 524288 | tf_op jit(solution)/shard_map/all_to_all | solution.py:436
  34.1 8.0 %collective-permute-start.7 = (bf16[512,256]{1,0:T(8,128)(2,1)S(1)}, bf16[512,256]{1,0:T(8,128)(2,1)S(1)}, u32[]{:S(2)}, u32[]{:S(2)}) collective-permute-start(bf16[512,256]{1,0:T(8,128)(2,1)S(1)} %get-tuple-element.60), channel_id=1, source_target_pairs={{0,1},{1,2},{2,3},{3,0},{4,5},{5,6},{6,7},{7,4},{8,9},{9,10},{10,1... | collective-permute-start | bytes 786440 | tf_op jit(solution)/shard_map/ppermute | solution.py:444
  35.4 6.9 %collective-permute-start.8 = (bf16[256,512]{1,0:T(8,128)(2,1)S(1)}, bf16[256,512]{1,0:T(8,128)(2,1)S(1)}, u32[]{:S(2)}, u32[]{:S(2)}) collective-permute-start(bf16[256,512]{1,0:T(8,128)(2,1)S(1)} %get-tuple-element.64), channel_id=1, source_target_pairs={{0,4},{4,8},{8,12},{12,16},{16,20},{20,24},{24,28},{28,32},{32,36}... | collective-permute-start | bytes 786440 | tf_op jit(solution)/shard_map/ppermute | solution.py:445
  39.0 9.1 %collective-permute-start.9 = (bf16[256,512]{1,0:T(8,128)(2,1)S(1)}, bf16[256,512]{1,0:T(8,128)(2,1)S(1)}, u32[]{:S(2)}, u32[]{:S(2)}) collective-permute-start(bf16[256,512]{1,0:T(8,128)(2,1)S(1)} %get-tuple-element.65), channel_id=1, source_target_pairs={{4,0},{8,4},{12,8},{16,12},{20,16},{24,20},{28,24},{32,28},{36,32}... | collective-permute-start | bytes 786440 | tf_op jit(solution)/shard_map/ppermute | solution.py:446

commit v8 on v7

--- a/solution.py
+++ b/solution.py
@@ -265,10 +265,9 @@
     return pairs
 
 
-def backward(queries, before, after, lse, grad_attention, deltas, second_up, from_below, own, from_above,
-             dscores, to_next, to_prev, edge, send_up, near, total):
+def backward(queries, before, after, lse, grad_attention, deltas, second_up, from_below,
+             dscores, to_next, to_prev, edge, send_up, total):
     send_up[...] = (second_up[...].astype(jnp.float32) + from_below[...].astype(jnp.float32)).astype(jnp.bfloat16)
-    near[...] = own[...].astype(jnp.float32) + from_above[...].astype(jnp.float32)
     widen(before, after, edge)
     width = queries.shape[1]
     for half in range(2):
@@ -301,9 +300,10 @@
     to_next[192:256] = (total[1472:1536] * 0.25).astype(jnp.bfloat16)
 
 
-def own_grads(queries, mine, edge, lse, grad_attention, deltas, dscores,
-              grad_queries, own, total, pooled, grad_q_here, sems):
+def own_grads(queries, mine, edge, lse, grad_attention, deltas, dscores, own_part, from_above,
+              grad_queries, own, near, total, pooled, grad_q_here, sems):
     pooled[...] = mm(pool_matrix(256, 2), mine[...], NN).astype(jnp.bfloat16)
+    near[...] = own_part[...].astype(jnp.float32) + from_above[...].astype(jnp.float32)
     stores = []
     width = queries.shape[1]
     for half in range(2):
@@ -435,18 +435,18 @@
     groups = [list(range(core, shards, 2)) for core in range(2)]
     spread = lax.all_to_all(pairs, "seq", 0, 0, axis_index_groups=groups)
 
-    dscores, to_next, to_prev, edge, send_up, near_out = run(
+    dscores, to_next, to_prev, edge, send_up = run(
         backward,
-        (queries, before, after, lse, grad_attention, deltas, second_up, from_below, own_out, from_above),
+        (queries, before, after, lse, grad_attention, deltas, second_up, from_below),
         [((4, 512, 256), bf16), ((256, 2 * width), bf16), ((256, 2 * width), bf16), ((768, 2 * width), bf16),
-         ((rows, width), bf16), ((rows, width), f32)],
+         ((rows, width), bf16)],
         [pltpu.VMEM((1536, 2 * width), f32)], flops=2 * 10 ** 9, moved=4 << 20)
     last_below = lax.ppermute(send_up, "head", up)
     grad_before = lax.ppermute(to_next, "seq", onward)
     grad_after = lax.ppermute(to_prev, "seq", back)
-    grad_queries, own_grad = run(
-        own_grads, (queries, mine, edge, lse, grad_attention, deltas, dscores),
-        [((rows, width), bf16), ((rows, 2 * width), bf16)],
+    grad_queries, own_grad, near_out = run(
+        own_grads, (queries, mine, edge, lse, grad_attention, deltas, dscores, own_out, from_above),
+        [((rows, width), bf16), ((rows, 2 * width), bf16), ((rows, width), f32)],
         [pltpu.VMEM((1536, 2 * width), f32), pltpu.VMEM((256, 2 * width), bf16), pltpu.VMEM((rows, width), bf16), dma((2,))],
         flops=3 * 10 ** 9, moved=6 << 20, far_outs=(0,))
 

time: 50.5 us -> 50.4 us (level)
  waiting for transfers between devices: 10.5 us -> 9.67 us
  local copies, waits for them, and re-layouts: 2.85 us -> 3.56 us
    unnamed x10 -> x14, local copies, waits for them, and re-layouts: 2.85 us -> 3.56 us
    ppermute x1, waiting for transfers between devices: 4.44 us -> 3.75 us  [local(): opposite = lax.ppermute(first_cot, 'head', down)]
where the time goes in v8:
time: 50.4 us; the launch traced here: 49.8 us
  starting transfers between devices  23.3 us (46%)
  Pallas kernels  12.3 us (24%)
  waiting for transfers between devices  9.67 us (19%)
  local copies, waits for them, and re-layouts  3.56 us (7%)
  between operations  0.95 us (2%)
    pallas_call x10, Pallas kernels, run(): pl.pallas_call(body, in_specs=[FAR if number in far_args else VMEM for nu...  12.3 us
    all_to_all x1, starting transfers between devices, local(): spread = lax.all_to_all(pairs, 'seq', 0, 0, axis_index_groups=groups)  8.19 us
    ppermute x1, waiting for transfers between devices, local(): grad_after = lax.ppermute(to_prev, 'seq', back)  5.8 us
    ppermute x1, starting transfers between devices, local(): before = lax.ppermute(to_next, 'seq', onward)  4.11 us
    ppermute x1, waiting for transfers between devices, local(): opposite = lax.ppermute(first_cot, 'head', down)  3.75 us
    ppermute x1, starting transfers between devices, local(): grad_before = lax.ppermute(to_next, 'seq', onward)  3.59 us
    unnamed x14, local copies, waits for them, and re-layouts  3.56 us
    ppermute x1, starting transfers between devices, local(): second_cot = lax.ppermute(grad_out, 'head', up)  2.13 us
  transfers between devices with their start and end apart: 12, of which 3 were waited for; matrix products, arithmetic and copies ran while one was open for 0% of the time, Pallas kernels for 20%

profile of v8, /device:TPU:127, one launch (start us, length us, event | category | flops | bytes accessed | tf_op | source)
XLA Modules:
  0.0 49.8 jit_solution(4030008489693992720)
XLA Ops:
  0.6 0.6 %collective-permute-start.2 = (bf16[512,256]{1,0:T(8,128)(2,1)}, bf16[512,256]{1,0:T(8,128)(2,1)S(1)}, u32[]{:S(2)}, u32[]{:S(2)}) collective-permute-start(bf16[512,256]{1,0:T(8,128)(2,1)} %mine.1), channel_id=1, source_target_pairs={{1,0},{2,1},{3,2},{0,3},{5,4},{6,5},{7,6},{4,7},{9,8},{10,9},{11,1... | collective-permute-start | bytes 786440 | tf_op jit(solution)/shard_map/ppermute | solution.py:398
  1.3 0.9 %copy-done.3 = bf16[512,256]{1,0:T(8,128)(2,1)S(1)} copy-done((bf16[512,256]{1,0:T(8,128)(2,1)S(1)}, bf16[512,256]{1,0:T(8,128)(2,1)}, u32[]{:S(2)}) %copy-start.3) | copy-done | bytes 262168
  2.2 0.9 %copy-done.4 = bf16[512,256]{1,0:T(8,128)(2,1)S(1)} copy-done((bf16[512,256]{1,0:T(8,128)(2,1)S(1)}, bf16[512,256]{1,0:T(8,128)(2,1)}, u32[]{:S(2)}) %copy-start.4) | copy-done | bytes 262168
  3.2 0.4 shard_map.92
  3.6 1.0 %collective-permute-start.1 = (bf16[256,512]{1,0:T(8,128)(2,1)S(1)}, bf16[256,512]{1,0:T(8,128)(2,1)S(1)}, u32[]{:S(2)}, u32[]{:S(2)}) collective-permute-start(bf16[256,512]{1,0:T(8,128)(2,1)S(1)} %get-tuple-element.42), channel_id=1, source_target_pairs={{4,0},{8,4},{12,8},{16,12},{20,16},{24,20},{28,24},{32,28},{36,32}... | collective-permute-start | bytes 786440 | tf_op jit(solution)/shard_map/ppermute | solution.py:406
  4.6 4.1 %collective-permute-start = (bf16[256,512]{1,0:T(8,128)(2,1)S(1)}, bf16[256,512]{1,0:T(8,128)(2,1)S(1)}, u32[]{:S(2)}, u32[]{:S(2)}) collective-permute-start(bf16[256,512]{1,0:T(8,128)(2,1)S(1)} %get-tuple-element.39._), channel_id=1, source_target_pairs={{0,4},{4,8},{8,12},{12,16},{16,20},{20,24},{24,28},{28,32},{32,36}... | collective-permute-start | bytes 786440 | tf_op jit(solution)/shard_map/ppermute | solution.py:405
  8.7 2.1 %collective-permute-start.4 = (bf16[512,256]{1,0:T(8,128)(2,1)}, bf16[512,256]{1,0:T(8,128)(2,1)S(1)}, u32[]{:S(2)}, u32[]{:S(2)}) collective-permute-start(bf16[512,256]{1,0:T(8,128)(2,1)} %mine.1), channel_id=1, source_target_pairs={{0,1},{1,2},{2,3},{3,0},{4,5},{5,6},{6,7},{7,4},{8,9},{9,10},{10,1... | collective-permute-start | bytes 786440 | tf_op jit(solution)/shard_map/ppermute | solution.py:399
  10.8 0.0 collective-permute-done.2.first_cot
  10.8 0.0 collective-permute-start.3
  10.9 0.0 copy-start.1
  10.9 0.9 %copy-done.1 = bf16[512,256]{1,0:T(8,128)(2,1)S(1)} copy-done((bf16[512,256]{1,0:T(8,128)(2,1)S(1)}, bf16[512,256]{1,0:T(8,128)(2,1)}, u32[]{:S(2)}) %copy-start.1) | copy-done | bytes 262168
  11.8 0.1 shard_map.93
  11.9 1.3 %shard_map.94 = (f32[2,512]{1,0:T(2,128)S(1)}, f32[2,512]{1,0:T(2,128)S(1)}, f32[256,512]{1,0:T(8,128)S(1)}) custom-call(bf16[512,256]{1,0:T(8,128)(2,1)S(1)} %get-tuple-element.40.queries, bf16[512,512]{1,0:T(8,128)(2,1)S(1)} %get-tuple-element.41.mine, bf16[256,512]{1,0:T(8,128)(2,1)S(1)} %get-tuple-element.39._), custom_call_target="tpu_custom_call" | custom-call | flops 1000000000 | bytes 2097152 | tf_op jit(solution)/shard_map/pallas_call | solution.py:28
  13.2 0.0 copy-start.2
  13.2 1.7 %shard_map.95 = (bf16[512,256]{1,0:T(8,128)(2,1)S(1)}, bf16[512,256]{1,0:T(8,128)(2,1)S(1)}, f32[2,512]{1,0:T(2,128)S(1)}, bf16[512,256]{1,0:T(8,128)(2,1)S(1)},...) custom-call(bf16[512,256]{1,0:T(8,128)(2,1)S(1)} %get-tuple-element.40.queries, ...), custom_call_target="tpu_custom_call" | custom-call | flops 1000000000 | bytes 3145728 | tf_op jit(solution)/shard_map/pallas_call | solution.py:28
  14.9 0.0 copy-start.5
  14.9 0.7 %copy-done.5 = bf16[512,256]{1,0:T(8,128)(2,1)} copy-done((bf16[512,256]{1,0:T(8,128)(2,1)}, bf16[512,256]{1,0:T(8,128)(2,1)S(1)}, u32[]{:S(2)}) %copy-start.5) | copy-done | bytes 262168
  15.6 0.6 %shard_map.96 = (f32[32,16,256]{2,1,0:T(8,128)S(1)}, bf16[32,16,256]{2,1,0:T(8,128)(2,1)S(1)}, f32[512,256]{1,0:T(8,128)S(1)}) custom-call(bf16[512,256]{1,0:T(8,128)(2,1)S(1)} %copy-done.2, bf16[512,256]{1,0:T(8,128)(2,1)S(1)} %collective-permute-done.2.first_cot, bf16[512,256]{1,0:T(8,128)(2,1)S(1)} %collective-permute-done.4.second_cot, ...), custom_call_target="tpu_custom_call" | custom-call | flops 400000000 | bytes 1048576 | tf_op jit(solution)/shard_map/pallas_call | solution.py:28
  16.2 3.8 %collective-permute-done.3.opposite = bf16[512,256]{1,0:T(8,128)(2,1)S(1)} collective-permute-done((bf16[512,256]{1,0:T(8,128)(2,1)S(1)}, bf16[512,256]{1,0:T(8,128)(2,1)S(1)}, u32[]{:S(2)}, u32[]{:S(2)}) %collective-permute-start.3) | collective-permute-done | bytes 262176 | tf_op jit(solution)/shard_map/ppermute | solution.py:414
  20.0 0.6 %shard_map.97 = (f32[32,16,256]{2,1,0:T(8,128)S(1)}, bf16[32,16,256]{2,1,0:T(8,128)(2,1)S(1)}, bf16[512,256]{1,0:T(8,128)(2,1)S(1)}, f32[2,512]{1,0:T(2,128)S(1)}) custom-call(bf16[512,256]{1,0:T(8,128)(2,1)S(1)} %collective-permute-done.3.opposite, bf16[512,256]{1,0:T(8,128)(2,1)S(1)} %get-tuple-element.48.attention, ...), custom_call_target="tpu_custom_call" | custom-call | tf_op jit(solution)/shard_map/pallas_call | solution.py:28
  20.6 0.9 %collective-permute-start.10 = (bf16[32,16,256]{2,1,0:T(8,128)(2,1)S(1)}, bf16[32,16,256]{2,1,0:T(8,128)(2,1)S(1)}, u32[]{:S(2)}, u32[]{:S(2)}) collective-permute-start(bf16[32,16,256]{2,1,0:T(8,128)(2,1)S(1)} %get-tuple-element.67), channel_id=1, source_target_pairs={{0,4},{4,0},{8,12},{12,8},{16,20},{20,16},{24,28},{28,24},{32,36},... | collective-permute-start | bytes 786440 | tf_op jit(solution)/shard_map/ppermute | solution.py:432
  21.5 1.5 %collective-permute-start.6 = (bf16[512,256]{1,0:T(8,128)(2,1)S(1)}, bf16[512,256]{1,0:T(8,128)(2,1)S(1)}, u32[]{:S(2)}, u32[]{:S(2)}) collective-permute-start(bf16[512,256]{1,0:T(8,128)(2,1)S(1)} %get-tuple-element.60), channel_id=1, source_target_pairs={{1,0},{2,1},{3,2},{0,3},{5,4},{6,5},{7,6},{4,7},{9,8},{10,9},{11,1... | collective-permute-start | bytes 786440 | tf_op jit(solution)/shard_map/ppermute | solution.py:422
  23.0 0.7 %shard_map.100 = bf16[32,16,256]{2,1,0:T(8,128)(2,1)} custom-call(f32[32,16,256]{2,1,0:T(8,128)S(1)} %get-tuple-element.66.keep, bf16[32,16,256]{2,1,0:T(8,128)(2,1)S(1)} %collective-permute-done.10.sibling), custom_call_target="tpu_custom_call" | custom-call | tf_op jit(solution)/shard_map/pallas_call | solution.py:28
  23.7 8.2 %all-to-all-start = ((bf16[32,16,256]{2,1,0:T(8,128)(2,1)}), bf16[32,16,256]{2,1,0:T(8,128)(2,1)S(1)}, u32[]{:S(2)}, u32[]{:S(2)}) async-start(bf16[32,16,256]{2,1,0:T(8,128)(2,1)} %shard_map.100), calls=%async_computation | async-start | bytes 524288 | tf_op jit(solution)/shard_map/all_to_all | solution.py:436
  31.9 0.0 copy-start.6
  31.9 2.1 %shard_map.98 = (bf16[4,512,256]{2,1,0:T(8,128)(2,1)S(1)}, bf16[256,512]{1,0:T(8,128)(2,1)S(1)}, bf16[256,512]{1,0:T(8,128)(2,1)S(1)}, bf16[768,512]{1,0:T(8,128)(2,1)S(1)}, bf16[512,256]{1,0:T(8,128)(2,1)S(1)}) custom-call(bf16[512,256]{1,0:T(8,128)(2,1)S(1)} %get-tuple-element.40.queries, bf16[256,512]{1,0:T(8,128)(2,1)S(1)} %collective-permute-done.before, ...), custom_call_target="tpu_custom_call" | custom-call | flops 2000000000 | bytes 4194304 | tf_op jit(solution)/shard_map/pallas_call | solution.py:28
  34.0 1.3 %collective-permute-start.7 = (bf16[512,256]{1,0:T(8,128)(2,1)S(1)}, bf16[512,256]{1,0:T(8,128)(2,1)S(1)}, u32[]{:S(2)}, u32[]{:S(2)}) collective-permute-start(bf16[512,256]{1,0:T(8,128)(2,1)S(1)} %get-tuple-element.62), channel_id=1, source_target_pairs={{0,1},{1,2},{2,3},{3,0},{4,5},{5,6},{6,7},{7,4},{8,9},{9,10},{10,1... | collective-permute-start | bytes 786440 | tf_op jit(solution)/shard_map/ppermute | solution.py:444
  35.3 3.6 %collective-permute-start.8 = (bf16[256,512]{1,0:T(8,128)(2,1)S(1)}, bf16[256,512]{1,0:T(8,128)(2,1)S(1)}, u32[]{:S(2)}, u32[]{:S(2)}) collective-permute-start(bf16[256,512]{1,0:T(8,128)(2,1)S(1)} %get-tuple-element.64), channel_id=1, source_target_pairs={{0,4},{4,8},{8,12},{12,16},{16,20},{20,24},{24,28},{28,32},{32,36}... | collective-permute-start | bytes 786440 | tf_op jit(solution)/shard_map/ppermute | solution.py:445
  38.9 3.2 %shard_map.99 = (bf16[512,256]{1,0:T(8,128)(2,1)}, bf16[512,512]{1,0:T(8,128)(2,1)S(1)}, f32[512,256]{1,0:T(8,128)S(1)}) custom-call(bf16[512,256]{1,0:T(8,128)(2,1)S(1)} %get-tuple-element.40.queries, bf16[512,512]{1,0:T(8,128)(2,1)S(1)} %get-tuple-element.41.mine, bf16[768,512]{1,0:T(8,128)(2,1)S(1)} %get-tuple-element.57.edge, ...), custom_call_target="tpu_custom_call" | custom-call | flops 3000000000 | bytes 6291456 | tf_op jit(solution)/shard_map/pallas_call | solution.py:28
  42.1 0.1 collective-permute-done.8.from_prev
  42.2 5.8 %collective-permute-done.9.from_next = bf16[256,512]{1,0:T(8,128)(2,1)S(1)} collective-permute-done((bf16[256,512]{1,0:T(8,128)(2,1)S(1)}, bf16[256,512]{1,0:T(8,128)(2,1)S(1)}, u32[]{:S(2)}, u32[]{:S(2)}) %collective-permute-start.9) | collective-permute-done | bytes 262176 | tf_op jit(solution)/shard_map/ppermute | solution.py:446
  48.0 1.6 %shard_map.101 = (bf16[512,256]{1,0:T(8,128)(2,1)}, bf16[512,256]{1,0:T(8,128)(2,1)}, bf16[512,256]{1,0:T(8,128)(2,1)}, f32[16,256]{1,0:T(8,128)}) custom-call(f32[512,256]{1,0:T(8,128)S(1)} %get-tuple-element.61.near_out, bf16[512,256]{1,0:T(8,128)(2,1)S(1)} %collective-permute-done.7.last_below, bf16[512,512]{1,0:T(8,128)(2,1)S(1)} %get-tuple-element.63.own, ...), custom_call_target="tpu_custom_call" | custom-call | bytes 4194304 | tf_op jit(solution)/shard_map/pallas_call | solution.py:28
  (16 shorter events, 0.0 us)
Async XLA Ops:
  0.6 10.2 %copy-start = (bf16[1024,256]{1,0:T(8,128)(2,1)S(1)}, bf16[1024,256]{1,0:T(8,128)(2,1)}, u32[]{:S(2)}) copy-start(bf16[1024,256]{1,0:T(8,128)(2,1)} %weight.1) | copy-start | bytes 1572868
  0.6 10.2 %collective-permute-start.2 = (bf16[512,256]{1,0:T(8,128)(2,1)}, bf16[512,256]{1,0:T(8,128)(2,1)S(1)}, u32[]{:S(2)}, u32[]{:S(2)}) collective-permute-start(bf16[512,256]{1,0:T(8,128)(2,1)} %mine.1), channel_id=1, source_target_pairs={{1,0},{2,1},{3,2},{0,3},{5,4},{6,5},{7,6},{4,7},{9,8},{10,9},{11,1... | collective-permute-start | bytes 786440 | tf_op jit(solution)/shard_map/ppermute | solution.py:398
  1.3 0.9 %copy-start.3 = (bf16[512,256]{1,0:T(8,128)(2,1)S(1)}, bf16[512,256]{1,0:T(8,128)(2,1)}, u32[]{:S(2)}) copy-start(bf16[512,256]{1,0:T(8,128)(2,1)} %keys.1) | copy-start | bytes 786436
  2.2 0.9 %copy-start.4 = (bf16[512,256]{1,0:T(8,128)(2,1)S(1)}, bf16[512,256]{1,0:T(8,128)(2,1)}, u32[]{:S(2)}) copy-start(bf16[512,256]{1,0:T(8,128)(2,1)} %values.1) | copy-start | bytes 786436
  3.6 9.6 %collective-permute-start.1 = (bf16[256,512]{1,0:T(8,128)(2,1)S(1)}, bf16[256,512]{1,0:T(8,128)(2,1)S(1)}, u32[]{:S(2)}, u32[]{:S(2)}) collective-permute-start(bf16[256,512]{1,0:T(8,128)(2,1)S(1)} %get-tuple-element.42), channel_id=1, source_target_pairs={{4,0},{8,4},{12,8},{16,12},{20,16},{24,20},{28,24},{32,28},{36,32}... | collective-permute-start | bytes 786440 | tf_op jit(solution)/shard_map/ppermute | solution.py:406
  4.6 8.6 %collective-permute-start = (bf16[256,512]{1,0:T(8,128)(2,1)S(1)}, bf16[256,512]{1,0:T(8,128)(2,1)S(1)}, u32[]{:S(2)}, u32[]{:S(2)}) collective-permute-start(bf16[256,512]{1,0:T(8,128)(2,1)S(1)} %get-tuple-element.39._), channel_id=1, source_target_pairs={{0,4},{4,8},{8,12},{12,16},{16,20},{20,24},{24,28},{28,32},{32,36}... | collective-permute-start | bytes 786440 | tf_op jit(solution)/shard_map/ppermute | solution.py:405
  8.7 6.9 %collective-permute-start.4 = (bf16[512,256]{1,0:T(8,128)(2,1)}, bf16[512,256]{1,0:T(8,128)(2,1)S(1)}, u32[]{:S(2)}, u32[]{:S(2)}) collective-permute-start(bf16[512,256]{1,0:T(8,128)(2,1)} %mine.1), channel_id=1, source_target_pairs={{0,1},{1,2},{2,3},{3,0},{4,5},{5,6},{6,7},{7,4},{8,9},{9,10},{10,1... | collective-permute-start | bytes 786440 | tf_op jit(solution)/shard_map/ppermute | solution.py:399
  10.8 9.1 %collective-permute-start.3 = (bf16[512,256]{1,0:T(8,128)(2,1)S(1)}, bf16[512,256]{1,0:T(8,128)(2,1)S(1)}, u32[]{:S(2)}, u32[]{:S(2)}) collective-permute-start(bf16[512,256]{1,0:T(8,128)(2,1)S(1)} %collective-permute-done.2.first_cot), channel_id=1, source_target_pairs={{1,0},{2,1},{3,2},{0,3},{5,4},{6,5},{7,6},{4,7},{9,8},{10,9},{11,1... | collective-permute-start | bytes 786440 | tf_op jit(solution)/shard_map/ppermute | solution.py:414
  10.9 1.0 %copy-start.1 = (bf16[512,256]{1,0:T(8,128)(2,1)S(1)}, bf16[512,256]{1,0:T(8,128)(2,1)}, u32[]{:S(2)}) copy-start(bf16[512,256]{1,0:T(8,128)(2,1)} %queries.1) | copy-start | bytes 786436
  13.2 2.4 %copy-start.2 = (bf16[512,256]{1,0:T(8,128)(2,1)S(1)}, bf16[512,256]{1,0:T(8,128)(2,1)}, u32[]{:S(2)}) copy-start(bf16[512,256]{1,0:T(8,128)(2,1)} %mine.1) | copy-start | bytes 786436
  14.9 0.7 %copy-start.5 = (bf16[512,256]{1,0:T(8,128)(2,1)}, bf16[512,256]{1,0:T(8,128)(2,1)S(1)}, u32[]{:S(2)}) copy-start(bf16[512,256]{1,0:T(8,128)(2,1)S(1)} %get-tuple-element.59.own_part) | copy-start | bytes 786436
  20.6 2.3 %collective-permute-start.10 = (bf16[32,16,256]{2,1,0:T(8,128)(2,1)S(1)}, bf16[32,16,256]{2,1,0:T(8,128)(2,1)S(1)}, u32[]{:S(2)}, u32[]{:S(2)}) collective-permute-start(bf16[32,16,256]{2,1,0:T(8,128)(2,1)S(1)} %get-tuple-element.67), channel_id=1, source_target_pairs={{0,4},{4,0},{8,12},{12,8},{16,20},{20,16},{24,28},{28,24},{32,36},... | collective-permute-start | bytes 786440 | tf_op jit(solution)/shard_map/ppermute | solution.py:432
  21.5 10.4 %collective-permute-start.5 = (bf16[512,256]{1,0:T(8,128)(2,1)S(1)}, bf16[512,256]{1,0:T(8,128)(2,1)S(1)}, u32[]{:S(2)}, u32[]{:S(2)}) collective-permute-start(bf16[512,256]{1,0:T(8,128)(2,1)S(1)} %get-tuple-element.56), channel_id=1, source_target_pairs={{0,1},{1,2},{2,3},{3,0},{4,5},{5,6},{6,7},{7,4},{8,9},{9,10},{10,1... | collective-permute-start | bytes 786440 | tf_op jit(solution)/shard_map/ppermute | solution.py:421
  21.5 17.4 %collective-permute-start.6 = (bf16[512,256]{1,0:T(8,128)(2,1)S(1)}, bf16[512,256]{1,0:T(8,128)(2,1)S(1)}, u32[]{:S(2)}, u32[]{:S(2)}) collective-permute-start(bf16[512,256]{1,0:T(8,128)(2,1)S(1)} %get-tuple-element.60), channel_id=1, source_target_pairs={{1,0},{2,1},{3,2},{0,3},{5,4},{6,5},{7,6},{4,7},{9,8},{10,9},{11,1... | collective-permute-start | bytes 786440 | tf_op jit(solution)/shard_map/ppermute | solution.py:422
  23.7 24.3 %all-to-all-start = ((bf16[32,16,256]{2,1,0:T(8,128)(2,1)}), bf16[32,16,256]{2,1,0:T(8,128)(2,1)S(1)}, u32[]{:S(2)}, u32[]{:S(2)}) async-start(bf16[32,16,256]{2,1,0:T(8,128)(2,1)} %shard_map.100), calls=%async_computation | async-start | bytes 524288 | tf_op jit(solution)/shard_map/all_to_all | solution.py:436
  31.9 7.0 %copy-start.6 = (bf16[512,256]{1,0:T(8,128)(2,1)S(1)}, bf16[512,256]{1,0:T(8,128)(2,1)}, u32[]{:S(2)}) copy-start(bf16[512,256]{1,0:T(8,128)(2,1)} %copy-done.5) | copy-start | bytes 786436
  34.0 8.1 %collective-permute-start.7 = (bf16[512,256]{1,0:T(8,128)(2,1)S(1)}, bf16[512,256]{1,0:T(8,128)(2,1)S(1)}, u32[]{:S(2)}, u32[]{:S(2)}) collective-permute-start(bf16[512,256]{1,0:T(8,128)(2,1)S(1)} %get-tuple-element.62), channel_id=1, source_target_pairs={{0,1},{1,2},{2,3},{3,0},{4,5},{5,6},{6,7},{7,4},{8,9},{9,10},{10,1... | collective-permute-start | bytes 786440 | tf_op jit(solution)/shard_map/ppermute | solution.py:444
  35.3 6.9 %collective-permute-start.8 = (bf16[256,512]{1,0:T(8,128)(2,1)S(1)}, bf16[256,512]{1,0:T(8,128)(2,1)S(1)}, u32[]{:S(2)}, u32[]{:S(2)}) collective-permute-start(bf16[256,512]{1,0:T(8,128)(2,1)S(1)} %get-tuple-element.64), channel_id=1, source_target_pairs={{0,4},{4,8},{8,12},{12,16},{16,20},{20,24},{24,28},{28,32},{32,36}... | collective-permute-start | bytes 786440 | tf_op jit(solution)/shard_map/ppermute | solution.py:445
  38.9 9.1 %collective-permute-start.9 = (bf16[256,512]{1,0:T(8,128)(2,1)S(1)}, bf16[256,512]{1,0:T(8,128)(2,1)S(1)}, u32[]{:S(2)}, u32[]{:S(2)}) collective-permute-start(bf16[256,512]{1,0:T(8,128)(2,1)S(1)} %get-tuple-element.65), channel_id=1, source_target_pairs={{4,0},{8,4},{12,8},{16,12},{20,16},{24,20},{28,24},{32,28},{36,32}... | collective-permute-start | bytes 786440 | tf_op jit(solution)/shard_map/ppermute | solution.py:446

commit v9 on v8

--- a/solution.py
+++ b/solution.py
@@ -14,7 +14,7 @@
 NEG = -1e30
 VMEM = pl.BlockSpec(memory_space=pltpu.VMEM)
 FAR = pl.BlockSpec(memory_space=pl.ANY)
-PIECES = 4
+PIECES = 8
 NT = (((1,), (1,)), ((), ()))
 TN = (((0,), (0,)), ((), ()))
 NN = (((1,), (0,)), ((), ()))

time: 50.4 us -> 50.4 us (level)
  no operation moved by 1% of the time
where the time goes in v9:
time: 50.4 us; the launch traced here: 49.8 us
  starting transfers between devices  23.3 us (46%)
  Pallas kernels  12.4 us (25%)
  waiting for transfers between devices  9.67 us (19%)
  local copies, waits for them, and re-layouts  3.56 us (7%)
  between operations  0.95 us (2%)
    pallas_call x10, Pallas kernels, run(): pl.pallas_call(body, in_specs=[FAR if number in far_args else VMEM for nu...  12.4 us
    all_to_all x1, starting transfers between devices, local(): spread = lax.all_to_all(pairs, 'seq', 0, 0, axis_index_groups=groups)  8.19 us
    ppermute x1, waiting for transfers between devices, local(): grad_after = lax.ppermute(to_prev, 'seq', back)  5.8 us
    ppermute x1, starting transfers between devices, local(): before = lax.ppermute(to_next, 'seq', onward)  4.11 us
    ppermute x1, waiting for transfers between devices, local(): opposite = lax.ppermute(first_cot, 'head', down)  3.75 us
    ppermute x1, starting transfers between devices, local(): grad_before = lax.ppermute(to_next, 'seq', onward)  3.59 us
    unnamed x14, local copies, waits for them, and re-layouts  3.56 us
    ppermute x1, starting transfers between devices, local(): second_cot = lax.ppermute(grad_out, 'head', up)  2.13 us
  transfers between devices with their start and end apart: 12, of which 3 were waited for; matrix products, arithmetic and copies ran while one was open for 0% of the time, Pallas kernels for 20%

profile of v9, /device:TPU:127, one launch (start us, length us, event | category | flops | bytes accessed | tf_op | source)
XLA Modules:
  0.0 49.8 jit_solution(4175468792885582484)
XLA Ops:
  0.6 0.6 %collective-permute-start.2 = (bf16[512,256]{1,0:T(8,128)(2,1)}, bf16[512,256]{1,0:T(8,128)(2,1)S(1)}, u32[]{:S(2)}, u32[]{:S(2)}) collective-permute-start(bf16[512,256]{1,0:T(8,128)(2,1)} %mine.1), channel_id=1, source_target_pairs={{1,0},{2,1},{3,2},{0,3},{5,4},{6,5},{7,6},{4,7},{9,8},{10,9},{11,1... | collective-permute-start | bytes 786440 | tf_op jit(solution)/shard_map/ppermute | solution.py:398
  1.3 0.9 %copy-done.3 = bf16[512,256]{1,0:T(8,128)(2,1)S(1)} copy-done((bf16[512,256]{1,0:T(8,128)(2,1)S(1)}, bf16[512,256]{1,0:T(8,128)(2,1)}, u32[]{:S(2)}) %copy-start.3) | copy-done | bytes 262168
  2.2 0.9 %copy-done.4 = bf16[512,256]{1,0:T(8,128)(2,1)S(1)} copy-done((bf16[512,256]{1,0:T(8,128)(2,1)S(1)}, bf16[512,256]{1,0:T(8,128)(2,1)}, u32[]{:S(2)}) %copy-start.4) | copy-done | bytes 262168
  3.2 0.4 shard_map.92
  3.6 1.0 %collective-permute-start.1 = (bf16[256,512]{1,0:T(8,128)(2,1)S(1)}, bf16[256,512]{1,0:T(8,128)(2,1)S(1)}, u32[]{:S(2)}, u32[]{:S(2)}) collective-permute-start(bf16[256,512]{1,0:T(8,128)(2,1)S(1)} %get-tuple-element.42), channel_id=1, source_target_pairs={{4,0},{8,4},{12,8},{16,12},{20,16},{24,20},{28,24},{32,28},{36,32}... | collective-permute-start | bytes 786440 | tf_op jit(solution)/shard_map/ppermute | solution.py:406
  4.6 4.1 %collective-permute-start = (bf16[256,512]{1,0:T(8,128)(2,1)S(1)}, bf16[256,512]{1,0:T(8,128)(2,1)S(1)}, u32[]{:S(2)}, u32[]{:S(2)}) collective-permute-start(bf16[256,512]{1,0:T(8,128)(2,1)S(1)} %get-tuple-element.39._), channel_id=1, source_target_pairs={{0,4},{4,8},{8,12},{12,16},{16,20},{20,24},{24,28},{28,32},{32,36}... | collective-permute-start | bytes 786440 | tf_op jit(solution)/shard_map/ppermute | solution.py:405
  8.7 2.1 %collective-permute-start.4 = (bf16[512,256]{1,0:T(8,128)(2,1)}, bf16[512,256]{1,0:T(8,128)(2,1)S(1)}, u32[]{:S(2)}, u32[]{:S(2)}) collective-permute-start(bf16[512,256]{1,0:T(8,128)(2,1)} %mine.1), channel_id=1, source_target_pairs={{0,1},{1,2},{2,3},{3,0},{4,5},{5,6},{6,7},{7,4},{8,9},{9,10},{10,1... | collective-permute-start | bytes 786440 | tf_op jit(solution)/shard_map/ppermute | solution.py:399
  10.8 0.0 collective-permute-done.2.first_cot
  10.8 0.0 collective-permute-start.3
  10.9 0.0 copy-start.1
  10.9 0.9 %copy-done.1 = bf16[512,256]{1,0:T(8,128)(2,1)S(1)} copy-done((bf16[512,256]{1,0:T(8,128)(2,1)S(1)}, bf16[512,256]{1,0:T(8,128)(2,1)}, u32[]{:S(2)}) %copy-start.1) | copy-done | bytes 262168
  11.8 0.1 shard_map.93
  11.9 1.3 %shard_map.94 = (f32[2,512]{1,0:T(2,128)S(1)}, f32[2,512]{1,0:T(2,128)S(1)}, f32[256,512]{1,0:T(8,128)S(1)}) custom-call(bf16[512,256]{1,0:T(8,128)(2,1)S(1)} %get-tuple-element.40.queries, bf16[512,512]{1,0:T(8,128)(2,1)S(1)} %get-tuple-element.41.mine, bf16[256,512]{1,0:T(8,128)(2,1)S(1)} %get-tuple-element.39._), custom_call_target="tpu_custom_call" | custom-call | flops 1000000000 | bytes 2097152 | tf_op jit(solution)/shard_map/pallas_call | solution.py:28
  13.2 0.0 copy-start.2
  13.2 1.7 %shard_map.95 = (bf16[512,256]{1,0:T(8,128)(2,1)S(1)}, bf16[512,256]{1,0:T(8,128)(2,1)S(1)}, f32[2,512]{1,0:T(2,128)S(1)}, bf16[512,256]{1,0:T(8,128)(2,1)S(1)},...) custom-call(bf16[512,256]{1,0:T(8,128)(2,1)S(1)} %get-tuple-element.40.queries, ...), custom_call_target="tpu_custom_call" | custom-call | flops 1000000000 | bytes 3145728 | tf_op jit(solution)/shard_map/pallas_call | solution.py:28
  14.9 0.0 copy-start.5
  14.9 0.7 %copy-done.5 = bf16[512,256]{1,0:T(8,128)(2,1)} copy-done((bf16[512,256]{1,0:T(8,128)(2,1)}, bf16[512,256]{1,0:T(8,128)(2,1)S(1)}, u32[]{:S(2)}) %copy-start.5) | copy-done | bytes 262168
  15.6 0.6 %shard_map.96 = (f32[32,16,256]{2,1,0:T(8,128)S(1)}, bf16[32,16,256]{2,1,0:T(8,128)(2,1)S(1)}, f32[512,256]{1,0:T(8,128)S(1)}) custom-call(bf16[512,256]{1,0:T(8,128)(2,1)S(1)} %copy-done.2, bf16[512,256]{1,0:T(8,128)(2,1)S(1)} %collective-permute-done.2.first_cot, bf16[512,256]{1,0:T(8,128)(2,1)S(1)} %collective-permute-done.4.second_cot, ...), custom_call_target="tpu_custom_call" | custom-call | flops 400000000 | bytes 1048576 | tf_op jit(solution)/shard_map/pallas_call | solution.py:28
  16.2 3.8 %collective-permute-done.3.opposite = bf16[512,256]{1,0:T(8,128)(2,1)S(1)} collective-permute-done((bf16[512,256]{1,0:T(8,128)(2,1)S(1)}, bf16[512,256]{1,0:T(8,128)(2,1)S(1)}, u32[]{:S(2)}, u32[]{:S(2)}) %collective-permute-start.3) | collective-permute-done | bytes 262176 | tf_op jit(solution)/shard_map/ppermute | solution.py:414
  20.0 0.6 %shard_map.97 = (f32[32,16,256]{2,1,0:T(8,128)S(1)}, bf16[32,16,256]{2,1,0:T(8,128)(2,1)S(1)}, bf16[512,256]{1,0:T(8,128)(2,1)S(1)}, f32[2,512]{1,0:T(2,128)S(1)}) custom-call(bf16[512,256]{1,0:T(8,128)(2,1)S(1)} %collective-permute-done.3.opposite, bf16[512,256]{1,0:T(8,128)(2,1)S(1)} %get-tuple-element.48.attention, ...), custom_call_target="tpu_custom_call" | custom-call | tf_op jit(solution)/shard_map/pallas_call | solution.py:28
  20.6 0.9 %collective-permute-start.10 = (bf16[32,16,256]{2,1,0:T(8,128)(2,1)S(1)}, bf16[32,16,256]{2,1,0:T(8,128)(2,1)S(1)}, u32[]{:S(2)}, u32[]{:S(2)}) collective-permute-start(bf16[32,16,256]{2,1,0:T(8,128)(2,1)S(1)} %get-tuple-element.67), channel_id=1, source_target_pairs={{0,4},{4,0},{8,12},{12,8},{16,20},{20,16},{24,28},{28,24},{32,36},... | collective-permute-start | bytes 786440 | tf_op jit(solution)/shard_map/ppermute | solution.py:432
  21.5 1.5 %collective-permute-start.6 = (bf16[512,256]{1,0:T(8,128)(2,1)S(1)}, bf16[512,256]{1,0:T(8,128)(2,1)S(1)}, u32[]{:S(2)}, u32[]{:S(2)}) collective-permute-start(bf16[512,256]{1,0:T(8,128)(2,1)S(1)} %get-tuple-element.60), channel_id=1, source_target_pairs={{1,0},{2,1},{3,2},{0,3},{5,4},{6,5},{7,6},{4,7},{9,8},{10,9},{11,1... | collective-permute-start | bytes 786440 | tf_op jit(solution)/shard_map/ppermute | solution.py:422
  23.0 0.8 %shard_map.100 = bf16[32,16,256]{2,1,0:T(8,128)(2,1)} custom-call(f32[32,16,256]{2,1,0:T(8,128)S(1)} %get-tuple-element.66.keep, bf16[32,16,256]{2,1,0:T(8,128)(2,1)S(1)} %collective-permute-done.10.sibling), custom_call_target="tpu_custom_call" | custom-call | tf_op jit(solution)/shard_map/pallas_call | solution.py:28
  23.7 8.2 %all-to-all-start = ((bf16[32,16,256]{2,1,0:T(8,128)(2,1)}), bf16[32,16,256]{2,1,0:T(8,128)(2,1)S(1)}, u32[]{:S(2)}, u32[]{:S(2)}) async-start(bf16[32,16,256]{2,1,0:T(8,128)(2,1)} %shard_map.100), calls=%async_computation | async-start | bytes 524288 | tf_op jit(solution)/shard_map/all_to_all | solution.py:436
  31.9 0.0 copy-start.6
  32.0 2.1 %shard_map.98 = (bf16[4,512,256]{2,1,0:T(8,128)(2,1)S(1)}, bf16[256,512]{1,0:T(8,128)(2,1)S(1)}, bf16[256,512]{1,0:T(8,128)(2,1)S(1)}, bf16[768,512]{1,0:T(8,128)(2,1)S(1)}, bf16[512,256]{1,0:T(8,128)(2,1)S(1)}) custom-call(bf16[512,256]{1,0:T(8,128)(2,1)S(1)} %get-tuple-element.40.queries, bf16[256,512]{1,0:T(8,128)(2,1)S(1)} %collective-permute-done.before, ...), custom_call_target="tpu_custom_call" | custom-call | flops 2000000000 | bytes 4194304 | tf_op jit(solution)/shard_map/pallas_call | solution.py:28
  34.1 1.3 %collective-permute-start.7 = (bf16[512,256]{1,0:T(8,128)(2,1)S(1)}, bf16[512,256]{1,0:T(8,128)(2,1)S(1)}, u32[]{:S(2)}, u32[]{:S(2)}) collective-permute-start(bf16[512,256]{1,0:T(8,128)(2,1)S(1)} %get-tuple-element.62), channel_id=1, source_target_pairs={{0,1},{1,2},{2,3},{3,0},{4,5},{5,6},{6,7},{7,4},{8,9},{9,10},{10,1... | collective-permute-start | bytes 786440 | tf_op jit(solution)/shard_map/ppermute | solution.py:444
  35.3 3.6 %collective-permute-start.8 = (bf16[256,512]{1,0:T(8,128)(2,1)S(1)}, bf16[256,512]{1,0:T(8,128)(2,1)S(1)}, u32[]{:S(2)}, u32[]{:S(2)}) collective-permute-start(bf16[256,512]{1,0:T(8,128)(2,1)S(1)} %get-tuple-element.64), channel_id=1, source_target_pairs={{0,4},{4,8},{8,12},{12,16},{16,20},{20,24},{24,28},{28,32},{32,36}... | collective-permute-start | bytes 786440 | tf_op jit(solution)/shard_map/ppermute | solution.py:445
  38.9 3.2 %shard_map.99 = (bf16[512,256]{1,0:T(8,128)(2,1)}, bf16[512,512]{1,0:T(8,128)(2,1)S(1)}, f32[512,256]{1,0:T(8,128)S(1)}) custom-call(bf16[512,256]{1,0:T(8,128)(2,1)S(1)} %get-tuple-element.40.queries, bf16[512,512]{1,0:T(8,128)(2,1)S(1)} %get-tuple-element.41.mine, bf16[768,512]{1,0:T(8,128)(2,1)S(1)} %get-tuple-element.57.edge, ...), custom_call_target="tpu_custom_call" | custom-call | flops 3000000000 | bytes 6291456 | tf_op jit(solution)/shard_map/pallas_call | solution.py:28
  42.1 0.1 collective-permute-done.8.from_prev
  42.2 5.8 %collective-permute-done.9.from_next = bf16[256,512]{1,0:T(8,128)(2,1)S(1)} collective-permute-done((bf16[256,512]{1,0:T(8,128)(2,1)S(1)}, bf16[256,512]{1,0:T(8,128)(2,1)S(1)}, u32[]{:S(2)}, u32[]{:S(2)}) %collective-permute-start.9) | collective-permute-done | bytes 262176 | tf_op jit(solution)/shard_map/ppermute | solution.py:446
  48.0 1.6 %shard_map.101 = (bf16[512,256]{1,0:T(8,128)(2,1)}, bf16[512,256]{1,0:T(8,128)(2,1)}, bf16[512,256]{1,0:T(8,128)(2,1)}, f32[16,256]{1,0:T(8,128)}) custom-call(f32[512,256]{1,0:T(8,128)S(1)} %get-tuple-element.61.near_out, bf16[512,256]{1,0:T(8,128)(2,1)S(1)} %collective-permute-done.7.last_below, bf16[512,512]{1,0:T(8,128)(2,1)S(1)} %get-tuple-element.63.own, ...), custom_call_target="tpu_custom_call" | custom-call | bytes 4194304 | tf_op jit(solution)/shard_map/pallas_call | solution.py:28
  (16 shorter events, 0.0 us)
Async XLA Ops:
  0.6 10.2 %copy-start = (bf16[1024,256]{1,0:T(8,128)(2,1)S(1)}, bf16[1024,256]{1,0:T(8,128)(2,1)}, u32[]{:S(2)}) copy-start(bf16[1024,256]{1,0:T(8,128)(2,1)} %weight.1) | copy-start | bytes 1572868
  0.6 10.2 %collective-permute-start.2 = (bf16[512,256]{1,0:T(8,128)(2,1)}, bf16[512,256]{1,0:T(8,128)(2,1)S(1)}, u32[]{:S(2)}, u32[]{:S(2)}) collective-permute-start(bf16[512,256]{1,0:T(8,128)(2,1)} %mine.1), channel_id=1, source_target_pairs={{1,0},{2,1},{3,2},{0,3},{5,4},{6,5},{7,6},{4,7},{9,8},{10,9},{11,1... | collective-permute-start | bytes 786440 | tf_op jit(solution)/shard_map/ppermute | solution.py:398
  1.3 0.9 %copy-start.3 = (bf16[512,256]{1,0:T(8,128)(2,1)S(1)}, bf16[512,256]{1,0:T(8,128)(2,1)}, u32[]{:S(2)}) copy-start(bf16[512,256]{1,0:T(8,128)(2,1)} %keys.1) | copy-start | bytes 786436
  2.2 0.9 %copy-start.4 = (bf16[512,256]{1,0:T(8,128)(2,1)S(1)}, bf16[512,256]{1,0:T(8,128)(2,1)}, u32[]{:S(2)}) copy-start(bf16[512,256]{1,0:T(8,128)(2,1)} %values.1) | copy-start | bytes 786436
  3.6 9.6 %collective-permute-start.1 = (bf16[256,512]{1,0:T(8,128)(2,1)S(1)}, bf16[256,512]{1,0:T(8,128)(2,1)S(1)}, u32[]{:S(2)}, u32[]{:S(2)}) collective-permute-start(bf16[256,512]{1,0:T(8,128)(2,1)S(1)} %get-tuple-element.42), channel_id=1, source_target_pairs={{4,0},{8,4},{12,8},{16,12},{20,16},{24,20},{28,24},{32,28},{36,32}... | collective-permute-start | bytes 786440 | tf_op jit(solution)/shard_map/ppermute | solution.py:406
  4.6 8.6 %collective-permute-start = (bf16[256,512]{1,0:T(8,128)(2,1)S(1)}, bf16[256,512]{1,0:T(8,128)(2,1)S(1)}, u32[]{:S(2)}, u32[]{:S(2)}) collective-permute-start(bf16[256,512]{1,0:T(8,128)(2,1)S(1)} %get-tuple-element.39._), channel_id=1, source_target_pairs={{0,4},{4,8},{8,12},{12,16},{16,20},{20,24},{24,28},{28,32},{32,36}... | collective-permute-start | bytes 786440 | tf_op jit(solution)/shard_map/ppermute | solution.py:405
  8.7 6.9 %collective-permute-start.4 = (bf16[512,256]{1,0:T(8,128)(2,1)}, bf16[512,256]{1,0:T(8,128)(2,1)S(1)}, u32[]{:S(2)}, u32[]{:S(2)}) collective-permute-start(bf16[512,256]{1,0:T(8,128)(2,1)} %mine.1), channel_id=1, source_target_pairs={{0,1},{1,2},{2,3},{3,0},{4,5},{5,6},{6,7},{7,4},{8,9},{9,10},{10,1... | collective-permute-start | bytes 786440 | tf_op jit(solution)/shard_map/ppermute | solution.py:399
  10.8 9.1 %collective-permute-start.3 = (bf16[512,256]{1,0:T(8,128)(2,1)S(1)}, bf16[512,256]{1,0:T(8,128)(2,1)S(1)}, u32[]{:S(2)}, u32[]{:S(2)}) collective-permute-start(bf16[512,256]{1,0:T(8,128)(2,1)S(1)} %collective-permute-done.2.first_cot), channel_id=1, source_target_pairs={{1,0},{2,1},{3,2},{0,3},{5,4},{6,5},{7,6},{4,7},{9,8},{10,9},{11,1... | collective-permute-start | bytes 786440 | tf_op jit(solution)/shard_map/ppermute | solution.py:414
  10.9 1.0 %copy-start.1 = (bf16[512,256]{1,0:T(8,128)(2,1)S(1)}, bf16[512,256]{1,0:T(8,128)(2,1)}, u32[]{:S(2)}) copy-start(bf16[512,256]{1,0:T(8,128)(2,1)} %queries.1) | copy-start | bytes 786436
  13.2 2.4 %copy-start.2 = (bf16[512,256]{1,0:T(8,128)(2,1)S(1)}, bf16[512,256]{1,0:T(8,128)(2,1)}, u32[]{:S(2)}) copy-start(bf16[512,256]{1,0:T(8,128)(2,1)} %mine.1) | copy-start | bytes 786436
  14.9 0.7 %copy-start.5 = (bf16[512,256]{1,0:T(8,128)(2,1)}, bf16[512,256]{1,0:T(8,128)(2,1)S(1)}, u32[]{:S(2)}) copy-start(bf16[512,256]{1,0:T(8,128)(2,1)S(1)} %get-tuple-element.59.own_part) | copy-start | bytes 786436
  20.6 2.3 %collective-permute-start.10 = (bf16[32,16,256]{2,1,0:T(8,128)(2,1)S(1)}, bf16[32,16,256]{2,1,0:T(8,128)(2,1)S(1)}, u32[]{:S(2)}, u32[]{:S(2)}) collective-permute-start(bf16[32,16,256]{2,1,0:T(8,128)(2,1)S(1)} %get-tuple-element.67), channel_id=1, source_target_pairs={{0,4},{4,0},{8,12},{12,8},{16,20},{20,16},{24,28},{28,24},{32,36},... | collective-permute-start | bytes 786440 | tf_op jit(solution)/shard_map/ppermute | solution.py:432
  21.5 10.5 %collective-permute-start.5 = (bf16[512,256]{1,0:T(8,128)(2,1)S(1)}, bf16[512,256]{1,0:T(8,128)(2,1)S(1)}, u32[]{:S(2)}, u32[]{:S(2)}) collective-permute-start(bf16[512,256]{1,0:T(8,128)(2,1)S(1)} %get-tuple-element.56), channel_id=1, source_target_pairs={{0,1},{1,2},{2,3},{3,0},{4,5},{5,6},{6,7},{7,4},{8,9},{9,10},{10,1... | collective-permute-start | bytes 786440 | tf_op jit(solution)/shard_map/ppermute | solution.py:421
  21.5 17.5 %collective-permute-start.6 = (bf16[512,256]{1,0:T(8,128)(2,1)S(1)}, bf16[512,256]{1,0:T(8,128)(2,1)S(1)}, u32[]{:S(2)}, u32[]{:S(2)}) collective-permute-start(bf16[512,256]{1,0:T(8,128)(2,1)S(1)} %get-tuple-element.60), channel_id=1, source_target_pairs={{1,0},{2,1},{3,2},{0,3},{5,4},{6,5},{7,6},{4,7},{9,8},{10,9},{11,1... | collective-permute-start | bytes 786440 | tf_op jit(solution)/shard_map/ppermute | solution.py:422
  23.7 24.3 %all-to-all-start = ((bf16[32,16,256]{2,1,0:T(8,128)(2,1)}), bf16[32,16,256]{2,1,0:T(8,128)(2,1)S(1)}, u32[]{:S(2)}, u32[]{:S(2)}) async-start(bf16[32,16,256]{2,1,0:T(8,128)(2,1)} %shard_map.100), calls=%async_computation | async-start | bytes 524288 | tf_op jit(solution)/shard_map/all_to_all | solution.py:436
  31.9 7.0 %copy-start.6 = (bf16[512,256]{1,0:T(8,128)(2,1)S(1)}, bf16[512,256]{1,0:T(8,128)(2,1)}, u32[]{:S(2)}) copy-start(bf16[512,256]{1,0:T(8,128)(2,1)} %copy-done.5) | copy-start | bytes 786436
  34.1 8.1 %collective-permute-start.7 = (bf16[512,256]{1,0:T(8,128)(2,1)S(1)}, bf16[512,256]{1,0:T(8,128)(2,1)S(1)}, u32[]{:S(2)}, u32[]{:S(2)}) collective-permute-start(bf16[512,256]{1,0:T(8,128)(2,1)S(1)} %get-tuple-element.62), channel_id=1, source_target_pairs={{0,1},{1,2},{2,3},{3,0},{4,5},{5,6},{6,7},{7,4},{8,9},{9,10},{10,1... | collective-permute-start | bytes 786440 | tf_op jit(solution)/shard_map/ppermute | solution.py:444
  35.3 6.9 %collective-permute-start.8 = (bf16[256,512]{1,0:T(8,128)(2,1)S(1)}, bf16[256,512]{1,0:T(8,128)(2,1)S(1)}, u32[]{:S(2)}, u32[]{:S(2)}) collective-permute-start(bf16[256,512]{1,0:T(8,128)(2,1)S(1)} %get-tuple-element.64), channel_id=1, source_target_pairs={{0,4},{4,8},{8,12},{12,16},{16,20},{20,24},{24,28},{28,32},{32,36}... | collective-permute-start | bytes 786440 | tf_op jit(solution)/shard_map/ppermute | solution.py:445
  38.9 9.1 %collective-permute-start.9 = (bf16[256,512]{1,0:T(8,128)(2,1)S(1)}, bf16[256,512]{1,0:T(8,128)(2,1)S(1)}, u32[]{:S(2)}, u32[]{:S(2)}) collective-permute-start(bf16[256,512]{1,0:T(8,128)(2,1)S(1)} %get-tuple-element.65), channel_id=1, source_target_pairs={{4,0},{8,4},{12,8},{16,12},{20,16},{24,20},{28,24},{32,28},{36,32}... | collective-permute-start | bytes 786440 | tf_op jit(solution)/shard_map/ppermute | solution.py:446
